TPU v7x, 32 devices: a whole 2x2x4 slice. The times are simulated.
32 devices in a mesh: group: 2 (over y), depth: 4 (over z), plane: 2 (over x), batch: 2 (over core).
Axes of the slice: x: 2, y: 2, z: 4, core: 2. Of those that a mesh axis runs over, the one named last changes fastest.
Arguments:
- source: bfloat16 [4, 2, 32, 65536], P('depth', None, ('group', 'batch'), 'plane'), parts along dimension 2, may hold values from -6 to 6
- pool: bfloat16 [12, 3, 2, 256, 256], P('depth')
- near_mask: int32 [12, 256, 3], P('depth', 'plane'), may hold values 0 or 1
- layer_count: int32 [4], P('depth'), may hold values from 1 to 3, 8 in all
Outputs:
- up_top: bfloat16 [4, 2, 32, 65536], P('depth', None, ('group', 'batch'), 'plane'), parts along dimension 2
- down_bottom: bfloat16 [4, 2, 32, 65536], P('depth', None, ('group', 'batch'), 'plane'), parts along dimension 2
There are 2 independent parts, one for each index of `group`. A program takes and returns all parts, laid end to end along the dimension named above; an argument that names none is the same for every part. Nothing has to cross between parts.
Inputs may be any that keep to these rules, and one draw needn't show every extreme that they name: `layer_count`: each section holds 1 to 3 layers, 8 in all; some section holds exactly 3.
All inputs are finite; a program needn't handle non-finite values. No bound on the sum of `near_mask` or of `layer_count` on one device may be relied on, other than what follows from the above.
Results may differ from a plain program's by a relative error of at most 0.012.
Values may be sent and summed in bfloat16 or wider, within the bound.
No kernel may reach another device: no remote copies, remote signals or barrier semaphores. Data moves between devices by JAX's collectives and lax.ppermute only.
A program may use at most 64 MiB of HBM per device.

v0:
```python
import functools

import jax
import jax.numpy as jnp
from jax import lax
from jax.experimental import pallas as pl
from jax.experimental.pallas import tpu as pltpu
from jax.sharding import PartitionSpec as P

NT = (((1,), (1,)), ((), ()))
CHUNKS = 4


def section_kernel(
    depth_n, chunks, sc, r1, r2, src, w, mask, state_in, top_in, bottom_in, o1, o2, state, top, bottom, up
):
    here, count, step = sc[0], sc[1], sc[2]
    rows = r1.shape[0]
    half = rows // 2
    window = mask.shape[2]
    down_at = step - here
    up_at = step - 2 * (depth_n - 1) + here
    down_due = (down_at >= 0) & (down_at < chunks)
    up_due = (up_at >= 0) & (up_at < chunks)
    even = lax.rem(here, 2) == 0
    odd = jnp.logical_not(even)

    def apply_layer(x, slot):
        wide = x.astype(jnp.float32)
        before = pltpu.roll(wide, 1, 0) * jnp.tile(mask[slot, 0], (rows // window, 2))
        after = pltpu.roll(wide, rows - 1, 0) * jnp.tile(mask[slot, 1], (rows // window, 2))
        total = lax.dot_general(before.astype(jnp.bfloat16), w[slot, 0], NT, preferred_element_type=jnp.float32)
        total = total + lax.dot_general(x, w[slot, 1], NT, preferred_element_type=jnp.float32)
        total = total + lax.dot_general(
            after.astype(jnp.bfloat16), w[slot, 2], NT, preferred_element_type=jnp.float32
        )
        block = total.shape[1] // 2
        real = total[:half, :block] - total[half:, block:]
        imag = total[half:, :block] + total[:half, block:]
        return real, imag

    @pl.when(down_due)
    def _():
        def enter(arrived):
            state[down_at, 0] = (
                arrived[...].astype(jnp.float32) + src[down_at].astype(jnp.float32)
            ).astype(jnp.bfloat16)

        pl.when(even)(lambda: enter(r2))
        pl.when(odd)(lambda: enter(r1))

        def layer(c, _):
            real, imag = apply_layer(state[down_at, c], c)
            state[down_at, c + 1, :half] = real.astype(jnp.bfloat16)
            state[down_at, c + 1, half:] = imag.astype(jnp.bfloat16)
            return 0

        lax.fori_loop(0, count, layer, 0)
        bottom[down_at] = state[down_at, count]

        @pl.when(even)
        def _():
            o1[...] = state[down_at, count]

        @pl.when(odd)
        def _():
            o2[...] = state[down_at, count]

    @pl.when(up_due)
    def _():
        @pl.when(even)
        def _():
            up[...] = r1[...]

        @pl.when(odd)
        def _():
            up[...] = r2[...]

        def layer(i, _):
            c = count - 1 - i
            real, imag = apply_layer(up[...], c)
            up[:half] = (real + state[up_at, c, :half].astype(jnp.float32)).astype(jnp.bfloat16)
            up[half:] = (imag + state[up_at, c, half:].astype(jnp.float32)).astype(jnp.bfloat16)
            return 0

        lax.fori_loop(0, count, layer, 0)
        top[up_at] = up[...]

        @pl.when(even)
        def _():
            o2[...] = up[...]

        @pl.when(odd)
        def _():
            o1[...] = up[...]


def section(depth_n, sc, r1, r2, src, w, mask, state, top, bottom):
    in_vmem = pl.BlockSpec(memory_space=pltpu.VMEM)
    held = lambda a: pltpu.with_memory_space_constraint(a, pltpu.VMEM)
    like = lambda a: pltpu.VMEM(a.shape, a.dtype)
    return pl.pallas_call(
        functools.partial(section_kernel, depth_n, src.shape[0]),
        out_shape=(like(r1), like(r2), like(state), like(top), like(bottom)),
        in_specs=[pl.BlockSpec(memory_space=pltpu.SMEM)] + [in_vmem] * 8,
        out_specs=(in_vmem,) * 5,
        scratch_shapes=[pltpu.VMEM(r1.shape, r1.dtype)],
        input_output_aliases={6: 2, 7: 3, 8: 4},
        compiler_params=pltpu.CompilerParams(vmem_limit_bytes=16 * 1024 * 1024),
    )(sc, *map(held, (r1, r2, src, w, mask, state, top, bottom)))


def windowed(cells, dim, tile, halo, start):
    planes = lax.axis_size("plane")
    if planes == 2:
        here = lax.axis_index("plane")
        tail = lax.slice_in_dim(cells, tile - halo, tile, axis=dim)
        head = lax.slice_in_dim(cells, 0, halo, axis=dim)
        arrived = lax.ppermute(jnp.where(here == 0, tail, head), "plane", [(0, 1), (1, 0)])
        first = jnp.concatenate([cells, arrived], axis=dim)
        second = jnp.concatenate([arrived, cells], axis=dim)
        return jnp.where(here == 0, first, second)
    whole = lax.all_gather(cells, "plane", axis=dim, tiled=True)
    size = min(whole.shape[dim], tile + 2 * halo)
    return lax.dynamic_slice_in_dim(whole, start, size, axis=dim)


def per_device(source, pool, near_mask, layer_count):
    depth_n = lax.axis_size("depth")
    planes = lax.axis_size("plane")
    here = lax.axis_index("depth")
    plane = lax.axis_index("plane")
    cap = pool.shape[0]
    block = pool.shape[-1]
    sources = source.shape[2]
    tile = source.shape[3] // block
    blocks = tile * planes
    halo = min(4 * depth_n, tile) if planes == 2 else 4 * depth_n
    window = tile + halo if planes == 2 else min(blocks, tile + 2 * halo)
    start = jnp.clip(plane * tile - halo, 0, blocks - window)
    own = plane * tile - start

    chunks = min(CHUNKS, sources)
    share = sources // chunks
    rows = 2 * share * window

    cells = windowed(source[0].reshape(2, sources, tile, block), 2, tile, halo, start)
    cells = cells.reshape(2, chunks, share, window, block).transpose(1, 0, 2, 3, 4)
    src = cells.reshape(chunks, rows, block)

    present = windowed(near_mask, 1, tile, halo, start).astype(jnp.float32)
    place = jnp.arange(window)[None, :]
    before = jnp.where(place == 0, 0.0, present[:, :, 0])
    after = jnp.where(place == window - 1, 0.0, present[:, :, 2])
    mask = jnp.broadcast_to(jnp.stack([before, after], axis=1)[..., None], (cap, 2, window, 128))
    w = pool.reshape(cap, 3, 2 * block, block)

    state = jnp.zeros((chunks, cap + 1, rows, block), jnp.bfloat16)
    top = jnp.zeros((chunks, rows, block), jnp.bfloat16)
    bottom = jnp.zeros((chunks, rows, block), jnp.bfloat16)
    r1 = jnp.zeros((rows, block), jnp.bfloat16)
    r2 = jnp.zeros((rows, block), jnp.bfloat16)

    def swaps(first):
        pairs = [(i, i + 1) for i in range(first, depth_n - 1, 2)]
        return pairs + [(j, i) for i, j in pairs]

    steps = chunks + 2 * (depth_n - 1)
    for step in range(steps):
        sc = jnp.stack([here, layer_count[0], jnp.int32(step)]).astype(jnp.int32)
        o1, o2, state, top, bottom = section(depth_n, sc, r1, r2, src, w, mask, state, top, bottom)
        if step < steps - 1:
            r1 = lax.ppermute(o1, "depth", swaps(0))
            if 0 < step < steps - 2:
                r2 = lax.ppermute(o2, "depth", swaps(1))

    def leave(held):
        held = held.reshape(chunks, 2, share, window, block)
        held = lax.dynamic_slice_in_dim(held, own, tile, axis=3)
        return held.transpose(1, 0, 2, 3, 4).reshape(1, 2, sources, tile * block)

    return (leave(top), leave(bottom))


def solution(mesh):
    return jax.shard_map(
        per_device,
        mesh=mesh,
        in_specs=(
            P("depth", None, ("group", "batch"), "plane"),
            P("depth", None, None, None, None),
            P("depth", "plane", None),
            P("depth"),
        ),
        out_specs=(
            P("depth", None, ("group", "batch"), "plane"),
            P("depth", None, ("group", "batch"), "plane"),
        ),
        check_vma=False,
    )
```

profile of v0, /device:TPU:0, one launch (start us, length us, event | category | flops | bytes accessed | tf_op | source)
XLA Modules:
  0.0 131.6 jit_solution(13547404535099649363)
XLA Ops:
  1.5 2.9 %collective-permute-start.1 = (s32[3,16,3]{1,2,0:T(4,128)S(1)}, s32[3,16,3]{1,2,0:T(4,128)S(1)}, u32[]{:S(2)}, u32[]{:S(2)}) collective-permute-start(s32[3,16,3]{1,2,0:T(4,128)S(1)} %slice_select_fusion.1), channel_id=1, source_target_pairs={{0,2},{2,0},{1,3},{3,1},{4,6},{6,4},{5,7},{7,5},{8,10},{10,8},{9,1... | collective-permute-start | bytes 1736 | tf_op jit(solution)/shard_map/ppermute | solution.py:119
  6.9 4.1 %collective-permute-done = bf16[2,8,16,256]{3,2,1,0:T(8,128)(2,1)S(1)} collective-permute-done((bf16[2,8,16,256]{3,2,1,0:T(8,128)(2,1)S(1)}, bf16[2,8,16,256]{3,2,1,0:T(8,128)(2,1)S(1)}, u32[]{:S(2)}, u32[]{:S(2)}) %collective-permute-start) | collective-permute-done | bytes 131104 | tf_op jit(solution)/shard_map/ppermute | solution.py:119
  13.5 2.7 %shard_map.59 = (bf16[576,256]{1,0:T(8,128)(2,1)S(1)}, bf16[576,256]{1,0:T(8,128)(2,1)}, bf16[4,4,576,256]{3,2,1,0:T(8,128)(2,1)S(1)}, bf16[4,576,256]{2,1,0:T(8,128)(2,1)S(1)}, bf16[4,576,256]{2,1,0:T(8,128)(2,1)S(1)}) custom-call(s32[3]{0:T(128)S(1)} %get-tuple-element.92.sc, ...), custom_call_target="tpu_custom_call", output_to_operand_aliasing={{2}: (6, {}), {3}: (7, {}), {4}: (8, {})} | custom-call | tf_op jit(solution)/shard_map/pallas_call | solution.py:102
  16.4 7.1 %collective-permute-done.2.r1 = bf16[576,256]{1,0:T(8,128)(2,1)S(1)} collective-permute-done((bf16[576,256]{1,0:T(8,128)(2,1)S(1)}, bf16[576,256]{1,0:T(8,128)(2,1)S(1)}, u32[]{:S(2)}, u32[]{:S(2)}) %collective-permute-start.2) | collective-permute-done | bytes 294944 | tf_op jit(solution)/shard_map/ppermute | solution.py:173
  27.3 5.1 %collective-permute-done.3.r1 = bf16[576,256]{1,0:T(8,128)(2,1)S(1)} collective-permute-done((bf16[576,256]{1,0:T(8,128)(2,1)S(1)}, bf16[576,256]{1,0:T(8,128)(2,1)S(1)}, u32[]{:S(2)}, u32[]{:S(2)}) %collective-permute-start.3) | collective-permute-done | bytes 294944 | tf_op jit(solution)/shard_map/ppermute | solution.py:173
  32.4 2.0 %shard_map.61 = (bf16[576,256]{1,0:T(8,128)(2,1)S(1)}, bf16[576,256]{1,0:T(8,128)(2,1)S(1)}, bf16[4,4,576,256]{3,2,1,0:T(8,128)(2,1)S(1)}, bf16[4,576,256]{2,1,0:T(8,128)(2,1)S(1)}, bf16[4,576,256]{2,1,0:T(8,128)(2,1)S(1)}) custom-call(s32[3]{0:T(128)S(1)} %get-tuple-element.101.sc, ...), custom_call_target="tpu_custom_call", output_to_operand_aliasing={{2}: (6, {}), {3}: (7, {}), {4}: (8, {})} | custom-call | tf_op jit(solution)/shard_map/pallas_call | solution.py:102
  34.4 4.6 %collective-permute-start.5 = (bf16[576,256]{1,0:T(8,128)(2,1)S(1)}, bf16[576,256]{1,0:T(8,128)(2,1)S(1)}, u32[]{:S(2)}, u32[]{:S(2)}) collective-permute-start(bf16[576,256]{1,0:T(8,128)(2,1)S(1)} %get-tuple-element.56), channel_id=1, source_target_pairs={{0,4},{8,12},{4,0},{12,8},{1,5},{9,13},{5,1},{13,9},{2,6},{10,14},... | collective-permute-start | bytes 884744 | tf_op jit(solution)/shard_map/ppermute | solution.py:173
  39.7 4.0 %collective-permute-done.5.r1 = bf16[576,256]{1,0:T(8,128)(2,1)S(1)} collective-permute-done((bf16[576,256]{1,0:T(8,128)(2,1)S(1)}, bf16[576,256]{1,0:T(8,128)(2,1)S(1)}, u32[]{:S(2)}, u32[]{:S(2)}) %collective-permute-start.5) | collective-permute-done | bytes 294944 | tf_op jit(solution)/shard_map/ppermute | solution.py:173
  45.8 4.7 %collective-permute-start.7 = (bf16[576,256]{1,0:T(8,128)(2,1)S(1)}, bf16[576,256]{1,0:T(8,128)(2,1)S(1)}, u32[]{:S(2)}, u32[]{:S(2)}) collective-permute-start(bf16[576,256]{1,0:T(8,128)(2,1)S(1)} %get-tuple-element.61), channel_id=1, source_target_pairs={{0,4},{8,12},{4,0},{12,8},{1,5},{9,13},{5,1},{13,9},{2,6},{10,14},... | collective-permute-start | bytes 884744 | tf_op jit(solution)/shard_map/ppermute | solution.py:173
  51.1 4.0 %collective-permute-done.7.r1 = bf16[576,256]{1,0:T(8,128)(2,1)S(1)} collective-permute-done((bf16[576,256]{1,0:T(8,128)(2,1)S(1)}, bf16[576,256]{1,0:T(8,128)(2,1)S(1)}, u32[]{:S(2)}, u32[]{:S(2)}) %collective-permute-start.7) | collective-permute-done | bytes 294944 | tf_op jit(solution)/shard_map/ppermute | solution.py:173
  55.7 6.1 %collective-permute-start.9 = (bf16[576,256]{1,0:T(8,128)(2,1)S(1)}, bf16[576,256]{1,0:T(8,128)(2,1)S(1)}, u32[]{:S(2)}, u32[]{:S(2)}) collective-permute-start(bf16[576,256]{1,0:T(8,128)(2,1)S(1)} %get-tuple-element.66), channel_id=1, source_target_pairs={{0,4},{8,12},{4,0},{12,8},{1,5},{9,13},{5,1},{13,9},{2,6},{10,14},... | collective-permute-start | bytes 884744 | tf_op jit(solution)/shard_map/ppermute | solution.py:173
  62.5 4.0 %collective-permute-done.9.r1 = bf16[576,256]{1,0:T(8,128)(2,1)S(1)} collective-permute-done((bf16[576,256]{1,0:T(8,128)(2,1)S(1)}, bf16[576,256]{1,0:T(8,128)(2,1)S(1)}, u32[]{:S(2)}, u32[]{:S(2)}) %collective-permute-start.9) | collective-permute-done | bytes 294944 | tf_op jit(solution)/shard_map/ppermute | solution.py:173
  67.1 6.1 %collective-permute-start.11 = (bf16[576,256]{1,0:T(8,128)(2,1)S(1)}, bf16[576,256]{1,0:T(8,128)(2,1)S(1)}, u32[]{:S(2)}, u32[]{:S(2)}) collective-permute-start(bf16[576,256]{1,0:T(8,128)(2,1)S(1)} %get-tuple-element.71), channel_id=1, source_target_pairs={{0,4},{8,12},{4,0},{12,8},{1,5},{9,13},{5,1},{13,9},{2,6},{10,14},... | collective-permute-start | bytes 884744 | tf_op jit(solution)/shard_map/ppermute | solution.py:173
  74.1 3.8 %collective-permute-done.11.r1 = bf16[576,256]{1,0:T(8,128)(2,1)S(1)} collective-permute-done((bf16[576,256]{1,0:T(8,128)(2,1)S(1)}, bf16[576,256]{1,0:T(8,128)(2,1)S(1)}, u32[]{:S(2)}, u32[]{:S(2)}) %collective-permute-start.11) | collective-permute-done | bytes 294944 | tf_op jit(solution)/shard_map/ppermute | solution.py:173
  80.0 4.9 %collective-permute-start.13 = (bf16[576,256]{1,0:T(8,128)(2,1)S(1)}, bf16[576,256]{1,0:T(8,128)(2,1)S(1)}, u32[]{:S(2)}, u32[]{:S(2)}) collective-permute-start(bf16[576,256]{1,0:T(8,128)(2,1)S(1)} %get-tuple-element.76), channel_id=1, source_target_pairs={{0,4},{8,12},{4,0},{12,8},{1,5},{9,13},{5,1},{13,9},{2,6},{10,14},... | collective-permute-start | bytes 884744 | tf_op jit(solution)/shard_map/ppermute | solution.py:173
  85.6 5.1 %collective-permute-done.13.r1 = bf16[576,256]{1,0:T(8,128)(2,1)S(1)} collective-permute-done((bf16[576,256]{1,0:T(8,128)(2,1)S(1)}, bf16[576,256]{1,0:T(8,128)(2,1)S(1)}, u32[]{:S(2)}, u32[]{:S(2)}) %collective-permute-start.13) | collective-permute-done | bytes 294944 | tf_op jit(solution)/shard_map/ppermute | solution.py:173
  92.6 5.0 %collective-permute-start.15 = (bf16[576,256]{1,0:T(8,128)(2,1)S(1)}, bf16[576,256]{1,0:T(8,128)(2,1)S(1)}, u32[]{:S(2)}, u32[]{:S(2)}) collective-permute-start(bf16[576,256]{1,0:T(8,128)(2,1)S(1)} %get-tuple-element.81), channel_id=1, source_target_pairs={{0,4},{8,12},{4,0},{12,8},{1,5},{9,13},{5,1},{13,9},{2,6},{10,14},... | collective-permute-start | bytes 884744 | tf_op jit(solution)/shard_map/ppermute | solution.py:173
  98.3 4.0 %collective-permute-done.15.r1 = bf16[576,256]{1,0:T(8,128)(2,1)S(1)} collective-permute-done((bf16[576,256]{1,0:T(8,128)(2,1)S(1)}, bf16[576,256]{1,0:T(8,128)(2,1)S(1)}, u32[]{:S(2)}, u32[]{:S(2)}) %collective-permute-start.15) | collective-permute-done | bytes 294944 | tf_op jit(solution)/shard_map/ppermute | solution.py:173
  102.3 2.9 %shard_map.67 = (bf16[576,256]{1,0:T(8,128)(2,1)}, bf16[576,256]{1,0:T(8,128)(2,1)}, bf16[4,4,576,256]{3,2,1,0:T(8,128)(2,1)S(1)}, bf16[4,576,256]{2,1,0:T(8,128)(2,1)S(1)}, bf16[4,576,256]{2,1,0:T(8,128)(2,1)S(1)}) custom-call(s32[3]{0:T(128)S(1)} %get-tuple-element.107.sc, ...), custom_call_target="tpu_custom_call", output_to_operand_aliasing={{2}: (6, {}), {3}: (7, {}), {4}: (8, {})} | custom-call | tf_op jit(solution)/shard_map/pallas_call | solution.py:102
  105.2 2.1 %copy-done = bf16[4,4,576,256]{3,2,1,0:T(8,128)(2,1)} copy-done((bf16[4,4,576,256]{3,2,1,0:T(8,128)(2,1)}, bf16[4,4,576,256]{3,2,1,0:T(8,128)(2,1)S(1)}, u32[]{:S(2)}) %copy-start) | copy-done | bytes 4718616
  108.3 4.6 %collective-permute-start.17 = (bf16[576,256]{1,0:T(8,128)(2,1)}, bf16[576,256]{1,0:T(8,128)(2,1)}, u32[]{:S(2)}, u32[]{:S(2)}) collective-permute-start(bf16[576,256]{1,0:T(8,128)(2,1)} %get-tuple-element.86), channel_id=1, source_target_pairs={{0,4},{8,12},{4,0},{12,8},{1,5},{9,13},{5,1},{13,9},{2,6},{10,14},... | collective-permute-start | bytes 884744 | tf_op jit(solution)/shard_map/ppermute | solution.py:173
  112.9 5.0 %collective-permute-done.17.r1 = bf16[576,256]{1,0:T(8,128)(2,1)} collective-permute-done((bf16[576,256]{1,0:T(8,128)(2,1)}, bf16[576,256]{1,0:T(8,128)(2,1)}, u32[]{:S(2)}, u32[]{:S(2)}) %collective-permute-start.17) | collective-permute-done | bytes 294944 | tf_op jit(solution)/shard_map/ppermute | solution.py:173
  118.0 2.3 %copy-done.1 = bf16[4,4,576,256]{3,2,1,0:T(8,128)(2,1)S(1)} copy-done((bf16[4,4,576,256]{3,2,1,0:T(8,128)(2,1)S(1)}, bf16[4,4,576,256]{3,2,1,0:T(8,128)(2,1)}, u32[]{:S(2)}) %copy-start.1) | copy-done | bytes 4718616
  124.8 3.2 %shard_map.68 = (bf16[576,256]{1,0:T(8,128)(2,1)}, bf16[576,256]{1,0:T(8,128)(2,1)}, bf16[4,4,576,256]{3,2,1,0:T(8,128)(2,1)S(1)}, bf16[4,576,256]{2,1,0:T(8,128)(2,1)S(1)}, bf16[4,576,256]{2,1,0:T(8,128)(2,1)S(1)}) custom-call(s32[3]{0:T(128)S(1)} %get-tuple-element.108.sc, ...), custom_call_target="tpu_custom_call", output_to_operand_aliasing={{2}: (6, {}), {3}: (7, {}), {4}: (8, {})} | custom-call | tf_op jit(solution)/shard_map/pallas_call | solution.py:102
  (68 shorter events, 29.3 us)
Async XLA Ops:
  1.5 5.3 %collective-permute-start.1 = (s32[3,16,3]{1,2,0:T(4,128)S(1)}, s32[3,16,3]{1,2,0:T(4,128)S(1)}, u32[]{:S(2)}, u32[]{:S(2)}) collective-permute-start(s32[3,16,3]{1,2,0:T(4,128)S(1)} %slice_select_fusion.1), channel_id=1, source_target_pairs={{0,2},{2,0},{1,3},{3,1},{4,6},{6,4},{5,7},{7,5},{8,10},{10,8},{9,1... | collective-permute-start | bytes 1736 | tf_op jit(solution)/shard_map/ppermute | solution.py:119
  4.4 2.3 %copy-start.11 = (s32[3,128,3]{1,2,0:T(4,128)S(1)}, s32[3,128,3]{1,2,0:T(4,128)}, u32[]{:S(2)}) copy-start(s32[3,128,3]{1,2,0:T(4,128)} %param.6) | copy-start | bytes 13828
  5.9 5.0 %collective-permute-start = (bf16[2,8,16,256]{3,2,1,0:T(8,128)(2,1)S(1)}, bf16[2,8,16,256]{3,2,1,0:T(8,128)(2,1)S(1)}, u32[]{:S(2)}, u32[]{:S(2)}) collective-permute-start(bf16[2,8,16,256]{3,2,1,0:T(8,128)(2,1)S(1)} %slice_select_fusion), channel_id=1, source_target_pairs={{0,2},{2,0},{1,3},{3,1},{4,6},{6,4},{5,7},{7,5},{8,10},{10,8},{9,1... | collective-permute-start | bytes 393224 | tf_op jit(solution)/shard_map/ppermute | solution.py:119
  11.3 91.1 %copy-start.5 = (bf16[2,4,2,144,256]{4,3,2,0,1:T(8,128)(2,1)}, bf16[2,4,2,144,256]{4,3,2,0,1:T(8,128)(2,1)S(1)}, u32[]{:S(2)}) copy-start(bf16[2,4,2,144,256]{4,3,2,0,1:T(8,128)(2,1)S(1)} %copy_select_fusion) | copy-start | bytes 3538948
  11.5 90.9 %copy-start.7 = (f32[3,2,144,128]{3,2,1,0:T(8,128)}, f32[3,2,144,128]{3,2,1,0:T(8,128)S(1)}, u32[]{:S(2)}) copy-start(f32[3,2,144,128]{3,2,1,0:T(8,128)S(1)} %broadcast_in_dim.31.mask) | copy-start | bytes 1327108
  16.2 7.3 %collective-permute-start.2 = (bf16[576,256]{1,0:T(8,128)(2,1)S(1)}, bf16[576,256]{1,0:T(8,128)(2,1)S(1)}, u32[]{:S(2)}, u32[]{:S(2)}) collective-permute-start(bf16[576,256]{1,0:T(8,128)(2,1)S(1)} %get-tuple-element.47), channel_id=1, source_target_pairs={{0,4},{8,12},{4,0},{12,8},{1,5},{9,13},{5,1},{13,9},{2,6},{10,14},... | collective-permute-start | bytes 884744 | tf_op jit(solution)/shard_map/ppermute | solution.py:173
  25.6 6.8 %collective-permute-start.3 = (bf16[576,256]{1,0:T(8,128)(2,1)S(1)}, bf16[576,256]{1,0:T(8,128)(2,1)S(1)}, u32[]{:S(2)}, u32[]{:S(2)}) collective-permute-start(bf16[576,256]{1,0:T(8,128)(2,1)S(1)} %get-tuple-element.51), channel_id=1, source_target_pairs={{0,4},{8,12},{4,0},{12,8},{1,5},{9,13},{5,1},{13,9},{2,6},{10,14},... | collective-permute-start | bytes 884744 | tf_op jit(solution)/shard_map/ppermute | solution.py:173
  26.6 5.8 %collective-permute-start.4 = (bf16[576,256]{1,0:T(8,128)(2,1)S(1)}, bf16[576,256]{1,0:T(8,128)(2,1)S(1)}, u32[]{:S(2)}, u32[]{:S(2)}) collective-permute-start(bf16[576,256]{1,0:T(8,128)(2,1)S(1)} %get-tuple-element.52), channel_id=1, source_target_pairs={{4,8},{8,4},{5,9},{9,5},{6,10},{10,6},{7,11},{11,7},{20,24},{24,20... | collective-permute-start | bytes 884744 | tf_op jit(solution)/shard_map/ppermute | solution.py:175
  34.4 9.3 %collective-permute-start.5 = (bf16[576,256]{1,0:T(8,128)(2,1)S(1)}, bf16[576,256]{1,0:T(8,128)(2,1)S(1)}, u32[]{:S(2)}, u32[]{:S(2)}) collective-permute-start(bf16[576,256]{1,0:T(8,128)(2,1)S(1)} %get-tuple-element.56), channel_id=1, source_target_pairs={{0,4},{8,12},{4,0},{12,8},{1,5},{9,13},{5,1},{13,9},{2,6},{10,14},... | collective-permute-start | bytes 884744 | tf_op jit(solution)/shard_map/ppermute | solution.py:173
  39.0 4.7 %collective-permute-start.6 = (bf16[576,256]{1,0:T(8,128)(2,1)S(1)}, bf16[576,256]{1,0:T(8,128)(2,1)S(1)}, u32[]{:S(2)}, u32[]{:S(2)}) collective-permute-start(bf16[576,256]{1,0:T(8,128)(2,1)S(1)} %get-tuple-element.57), channel_id=1, source_target_pairs={{4,8},{8,4},{5,9},{9,5},{6,10},{10,6},{7,11},{11,7},{20,24},{24,20... | collective-permute-start | bytes 884744 | tf_op jit(solution)/shard_map/ppermute | solution.py:175
  45.8 9.4 %collective-permute-start.7 = (bf16[576,256]{1,0:T(8,128)(2,1)S(1)}, bf16[576,256]{1,0:T(8,128)(2,1)S(1)}, u32[]{:S(2)}, u32[]{:S(2)}) collective-permute-start(bf16[576,256]{1,0:T(8,128)(2,1)S(1)} %get-tuple-element.61), channel_id=1, source_target_pairs={{0,4},{8,12},{4,0},{12,8},{1,5},{9,13},{5,1},{13,9},{2,6},{10,14},... | collective-permute-start | bytes 884744 | tf_op jit(solution)/shard_map/ppermute | solution.py:173
  50.4 4.7 %collective-permute-start.8 = (bf16[576,256]{1,0:T(8,128)(2,1)S(1)}, bf16[576,256]{1,0:T(8,128)(2,1)S(1)}, u32[]{:S(2)}, u32[]{:S(2)}) collective-permute-start(bf16[576,256]{1,0:T(8,128)(2,1)S(1)} %get-tuple-element.62), channel_id=1, source_target_pairs={{4,8},{8,4},{5,9},{9,5},{6,10},{10,6},{7,11},{11,7},{20,24},{24,20... | collective-permute-start | bytes 884744 | tf_op jit(solution)/shard_map/ppermute | solution.py:175
  55.7 10.8 %collective-permute-start.9 = (bf16[576,256]{1,0:T(8,128)(2,1)S(1)}, bf16[576,256]{1,0:T(8,128)(2,1)S(1)}, u32[]{:S(2)}, u32[]{:S(2)}) collective-permute-start(bf16[576,256]{1,0:T(8,128)(2,1)S(1)} %get-tuple-element.66), channel_id=1, source_target_pairs={{0,4},{8,12},{4,0},{12,8},{1,5},{9,13},{5,1},{13,9},{2,6},{10,14},... | collective-permute-start | bytes 884744 | tf_op jit(solution)/shard_map/ppermute | solution.py:173
  61.8 4.7 %collective-permute-start.10 = (bf16[576,256]{1,0:T(8,128)(2,1)S(1)}, bf16[576,256]{1,0:T(8,128)(2,1)S(1)}, u32[]{:S(2)}, u32[]{:S(2)}) collective-permute-start(bf16[576,256]{1,0:T(8,128)(2,1)S(1)} %get-tuple-element.67), channel_id=1, source_target_pairs={{4,8},{8,4},{5,9},{9,5},{6,10},{10,6},{7,11},{11,7},{20,24},{24,20... | collective-permute-start | bytes 884744 | tf_op jit(solution)/shard_map/ppermute | solution.py:175
  67.1 10.8 %collective-permute-start.11 = (bf16[576,256]{1,0:T(8,128)(2,1)S(1)}, bf16[576,256]{1,0:T(8,128)(2,1)S(1)}, u32[]{:S(2)}, u32[]{:S(2)}) collective-permute-start(bf16[576,256]{1,0:T(8,128)(2,1)S(1)} %get-tuple-element.71), channel_id=1, source_target_pairs={{0,4},{8,12},{4,0},{12,8},{1,5},{9,13},{5,1},{13,9},{2,6},{10,14},... | collective-permute-start | bytes 884744 | tf_op jit(solution)/shard_map/ppermute | solution.py:173
  73.3 4.7 %collective-permute-start.12 = (bf16[576,256]{1,0:T(8,128)(2,1)S(1)}, bf16[576,256]{1,0:T(8,128)(2,1)S(1)}, u32[]{:S(2)}, u32[]{:S(2)}) collective-permute-start(bf16[576,256]{1,0:T(8,128)(2,1)S(1)} %get-tuple-element.72), channel_id=1, source_target_pairs={{4,8},{8,4},{5,9},{9,5},{6,10},{10,6},{7,11},{11,7},{20,24},{24,20... | collective-permute-start | bytes 884744 | tf_op jit(solution)/shard_map/ppermute | solution.py:175
  80.0 10.7 %collective-permute-start.13 = (bf16[576,256]{1,0:T(8,128)(2,1)S(1)}, bf16[576,256]{1,0:T(8,128)(2,1)S(1)}, u32[]{:S(2)}, u32[]{:S(2)}) collective-permute-start(bf16[576,256]{1,0:T(8,128)(2,1)S(1)} %get-tuple-element.76), channel_id=1, source_target_pairs={{0,4},{8,12},{4,0},{12,8},{1,5},{9,13},{5,1},{13,9},{2,6},{10,14},... | collective-permute-start | bytes 884744 | tf_op jit(solution)/shard_map/ppermute | solution.py:173
  84.9 5.7 %collective-permute-start.14 = (bf16[576,256]{1,0:T(8,128)(2,1)S(1)}, bf16[576,256]{1,0:T(8,128)(2,1)S(1)}, u32[]{:S(2)}, u32[]{:S(2)}) collective-permute-start(bf16[576,256]{1,0:T(8,128)(2,1)S(1)} %get-tuple-element.77), channel_id=1, source_target_pairs={{4,8},{8,4},{5,9},{9,5},{6,10},{10,6},{7,11},{11,7},{20,24},{24,20... | collective-permute-start | bytes 884744 | tf_op jit(solution)/shard_map/ppermute | solution.py:175
  92.6 9.7 %collective-permute-start.15 = (bf16[576,256]{1,0:T(8,128)(2,1)S(1)}, bf16[576,256]{1,0:T(8,128)(2,1)S(1)}, u32[]{:S(2)}, u32[]{:S(2)}) collective-permute-start(bf16[576,256]{1,0:T(8,128)(2,1)S(1)} %get-tuple-element.81), channel_id=1, source_target_pairs={{0,4},{8,12},{4,0},{12,8},{1,5},{9,13},{5,1},{13,9},{2,6},{10,14},... | collective-permute-start | bytes 884744 | tf_op jit(solution)/shard_map/ppermute | solution.py:173
  97.6 4.7 %collective-permute-start.16 = (bf16[576,256]{1,0:T(8,128)(2,1)S(1)}, bf16[576,256]{1,0:T(8,128)(2,1)S(1)}, u32[]{:S(2)}, u32[]{:S(2)}) collective-permute-start(bf16[576,256]{1,0:T(8,128)(2,1)S(1)} %get-tuple-element.82), channel_id=1, source_target_pairs={{4,8},{8,4},{5,9},{9,5},{6,10},{10,6},{7,11},{11,7},{20,24},{24,20... | collective-permute-start | bytes 884744 | tf_op jit(solution)/shard_map/ppermute | solution.py:175
  102.3 2.9 %copy-start.9 = (bf16[576,256]{1,0:T(8,128)(2,1)}, bf16[576,256]{1,0:T(8,128)(2,1)S(1)}, u32[]{:S(2)}) copy-start(bf16[576,256]{1,0:T(8,128)(2,1)S(1)} %collective-permute-done.16.r2) | copy-start | bytes 884740
  105.2 2.1 %copy-start = (bf16[4,4,576,256]{3,2,1,0:T(8,128)(2,1)}, bf16[4,4,576,256]{3,2,1,0:T(8,128)(2,1)S(1)}, u32[]{:S(2)}) copy-start(bf16[4,4,576,256]{3,2,1,0:T(8,128)(2,1)S(1)} %get-tuple-element.87.state_in) | copy-start | bytes 14155780
  108.3 9.6 %collective-permute-start.17 = (bf16[576,256]{1,0:T(8,128)(2,1)}, bf16[576,256]{1,0:T(8,128)(2,1)}, u32[]{:S(2)}, u32[]{:S(2)}) collective-permute-start(bf16[576,256]{1,0:T(8,128)(2,1)} %get-tuple-element.86), channel_id=1, source_target_pairs={{0,4},{8,12},{4,0},{12,8},{1,5},{9,13},{5,1},{13,9},{2,6},{10,14},... | collective-permute-start | bytes 884744 | tf_op jit(solution)/shard_map/ppermute | solution.py:173
  118.0 2.3 %copy-start.1 = (bf16[4,4,576,256]{3,2,1,0:T(8,128)(2,1)S(1)}, bf16[4,4,576,256]{3,2,1,0:T(8,128)(2,1)}, u32[]{:S(2)}) copy-start(bf16[4,4,576,256]{3,2,1,0:T(8,128)(2,1)} %copy-done) | copy-start | bytes 14155780
  (6 other events, 7.4 us)
where the time goes:
time: 132 us
  waiting for transfers between devices  46.4 us (35%)
  starting transfers between devices  45.1 us (34%)
  Pallas kernels  20 us (15%)
  local copies, waits for them, and re-layouts  17.2 us (13%)
  between operations  1.59 us (1%)
  other arithmetic  1.42 us (1%)
    ppermute x9, waiting for transfers between devices, per_device(): r1 = lax.ppermute(o1, 'depth', swaps(0))  42.2 us
    ppermute x9, starting transfers between devices, per_device(): r1 = lax.ppermute(o1, 'depth', swaps(0))  37.2 us
    pallas_call x10, Pallas kernels, section(): pl.pallas_call(functools.partial(section_kernel, depth_n, src.shape[0]),...  20 us
    unnamed x24, local copies, waits for them, and re-layouts  11.4 us
    ppermute x7, starting transfers between devices, per_device(): r2 = lax.ppermute(o2, 'depth', swaps(1))  4.85 us
    ppermute x2, waiting for transfers between devices, windowed(): lax.ppermute(jnp.where(here == 0, tail, head), 'plane', [(0, 1), (1, 0)])  4.1 us
    ppermute x2, starting transfers between devices, windowed(): lax.ppermute(jnp.where(here == 0, tail, head), 'plane', [(0, 1), (1, 0)])  3.01 us
  transfers between devices with their start and end apart: 18, of which 10 were waited for; matrix products, arithmetic and copies ran while one was open for 1% of the time, Pallas kernels for 0%

commit v1 on v0

--- a/solution.py
+++ b/solution.py
@@ -8,7 +8,8 @@
 from jax.sharding import PartitionSpec as P
 
 NT = (((1,), (1,)), ((), ()))
-CHUNKS = 4
+CHUNKS = 8
+LAG = 2
 
 
 def section_kernel(
@@ -18,8 +19,8 @@
     rows = r1.shape[0]
     half = rows // 2
     window = mask.shape[2]
-    down_at = step - here
-    up_at = step - 2 * (depth_n - 1) + here
+    down_at = step - LAG * here
+    up_at = step - LAG * (2 * (depth_n - 1) - here)
     down_due = (down_at >= 0) & (down_at < chunks)
     up_due = (up_at >= 0) & (up_at < chunks)
     even = lax.rem(here, 2) == 0
@@ -95,6 +96,10 @@
             o1[...] = up[...]
 
 
+def rows_of(a):
+    return a.shape[0]
+
+
 def section(depth_n, sc, r1, r2, src, w, mask, state, top, bottom):
     in_vmem = pl.BlockSpec(memory_space=pltpu.VMEM)
     held = lambda a: pltpu.with_memory_space_constraint(a, pltpu.VMEM)
@@ -107,6 +112,7 @@
         scratch_shapes=[pltpu.VMEM(r1.shape, r1.dtype)],
         input_output_aliases={6: 2, 7: 3, 8: 4},
         compiler_params=pltpu.CompilerParams(vmem_limit_bytes=16 * 1024 * 1024),
+        cost_estimate=pl.CostEstimate(flops=2 * 6 * 3 * 2 * rows_of(r1) * 256 * 256 * 2, bytes_accessed=1 << 20, transcendentals=0),
     )(sc, *map(held, (r1, r2, src, w, mask, state, top, bottom)))
 
 
@@ -165,14 +171,16 @@
         pairs = [(i, i + 1) for i in range(first, depth_n - 1, 2)]
         return pairs + [(j, i) for i, j in pairs]
 
-    steps = chunks + 2 * (depth_n - 1)
+    steps = chunks + 2 * LAG * (depth_n - 1)
+    queue = [(r1, r2)] * LAG
     for step in range(steps):
         sc = jnp.stack([here, layer_count[0], jnp.int32(step)]).astype(jnp.int32)
+        r1, r2 = queue.pop(0)
         o1, o2, state, top, bottom = section(depth_n, sc, r1, r2, src, w, mask, state, top, bottom)
-        if step < steps - 1:
-            r1 = lax.ppermute(o1, "depth", swaps(0))
-            if 0 < step < steps - 2:
-                r2 = lax.ppermute(o2, "depth", swaps(1))
+        if step < steps - LAG:
+            n1 = lax.ppermute(o1, "depth", swaps(0))
+            n2 = lax.ppermute(o2, "depth", swaps(1)) if LAG <= step < steps - 2 * LAG else r2
+            queue.append((n1, n2))
 
     def leave(held):
         held = held.reshape(chunks, 2, share, window, block)

time: 132 us -> 109 us (0.83)
  waiting for transfers between devices: 46.4 us -> 6.62 us
  Pallas kernels: 20 us -> 37 us
  local copies, waits for them, and re-layouts: 17.2 us -> 8.31 us
  starting transfers between devices: 45.1 us -> 52.9 us
    ppermute x16 -> x32, waiting for transfers between devices: 42.3 us -> 4.18 us  [the longest x18 4.15 us: per_device(): n1 = lax.ppermute(o1, 'depth', swaps(0))]
    pallas_call x10 -> x20, Pallas kernels: 20 us -> 37 us  [section(): pl.pallas_call(functools.partial(section_kernel, depth_n, src.shape[0]),...]
    unnamed x24 -> x4, local copies, waits for them, and re-layouts: 11.4 us -> 1.13 us
    ppermute x16 -> x32, starting transfers between devices: 42 us -> 49.9 us  [the longest x18 40.5 us: per_device(): n1 = lax.ppermute(o1, 'depth', swaps(0))]
    transpose x4, local copies, waits for them, and re-layouts: 0.9 us -> 3.87 us  [leave(): return held.transpose(1, 0, 2, 3, 4).reshape(1, 2, sources, tile * block)]
    reshape x2 -> x0, local copies, waits for them, and re-layouts: 2.62 us -> none  [leave(): return held.transpose(1, 0, 2, 3, 4).reshape(1, 2, sources, tile * block)]
    ppermute x2, waiting for transfers between devices: 4.1 us -> 2.44 us  [windowed(): lax.ppermute(jnp.where(here == 0, tail, head), 'plane', [(0, 1), (1, 0)])]
    another operation x4 -> x3, local copies, waits for them, and re-layouts: 1.64 us -> 0.17 us  [the longest x1 1.46 us: per_device(): source[0].reshape(2, sources, tile, block)]
  transfers between devices with their start and end apart: 18 -> 34, of which waited for: 10 -> 4; matrix products, arithmetic and copies ran while one was open for 1% -> 3% of each run, Pallas kernels for 0% -> 29%
where the time goes in v1:
time: 109 us; the launch traced here: 108 us
  starting transfers between devices  52.9 us (49%)
  Pallas kernels  37 us (34%)
  local copies, waits for them, and re-layouts  8.31 us (8%)
  waiting for transfers between devices  6.62 us (6%)
  between operations  1.89 us (2%)
  other arithmetic  1.67 us (2%)
    ppermute x18, starting transfers between devices, per_device(): n1 = lax.ppermute(o1, 'depth', swaps(0))  40.5 us
    pallas_call x20, Pallas kernels, section(): pl.pallas_call(functools.partial(section_kernel, depth_n, src.shape[0]),...  37 us
    ppermute x14, starting transfers between devices, per_device(): lax.ppermute(o2, 'depth', swaps(1))  9.39 us
    ppermute x18, waiting for transfers between devices, per_device(): n1 = lax.ppermute(o1, 'depth', swaps(0))  4.15 us
    transpose x4, local copies, waits for them, and re-layouts, leave(): return held.transpose(1, 0, 2, 3, 4).reshape(1, 2, sources, tile * block)  3.87 us
    ppermute x2, starting transfers between devices, windowed(): lax.ppermute(jnp.where(here == 0, tail, head), 'plane', [(0, 1), (1, 0)])  3.01 us
    ppermute x2, waiting for transfers between devices, windowed(): lax.ppermute(jnp.where(here == 0, tail, head), 'plane', [(0, 1), (1, 0)])  2.44 us
  transfers between devices with their start and end apart: 34, of which 4 were waited for; matrix products, arithmetic and copies ran while one was open for 3% of the time, Pallas kernels for 29%

profile of v1, /device:TPU:0, one launch (start us, length us, event | category | flops | bytes accessed | tf_op | source)
XLA Modules:
  0.0 108.4 jit_solution(15112970173601126965)
XLA Ops:
  1.5 2.9 %collective-permute-start.1 = (s32[3,16,3]{1,2,0:T(4,128)S(1)}, s32[3,16,3]{1,2,0:T(4,128)S(1)}, u32[]{:S(2)}, u32[]{:S(2)}) collective-permute-start(s32[3,16,3]{1,2,0:T(4,128)S(1)} %slice_select_fusion), channel_id=1, source_target_pairs={{0,2},{2,0},{1,3},{3,1},{4,6},{6,4},{5,7},{7,5},{8,10},{10,8},{9,1... | collective-permute-start | bytes 1736 | tf_op jit(solution)/shard_map/ppermute | solution.py:125
  8.1 2.4 %collective-permute-done = bf16[2,8,16,256]{3,2,0,1:T(8,128)(2,1)S(1)} collective-permute-done((bf16[2,8,16,256]{3,2,0,1:T(8,128)(2,1)S(1)}, bf16[2,8,16,256]{3,2,0,1:T(8,128)(2,1)S(1)}, u32[]{:S(2)}, u32[]{:S(2)}) %collective-permute-start) | collective-permute-done | bytes 131104 | tf_op jit(solution)/shard_map/ppermute | solution.py:125
  13.0 2.6 %shard_map.59 = (bf16[288,256]{1,0:T(8,128)(2,1)S(1)}, bf16[288,256]{1,0:T(8,128)(2,1)}, bf16[8,4,288,256]{3,2,1,0:T(8,128)(2,1)S(1)}, bf16[8,288,256]{2,1,0:T(8,128)(2,1)S(1)}, bf16[8,288,256]{2,1,0:T(8,128)(2,1)S(1)}) custom-call(s32[3]{0:T(128)S(1)} %get-tuple-element.198.sc, ...), custom_call_target="tpu_custom_call", output_to_operand_aliasing={{2}: (6, {}), {3}: (7, {}), {4}: (8, {})} | custom-call | flops 2717908992 | bytes 1048576 | tf_op jit(solution)/shard_map/pallas_call | solution.py:107
  15.8 2.6 %shard_map.60 = (bf16[288,256]{1,0:T(8,128)(2,1)S(1)}, bf16[288,256]{1,0:T(8,128)(2,1)}, bf16[8,4,288,256]{3,2,1,0:T(8,128)(2,1)S(1)}, bf16[8,288,256]{2,1,0:T(8,128)(2,1)S(1)}, bf16[8,288,256]{2,1,0:T(8,128)(2,1)S(1)}) custom-call(s32[3]{0:T(128)S(1)} %get-tuple-element.199.sc, ...), custom_call_target="tpu_custom_call", output_to_operand_aliasing={{2}: (6, {}), {3}: (7, {}), {4}: (8, {})} | custom-call | flops 2717908992 | bytes 1048576 | tf_op jit(solution)/shard_map/pallas_call | solution.py:107
  18.8 3.5 %collective-permute-done.3.r1 = bf16[288,256]{1,0:T(8,128)(2,1)S(1)} collective-permute-done((bf16[288,256]{1,0:T(8,128)(2,1)S(1)}, bf16[288,256]{1,0:T(8,128)(2,1)S(1)}, u32[]{:S(2)}, u32[]{:S(2)}) %collective-permute-start.3) | collective-permute-done | bytes 147488 | tf_op jit(solution)/shard_map/ppermute | solution.py:181
  27.1 3.2 %collective-permute-start.4 = (bf16[288,256]{1,0:T(8,128)(2,1)S(1)}, bf16[288,256]{1,0:T(8,128)(2,1)S(1)}, u32[]{:S(2)}, u32[]{:S(2)}) collective-permute-start(bf16[288,256]{1,0:T(8,128)(2,1)S(1)} %get-tuple-element.104), channel_id=1, source_target_pairs={{0,4},{8,12},{4,0},{12,8},{1,5},{9,13},{5,1},{13,9},{2,6},{10,14},... | collective-permute-start | bytes 442376 | tf_op jit(solution)/shard_map/ppermute | solution.py:181
  30.9 1.9 %shard_map.63 = (bf16[288,256]{1,0:T(8,128)(2,1)S(1)}, bf16[288,256]{1,0:T(8,128)(2,1)S(1)}, bf16[8,4,288,256]{3,2,1,0:T(8,128)(2,1)S(1)}, bf16[8,288,256]{2,1,0:T(8,128)(2,1)S(1)}, bf16[8,288,256]{2,1,0:T(8,128)(2,1)S(1)}) custom-call(s32[3]{0:T(128)S(1)} %get-tuple-element.196.sc, ...), custom_call_target="tpu_custom_call", output_to_operand_aliasing={{2}: (6, {}), {3}: (7, {}), {4}: (8, {})} | custom-call | flops 2717908992 | bytes 1048576 | tf_op jit(solution)/shard_map/pallas_call | solution.py:107
  32.8 2.9 %collective-permute-start.10 = (bf16[288,256]{1,0:T(8,128)(2,1)S(1)}, bf16[288,256]{1,0:T(8,128)(2,1)S(1)}, u32[]{:S(2)}, u32[]{:S(2)}) collective-permute-start(bf16[288,256]{1,0:T(8,128)(2,1)S(1)} %get-tuple-element.116), channel_id=1, source_target_pairs={{0,4},{8,12},{4,0},{12,8},{1,5},{9,13},{5,1},{13,9},{2,6},{10,14},... | collective-permute-start | bytes 442376 | tf_op jit(solution)/shard_map/ppermute | solution.py:181
  36.5 1.9 %shard_map.64 = (bf16[288,256]{1,0:T(8,128)(2,1)S(1)}, bf16[288,256]{1,0:T(8,128)(2,1)S(1)}, bf16[8,4,288,256]{3,2,1,0:T(8,128)(2,1)S(1)}, bf16[8,288,256]{2,1,0:T(8,128)(2,1)S(1)}, bf16[8,288,256]{2,1,0:T(8,128)(2,1)S(1)}) custom-call(s32[3]{0:T(128)S(1)} %get-tuple-element.201.sc, ...), custom_call_target="tpu_custom_call", output_to_operand_aliasing={{2}: (6, {}), {3}: (7, {}), {4}: (8, {})} | custom-call | flops 2717908992 | bytes 1048576 | tf_op jit(solution)/shard_map/pallas_call | solution.py:107
  40.4 1.9 %shard_map.65 = (bf16[288,256]{1,0:T(8,128)(2,1)S(1)}, bf16[288,256]{1,0:T(8,128)(2,1)S(1)}, bf16[8,4,288,256]{3,2,1,0:T(8,128)(2,1)S(1)}, bf16[8,288,256]{2,1,0:T(8,128)(2,1)S(1)}, bf16[8,288,256]{2,1,0:T(8,128)(2,1)S(1)}) custom-call(s32[3]{0:T(128)S(1)} %get-tuple-element.195.sc, ...), custom_call_target="tpu_custom_call", output_to_operand_aliasing={{2}: (6, {}), {3}: (7, {}), {4}: (8, {})} | custom-call | flops 2717908992 | bytes 1048576 | tf_op jit(solution)/shard_map/pallas_call | solution.py:107
  42.4 2.5 %collective-permute-start.14 = (bf16[288,256]{1,0:T(8,128)(2,1)S(1)}, bf16[288,256]{1,0:T(8,128)(2,1)S(1)}, u32[]{:S(2)}, u32[]{:S(2)}) collective-permute-start(bf16[288,256]{1,0:T(8,128)(2,1)S(1)} %get-tuple-element.126), channel_id=1, source_target_pairs={{0,4},{8,12},{4,0},{12,8},{1,5},{9,13},{5,1},{13,9},{2,6},{10,14},... | collective-permute-start | bytes 442376 | tf_op jit(solution)/shard_map/ppermute | solution.py:181
  45.5 1.9 %shard_map.66 = (bf16[288,256]{1,0:T(8,128)(2,1)S(1)}, bf16[288,256]{1,0:T(8,128)(2,1)S(1)}, bf16[8,4,288,256]{3,2,1,0:T(8,128)(2,1)S(1)}, bf16[8,288,256]{2,1,0:T(8,128)(2,1)S(1)}, bf16[8,288,256]{2,1,0:T(8,128)(2,1)S(1)}) custom-call(s32[3]{0:T(128)S(1)} %get-tuple-element.202.sc, ...), custom_call_target="tpu_custom_call", output_to_operand_aliasing={{2}: (6, {}), {3}: (7, {}), {4}: (8, {})} | custom-call | flops 2717908992 | bytes 1048576 | tf_op jit(solution)/shard_map/pallas_call | solution.py:107
  47.5 2.1 %collective-permute-start.12 = (bf16[288,256]{1,0:T(8,128)(2,1)S(1)}, bf16[288,256]{1,0:T(8,128)(2,1)S(1)}, u32[]{:S(2)}, u32[]{:S(2)}) collective-permute-start(bf16[288,256]{1,0:T(8,128)(2,1)S(1)} %get-tuple-element.124), channel_id=1, source_target_pairs={{0,4},{8,12},{4,0},{12,8},{1,5},{9,13},{5,1},{13,9},{2,6},{10,14},... | collective-permute-start | bytes 442376 | tf_op jit(solution)/shard_map/ppermute | solution.py:181
  50.8 3.1 %collective-permute-start.18 = (bf16[288,256]{1,0:T(8,128)(2,1)S(1)}, bf16[288,256]{1,0:T(8,128)(2,1)S(1)}, u32[]{:S(2)}, u32[]{:S(2)}) collective-permute-start(bf16[288,256]{1,0:T(8,128)(2,1)S(1)} %get-tuple-element.136), channel_id=1, source_target_pairs={{0,4},{8,12},{4,0},{12,8},{1,5},{9,13},{5,1},{13,9},{2,6},{10,14},... | collective-permute-start | bytes 442376 | tf_op jit(solution)/shard_map/ppermute | solution.py:181
  55.1 3.9 %collective-permute-start.16 = (bf16[288,256]{1,0:T(8,128)(2,1)S(1)}, bf16[288,256]{1,0:T(8,128)(2,1)S(1)}, u32[]{:S(2)}, u32[]{:S(2)}) collective-permute-start(bf16[288,256]{1,0:T(8,128)(2,1)S(1)} %get-tuple-element.134), channel_id=1, source_target_pairs={{0,4},{8,12},{4,0},{12,8},{1,5},{9,13},{5,1},{13,9},{2,6},{10,14},... | collective-permute-start | bytes 442376 | tf_op jit(solution)/shard_map/ppermute | solution.py:181
  60.5 3.1 %collective-permute-start.22 = (bf16[288,256]{1,0:T(8,128)(2,1)S(1)}, bf16[288,256]{1,0:T(8,128)(2,1)S(1)}, u32[]{:S(2)}, u32[]{:S(2)}) collective-permute-start(bf16[288,256]{1,0:T(8,128)(2,1)S(1)} %get-tuple-element.146), channel_id=1, source_target_pairs={{0,4},{8,12},{4,0},{12,8},{1,5},{9,13},{5,1},{13,9},{2,6},{10,14},... | collective-permute-start | bytes 442376 | tf_op jit(solution)/shard_map/ppermute | solution.py:181
  64.8 3.9 %collective-permute-start.20 = (bf16[288,256]{1,0:T(8,128)(2,1)S(1)}, bf16[288,256]{1,0:T(8,128)(2,1)S(1)}, u32[]{:S(2)}, u32[]{:S(2)}) collective-permute-start(bf16[288,256]{1,0:T(8,128)(2,1)S(1)} %get-tuple-element.144), channel_id=1, source_target_pairs={{0,4},{8,12},{4,0},{12,8},{1,5},{9,13},{5,1},{13,9},{2,6},{10,14},... | collective-permute-start | bytes 442376 | tf_op jit(solution)/shard_map/ppermute | solution.py:181
  75.9 3.4 %collective-permute-start.24 = (bf16[288,256]{1,0:T(8,128)(2,1)S(1)}, bf16[288,256]{1,0:T(8,128)(2,1)S(1)}, u32[]{:S(2)}, u32[]{:S(2)}) collective-permute-start(bf16[288,256]{1,0:T(8,128)(2,1)S(1)} %get-tuple-element.154), channel_id=1, source_target_pairs={{0,4},{8,12},{4,0},{12,8},{1,5},{9,13},{5,1},{13,9},{2,6},{10,14},... | collective-permute-start | bytes 442376 | tf_op jit(solution)/shard_map/ppermute | solution.py:181
  86.3 2.8 %collective-permute-start.28 = (bf16[288,256]{1,0:T(8,128)(2,1)S(1)}, bf16[288,256]{1,0:T(8,128)(2,1)S(1)}, u32[]{:S(2)}, u32[]{:S(2)}) collective-permute-start(bf16[288,256]{1,0:T(8,128)(2,1)S(1)} %get-tuple-element.164), channel_id=1, source_target_pairs={{0,4},{8,12},{4,0},{12,8},{1,5},{9,13},{5,1},{13,9},{2,6},{10,14},... | collective-permute-start | bytes 442376 | tf_op jit(solution)/shard_map/ppermute | solution.py:181
  89.8 2.6 %shard_map.75 = (bf16[288,256]{1,0:T(8,128)(2,1)S(1)}, bf16[288,256]{1,0:T(8,128)(2,1)}, bf16[8,4,288,256]{3,2,1,0:T(8,128)(2,1)S(1)}, bf16[8,288,256]{2,1,0:T(8,128)(2,1)S(1)}, bf16[8,288,256]{2,1,0:T(8,128)(2,1)S(1)}) custom-call(s32[3]{0:T(128)S(1)} %get-tuple-element.190.sc, ...), custom_call_target="tpu_custom_call", output_to_operand_aliasing={{2}: (6, {}), {3}: (7, {}), {4}: (8, {})} | custom-call | flops 2717908992 | bytes 1048576 | tf_op jit(solution)/shard_map/pallas_call | solution.py:107
  93.6 2.6 %shard_map.76 = (bf16[288,256]{1,0:T(8,128)(2,1)S(1)}, bf16[288,256]{1,0:T(8,128)(2,1)}, bf16[8,4,288,256]{3,2,1,0:T(8,128)(2,1)S(1)}, bf16[8,288,256]{2,1,0:T(8,128)(2,1)S(1)}, bf16[8,288,256]{2,1,0:T(8,128)(2,1)S(1)}) custom-call(s32[3]{0:T(128)S(1)} %get-tuple-element.207.sc, ...), custom_call_target="tpu_custom_call", output_to_operand_aliasing={{2}: (6, {}), {3}: (7, {}), {4}: (8, {})} | custom-call | flops 2717908992 | bytes 1048576 | tf_op jit(solution)/shard_map/pallas_call | solution.py:107
  96.2 2.5 %collective-permute-start.32 = (bf16[288,256]{1,0:T(8,128)(2,1)S(1)}, bf16[288,256]{1,0:T(8,128)(2,1)S(1)}, u32[]{:S(2)}, u32[]{:S(2)}) collective-permute-start(bf16[288,256]{1,0:T(8,128)(2,1)S(1)} %get-tuple-element.174), channel_id=1, source_target_pairs={{0,4},{8,12},{4,0},{12,8},{1,5},{9,13},{5,1},{13,9},{2,6},{10,14},... | collective-permute-start | bytes 442376 | tf_op jit(solution)/shard_map/ppermute | solution.py:181
  98.7 2.6 %shard_map.77 = (bf16[288,256]{1,0:T(8,128)(2,1)}, bf16[288,256]{1,0:T(8,128)(2,1)}, bf16[8,4,288,256]{3,2,1,0:T(8,128)(2,1)S(1)}, bf16[8,288,256]{2,1,0:T(8,128)(2,1)S(1)}, bf16[8,288,256]{2,1,0:T(8,128)(2,1)S(1)}) custom-call(s32[3]{0:T(128)S(1)} %get-tuple-element.184.sc, ...), custom_call_target="tpu_custom_call", output_to_operand_aliasing={{2}: (6, {}), {3}: (7, {}), {4}: (8, {})} | custom-call | flops 2717908992 | bytes 1048576 | tf_op jit(solution)/shard_map/pallas_call | solution.py:107
  101.9 2.6 %shard_map.78 = (bf16[288,256]{1,0:T(8,128)(2,1)}, bf16[288,256]{1,0:T(8,128)(2,1)}, bf16[8,4,288,256]{3,2,1,0:T(8,128)(2,1)S(1)}, bf16[8,288,256]{2,1,0:T(8,128)(2,1)S(1)}, bf16[8,288,256]{2,1,0:T(8,128)(2,1)S(1)}) custom-call(s32[3]{0:T(128)S(1)} %pad_add_fusion.sc, ...), custom_call_target="tpu_custom_call", output_to_operand_aliasing={{2}: (6, {}), {3}: (7, {}), {4}: (8, {})} | custom-call | flops 2717908992 | bytes 1048576 | tf_op jit(solution)/shard_map/pallas_call | solution.py:107
  (89 shorter events, 41.0 us)
Async XLA Ops:
  1.5 6.5 %collective-permute-start.1 = (s32[3,16,3]{1,2,0:T(4,128)S(1)}, s32[3,16,3]{1,2,0:T(4,128)S(1)}, u32[]{:S(2)}, u32[]{:S(2)}) collective-permute-start(s32[3,16,3]{1,2,0:T(4,128)S(1)} %slice_select_fusion), channel_id=1, source_target_pairs={{0,2},{2,0},{1,3},{3,1},{4,6},{6,4},{5,7},{7,5},{8,10},{10,8},{9,1... | collective-permute-start | bytes 1736 | tf_op jit(solution)/shard_map/ppermute | solution.py:125
  15.6 6.7 %collective-permute-start.3 = (bf16[288,256]{1,0:T(8,128)(2,1)S(1)}, bf16[288,256]{1,0:T(8,128)(2,1)S(1)}, u32[]{:S(2)}, u32[]{:S(2)}) collective-permute-start(bf16[288,256]{1,0:T(8,128)(2,1)S(1)} %get-tuple-element.97), channel_id=1, source_target_pairs={{0,4},{8,12},{4,0},{12,8},{1,5},{9,13},{5,1},{13,9},{2,6},{10,14},... | collective-permute-start | bytes 442376 | tf_op jit(solution)/shard_map/ppermute | solution.py:181
  18.4 6.8 %collective-permute-start.2 = (bf16[288,256]{1,0:T(8,128)(2,1)S(1)}, bf16[288,256]{1,0:T(8,128)(2,1)S(1)}, u32[]{:S(2)}, u32[]{:S(2)}) collective-permute-start(bf16[288,256]{1,0:T(8,128)(2,1)S(1)} %get-tuple-element.96), channel_id=1, source_target_pairs={{0,4},{8,12},{4,0},{12,8},{1,5},{9,13},{5,1},{13,9},{2,6},{10,14},... | collective-permute-start | bytes 442376 | tf_op jit(solution)/shard_map/ppermute | solution.py:181
  24.2 6.7 %collective-permute-start.6 = (bf16[288,256]{1,0:T(8,128)(2,1)S(1)}, bf16[288,256]{1,0:T(8,128)(2,1)S(1)}, u32[]{:S(2)}, u32[]{:S(2)}) collective-permute-start(bf16[288,256]{1,0:T(8,128)(2,1)S(1)} %get-tuple-element.106), channel_id=1, source_target_pairs={{0,4},{8,12},{4,0},{12,8},{1,5},{9,13},{5,1},{13,9},{2,6},{10,14},... | collective-permute-start | bytes 442376 | tf_op jit(solution)/shard_map/ppermute | solution.py:181
  24.3 6.6 %collective-permute-start.7 = (bf16[288,256]{1,0:T(8,128)(2,1)S(1)}, bf16[288,256]{1,0:T(8,128)(2,1)S(1)}, u32[]{:S(2)}, u32[]{:S(2)}) collective-permute-start(bf16[288,256]{1,0:T(8,128)(2,1)S(1)} %get-tuple-element.107), channel_id=1, source_target_pairs={{4,8},{8,4},{5,9},{9,5},{6,10},{10,6},{7,11},{11,7},{20,24},{24,20... | collective-permute-start | bytes 442376 | tf_op jit(solution)/shard_map/ppermute | solution.py:182
  27.1 9.4 %collective-permute-start.4 = (bf16[288,256]{1,0:T(8,128)(2,1)S(1)}, bf16[288,256]{1,0:T(8,128)(2,1)S(1)}, u32[]{:S(2)}, u32[]{:S(2)}) collective-permute-start(bf16[288,256]{1,0:T(8,128)(2,1)S(1)} %get-tuple-element.104), channel_id=1, source_target_pairs={{0,4},{8,12},{4,0},{12,8},{1,5},{9,13},{5,1},{13,9},{2,6},{10,14},... | collective-permute-start | bytes 442376 | tf_op jit(solution)/shard_map/ppermute | solution.py:181
  30.2 6.2 %collective-permute-start.5 = (bf16[288,256]{1,0:T(8,128)(2,1)S(1)}, bf16[288,256]{1,0:T(8,128)(2,1)S(1)}, u32[]{:S(2)}, u32[]{:S(2)}) collective-permute-start(bf16[288,256]{1,0:T(8,128)(2,1)S(1)} %get-tuple-element.105), channel_id=1, source_target_pairs={{4,8},{8,4},{5,9},{9,5},{6,10},{10,6},{7,11},{11,7},{20,24},{24,20... | collective-permute-start | bytes 442376 | tf_op jit(solution)/shard_map/ppermute | solution.py:182
  32.8 7.6 %collective-permute-start.10 = (bf16[288,256]{1,0:T(8,128)(2,1)S(1)}, bf16[288,256]{1,0:T(8,128)(2,1)S(1)}, u32[]{:S(2)}, u32[]{:S(2)}) collective-permute-start(bf16[288,256]{1,0:T(8,128)(2,1)S(1)} %get-tuple-element.116), channel_id=1, source_target_pairs={{0,4},{8,12},{4,0},{12,8},{1,5},{9,13},{5,1},{13,9},{2,6},{10,14},... | collective-permute-start | bytes 442376 | tf_op jit(solution)/shard_map/ppermute | solution.py:181
  38.4 7.1 %collective-permute-start.8 = (bf16[288,256]{1,0:T(8,128)(2,1)S(1)}, bf16[288,256]{1,0:T(8,128)(2,1)S(1)}, u32[]{:S(2)}, u32[]{:S(2)}) collective-permute-start(bf16[288,256]{1,0:T(8,128)(2,1)S(1)} %get-tuple-element.114), channel_id=1, source_target_pairs={{0,4},{8,12},{4,0},{12,8},{1,5},{9,13},{5,1},{13,9},{2,6},{10,14},... | collective-permute-start | bytes 442376 | tf_op jit(solution)/shard_map/ppermute | solution.py:181
  42.4 7.8 %collective-permute-start.14 = (bf16[288,256]{1,0:T(8,128)(2,1)S(1)}, bf16[288,256]{1,0:T(8,128)(2,1)S(1)}, u32[]{:S(2)}, u32[]{:S(2)}) collective-permute-start(bf16[288,256]{1,0:T(8,128)(2,1)S(1)} %get-tuple-element.126), channel_id=1, source_target_pairs={{0,4},{8,12},{4,0},{12,8},{1,5},{9,13},{5,1},{13,9},{2,6},{10,14},... | collective-permute-start | bytes 442376 | tf_op jit(solution)/shard_map/ppermute | solution.py:181
  47.5 7.1 %collective-permute-start.12 = (bf16[288,256]{1,0:T(8,128)(2,1)S(1)}, bf16[288,256]{1,0:T(8,128)(2,1)S(1)}, u32[]{:S(2)}, u32[]{:S(2)}) collective-permute-start(bf16[288,256]{1,0:T(8,128)(2,1)S(1)} %get-tuple-element.124), channel_id=1, source_target_pairs={{0,4},{8,12},{4,0},{12,8},{1,5},{9,13},{5,1},{13,9},{2,6},{10,14},... | collective-permute-start | bytes 442376 | tf_op jit(solution)/shard_map/ppermute | solution.py:181
  50.8 9.1 %collective-permute-start.18 = (bf16[288,256]{1,0:T(8,128)(2,1)S(1)}, bf16[288,256]{1,0:T(8,128)(2,1)S(1)}, u32[]{:S(2)}, u32[]{:S(2)}) collective-permute-start(bf16[288,256]{1,0:T(8,128)(2,1)S(1)} %get-tuple-element.136), channel_id=1, source_target_pairs={{0,4},{8,12},{4,0},{12,8},{1,5},{9,13},{5,1},{13,9},{2,6},{10,14},... | collective-permute-start | bytes 442376 | tf_op jit(solution)/shard_map/ppermute | solution.py:181
  53.9 6.0 %collective-permute-start.19 = (bf16[288,256]{1,0:T(8,128)(2,1)S(1)}, bf16[288,256]{1,0:T(8,128)(2,1)S(1)}, u32[]{:S(2)}, u32[]{:S(2)}) collective-permute-start(bf16[288,256]{1,0:T(8,128)(2,1)S(1)} %get-tuple-element.137), channel_id=1, source_target_pairs={{4,8},{8,4},{5,9},{9,5},{6,10},{10,6},{7,11},{11,7},{20,24},{24,20... | collective-permute-start | bytes 442376 | tf_op jit(solution)/shard_map/ppermute | solution.py:182
  55.1 9.1 %collective-permute-start.16 = (bf16[288,256]{1,0:T(8,128)(2,1)S(1)}, bf16[288,256]{1,0:T(8,128)(2,1)S(1)}, u32[]{:S(2)}, u32[]{:S(2)}) collective-permute-start(bf16[288,256]{1,0:T(8,128)(2,1)S(1)} %get-tuple-element.134), channel_id=1, source_target_pairs={{0,4},{8,12},{4,0},{12,8},{1,5},{9,13},{5,1},{13,9},{2,6},{10,14},... | collective-permute-start | bytes 442376 | tf_op jit(solution)/shard_map/ppermute | solution.py:181
  60.5 8.9 %collective-permute-start.22 = (bf16[288,256]{1,0:T(8,128)(2,1)S(1)}, bf16[288,256]{1,0:T(8,128)(2,1)S(1)}, u32[]{:S(2)}, u32[]{:S(2)}) collective-permute-start(bf16[288,256]{1,0:T(8,128)(2,1)S(1)} %get-tuple-element.146), channel_id=1, source_target_pairs={{0,4},{8,12},{4,0},{12,8},{1,5},{9,13},{5,1},{13,9},{2,6},{10,14},... | collective-permute-start | bytes 442376 | tf_op jit(solution)/shard_map/ppermute | solution.py:181
  63.6 5.8 %collective-permute-start.23 = (bf16[288,256]{1,0:T(8,128)(2,1)S(1)}, bf16[288,256]{1,0:T(8,128)(2,1)S(1)}, u32[]{:S(2)}, u32[]{:S(2)}) collective-permute-start(bf16[288,256]{1,0:T(8,128)(2,1)S(1)} %get-tuple-element.147), channel_id=1, source_target_pairs={{4,8},{8,4},{5,9},{9,5},{6,10},{10,6},{7,11},{11,7},{20,24},{24,20... | collective-permute-start | bytes 442376 | tf_op jit(solution)/shard_map/ppermute | solution.py:182
  64.8 9.1 %collective-permute-start.20 = (bf16[288,256]{1,0:T(8,128)(2,1)S(1)}, bf16[288,256]{1,0:T(8,128)(2,1)S(1)}, u32[]{:S(2)}, u32[]{:S(2)}) collective-permute-start(bf16[288,256]{1,0:T(8,128)(2,1)S(1)} %get-tuple-element.144), channel_id=1, source_target_pairs={{0,4},{8,12},{4,0},{12,8},{1,5},{9,13},{5,1},{13,9},{2,6},{10,14},... | collective-permute-start | bytes 442376 | tf_op jit(solution)/shard_map/ppermute | solution.py:181
  71.4 8.6 %collective-permute-start.26 = (bf16[288,256]{1,0:T(8,128)(2,1)S(1)}, bf16[288,256]{1,0:T(8,128)(2,1)S(1)}, u32[]{:S(2)}, u32[]{:S(2)}) collective-permute-start(bf16[288,256]{1,0:T(8,128)(2,1)S(1)} %get-tuple-element.156), channel_id=1, source_target_pairs={{0,4},{8,12},{4,0},{12,8},{1,5},{9,13},{5,1},{13,9},{2,6},{10,14},... | collective-permute-start | bytes 442376 | tf_op jit(solution)/shard_map/ppermute | solution.py:181
  73.3 6.6 %collective-permute-start.27 = (bf16[288,256]{1,0:T(8,128)(2,1)S(1)}, bf16[288,256]{1,0:T(8,128)(2,1)S(1)}, u32[]{:S(2)}, u32[]{:S(2)}) collective-permute-start(bf16[288,256]{1,0:T(8,128)(2,1)S(1)} %get-tuple-element.157), channel_id=1, source_target_pairs={{4,8},{8,4},{5,9},{9,5},{6,10},{10,6},{7,11},{11,7},{20,24},{24,20... | collective-permute-start | bytes 442376 | tf_op jit(solution)/shard_map/ppermute | solution.py:182
  75.9 8.5 %collective-permute-start.24 = (bf16[288,256]{1,0:T(8,128)(2,1)S(1)}, bf16[288,256]{1,0:T(8,128)(2,1)S(1)}, u32[]{:S(2)}, u32[]{:S(2)}) collective-permute-start(bf16[288,256]{1,0:T(8,128)(2,1)S(1)} %get-tuple-element.154), channel_id=1, source_target_pairs={{0,4},{8,12},{4,0},{12,8},{1,5},{9,13},{5,1},{13,9},{2,6},{10,14},... | collective-permute-start | bytes 442376 | tf_op jit(solution)/shard_map/ppermute | solution.py:181
  81.9 7.9 %collective-permute-start.30 = (bf16[288,256]{1,0:T(8,128)(2,1)S(1)}, bf16[288,256]{1,0:T(8,128)(2,1)S(1)}, u32[]{:S(2)}, u32[]{:S(2)}) collective-permute-start(bf16[288,256]{1,0:T(8,128)(2,1)S(1)} %get-tuple-element.166), channel_id=1, source_target_pairs={{0,4},{8,12},{4,0},{12,8},{1,5},{9,13},{5,1},{13,9},{2,6},{10,14},... | collective-permute-start | bytes 442376 | tf_op jit(solution)/shard_map/ppermute | solution.py:181
  83.7 6.1 %collective-permute-start.31 = (bf16[288,256]{1,0:T(8,128)(2,1)S(1)}, bf16[288,256]{1,0:T(8,128)(2,1)S(1)}, u32[]{:S(2)}, u32[]{:S(2)}) collective-permute-start(bf16[288,256]{1,0:T(8,128)(2,1)S(1)} %get-tuple-element.167), channel_id=1, source_target_pairs={{4,8},{8,4},{5,9},{9,5},{6,10},{10,6},{7,11},{11,7},{20,24},{24,20... | collective-permute-start | bytes 442376 | tf_op jit(solution)/shard_map/ppermute | solution.py:182
  86.3 7.4 %collective-permute-start.28 = (bf16[288,256]{1,0:T(8,128)(2,1)S(1)}, bf16[288,256]{1,0:T(8,128)(2,1)S(1)}, u32[]{:S(2)}, u32[]{:S(2)}) collective-permute-start(bf16[288,256]{1,0:T(8,128)(2,1)S(1)} %get-tuple-element.164), channel_id=1, source_target_pairs={{0,4},{8,12},{4,0},{12,8},{1,5},{9,13},{5,1},{13,9},{2,6},{10,14},... | collective-permute-start | bytes 442376 | tf_op jit(solution)/shard_map/ppermute | solution.py:181
  92.4 6.4 %collective-permute-start.33 = (bf16[288,256]{1,0:T(8,128)(2,1)S(1)}, bf16[288,256]{1,0:T(8,128)(2,1)S(1)}, u32[]{:S(2)}, u32[]{:S(2)}) collective-permute-start(bf16[288,256]{1,0:T(8,128)(2,1)S(1)} %get-tuple-element.175), channel_id=1, source_target_pairs={{0,4},{8,12},{4,0},{12,8},{1,5},{9,13},{5,1},{13,9},{2,6},{10,14},... | collective-permute-start | bytes 442376 | tf_op jit(solution)/shard_map/ppermute | solution.py:181
  (12 other events, 55.8 us)

commit v2 on v1

v2 whole, which is shorter than its diff:
```python
import functools

import jax
import jax.numpy as jnp
from jax import lax
from jax.experimental import pallas as pl
from jax.experimental.pallas import tpu as pltpu
from jax.sharding import PartitionSpec as P

NT = (((1,), (1,)), ((), ()))
CHUNKS = 8
LAG = 2
VMEM_LIMIT = 16 * 1024 * 1024


def apply_layer(x, w, mask, slot):
    rows, window = x.shape[0], mask.shape[2]
    half = rows // 2
    wide = x.astype(jnp.float32)
    before = pltpu.roll(wide, 1, 0) * jnp.tile(mask[slot, 0], (rows // window, 2))
    after = pltpu.roll(wide, rows - 1, 0) * jnp.tile(mask[slot, 1], (rows // window, 2))
    total = lax.dot_general(before.astype(jnp.bfloat16), w[slot, 0], NT, preferred_element_type=jnp.float32)
    total = total + lax.dot_general(x, w[slot, 1], NT, preferred_element_type=jnp.float32)
    total = total + lax.dot_general(after.astype(jnp.bfloat16), w[slot, 2], NT, preferred_element_type=jnp.float32)
    block = total.shape[1] // 2
    real = total[:half, :block] - total[half:, block:]
    imag = total[half:, :block] + total[:half, block:]
    return real, imag


def section_kernel(depth_n, chunks, step, plan, *refs):
    refs = dict(zip(plan, refs))
    sc, src, w, mask, state = (refs[name] for name in ("sc", "src", "w", "mask", "state"))
    here, count = sc[0], sc[1]
    down_at = step - LAG * here
    up_at = step - LAG * (2 * (depth_n - 1) - here)
    even = lax.rem(here, 2) == 0
    odd = jnp.logical_not(even)
    half = src.shape[1] // 2

    def choose(first, second, then):
        pl.when(even)(lambda: then(refs.get(first)))
        pl.when(odd)(lambda: then(refs.get(second)))

    def down():
        def enter(arrived):
            x = src[down_at]
            if arrived is not None:
                x = (arrived[...].astype(jnp.float32) + x.astype(jnp.float32)).astype(jnp.bfloat16)
            state[down_at, 0] = x

        choose("r2", "r1", enter)

        def layer(c, _):
            real, imag = apply_layer(state[down_at, c], w, mask, c)
            state[down_at, c + 1, :half] = real.astype(jnp.bfloat16)
            state[down_at, c + 1, half:] = imag.astype(jnp.bfloat16)
            return 0

        lax.fori_loop(0, count, layer, 0)
        refs["bottom"][down_at] = state[down_at, count]

        def send(out):
            if out is not None:
                out[...] = state[down_at, count]

        choose("o1", "o2", send)

    def rise():
        up = refs["up"]

        def enter(arrived):
            up[...] = jnp.zeros_like(up) if arrived is None else arrived[...]

        choose("r1", "r2", enter)

        def layer(i, _):
            c = count - 1 - i
            real, imag = apply_layer(up[...], w, mask, c)
            up[:half] = (real + state[up_at, c, :half].astype(jnp.float32)).astype(jnp.bfloat16)
            up[half:] = (imag + state[up_at, c, half:].astype(jnp.float32)).astype(jnp.bfloat16)
            return 0

        lax.fori_loop(0, count, layer, 0)
        refs["top"][up_at] = up[...]

        def send(out):
            if out is not None:
                out[...] = up[...]

        choose("o2", "o1", send)

    if "bottom" in refs:
        pl.when((down_at >= 0) & (down_at < chunks))(down)
    if "top" in refs:
        pl.when((up_at >= 0) & (up_at < chunks))(rise)


def held(a):
    return pltpu.with_memory_space_constraint(a, pltpu.VMEM)


def section(depth_n, step, sc, fixed, arrived, kept, sends):
    src = fixed["src"]
    chunks, rows, block = src.shape
    cap = fixed["w"].shape[0]
    in_vmem = pl.BlockSpec(memory_space=pltpu.VMEM)
    shapes = {"state": (chunks, cap + 1, rows, block), "bottom": src.shape, "top": src.shape}
    writes = ["state"] * ("bottom" in kept) + [name for name in ("bottom", "top") if name in kept]
    ins = {**fixed, **arrived, **{name: a for name, a in kept.items() if a is not None}}
    outs = writes + list(sends)
    aliases = {1 + list(ins).index(name): outs.index(name) for name in writes if name in ins}
    plan = ["sc"] + list(ins) + outs + ["up"]
    results = pl.pallas_call(
        functools.partial(section_kernel, depth_n, chunks, step, plan),
        out_shape=tuple(pltpu.VMEM(shapes.get(name, (rows, block)), src.dtype) for name in outs),
        in_specs=[pl.BlockSpec(memory_space=pltpu.SMEM)] + [in_vmem] * len(ins),
        out_specs=(in_vmem,) * len(outs),
        scratch_shapes=[pltpu.VMEM((rows, block), src.dtype)],
        input_output_aliases=aliases,
        compiler_params=pltpu.CompilerParams(vmem_limit_bytes=VMEM_LIMIT),
        cost_estimate=pl.CostEstimate(
            flops=12 * rows * 6 * block * block, bytes_accessed=8 * rows * block, transcendentals=0
        ),
    )(pltpu.with_memory_space_constraint(sc, pltpu.SMEM), *map(held, ins.values()))
    return dict(zip(outs, results))


LANES = 128


def enter_kernel(source, pool, own_mask, sc, src, mask, w, natural, wide, sems):
    own = pl.multiple_of(sc[2], 16)
    bring = pltpu.make_async_copy(pool, w, sems.at[0])
    load = pltpu.make_async_copy(source, natural, sems.at[1])
    load.start()
    bring.start()
    sources, window = src.shape[0], wide.shape[2] // src.shape[0]
    tile = own_mask.shape[0]
    cap = mask.shape[0]
    columns = own_mask[...].astype(jnp.float32)
    for slot in range(cap):
        for side in range(2):
            at = slot * 3 + 2 * side
            mask[slot, side, pl.ds(own, tile), :] = jnp.broadcast_to(columns[:, at : at + 1], (tile, LANES))
    load.wait()
    spread(natural, wide, own, tile, sources, window)
    for part in range(2):
        for s in range(sources):
            for h in range(2):
                src[s, pl.ds(part * window + own, tile), h * LANES : (h + 1) * LANES] = wide[
                    part, h, pl.ds(s * window + own, tile), :
                ].astype(src.dtype)
    bring.wait()


def spread(natural, wide, first, count, sources, window):
    def block(n, _):
        for part in range(2):
            for h in range(2):
                lanes = pl.ds(pl.multiple_of((2 * n + h) * LANES, LANES), LANES)
                wide[part, h, pl.ds(first + n, sources, stride=window), :] = natural[part, :, lanes].astype(jnp.float32)
        return 0

    lax.fori_loop(0, count, block, 0, unroll=4)


def join_kernel(arrived, sc, src_in, mask_in, src, mask, wide):
    own = sc[2]
    sources, window = src.shape[0], wide.shape[2] // src.shape[0]
    cap = mask.shape[0]
    halo = arrived.shape[2] // (2 * LANES)
    at = pl.multiple_of(jnp.where(own == 0, window - halo, 0), 16)
    spread(arrived, wide, at, halo, sources, window)
    for part in range(2):
        for s in range(sources):
            for h in range(2):
                src[s, pl.ds(part * window + at, halo), h * LANES : (h + 1) * LANES] = wide[
                    part, h, pl.ds(s * window + at, halo), :
                ].astype(src.dtype)
    columns = arrived[:, :, 2 * halo * LANES :].astype(jnp.float32).reshape(-1, LANES)[:halo]
    place = lax.broadcasted_iota(jnp.int32, (window, LANES), 0)
    for slot in range(cap):
        for side in range(2):
            j = slot * 3 + 2 * side
            mask[slot, side, pl.ds(at, halo), :] = jnp.broadcast_to(
                columns[:, j : j + 1], (halo, LANES)
            )
            end = 0 if side == 0 else window - 1
            mask[slot, side] = jnp.where(place == end, 0.0, mask[slot, side])


def leave_kernel(result, sc, out, wide, natural, sem):
    own = sc[2]
    sources, window = result.shape[0], result.shape[1] // 2
    tile = out.shape[2] // (2 * LANES)
    for part in range(2):
        for s in range(sources):
            for h in range(2):
                wide[part, h, pl.ds(s * window, window), :] = result[
                    s, pl.ds(part * window, window), h * LANES : (h + 1) * LANES
                ].astype(jnp.float32)

    def block(n, _):
        for part in range(2):
            for h in range(2):
                lanes = pl.ds(pl.multiple_of((2 * n + h) * LANES, LANES), LANES)
                natural[part, :, lanes] = wide[part, h, pl.ds(own + n, sources, stride=window), :].astype(out.dtype)
        return 0

    lax.fori_loop(0, tile, block, 0, unroll=4)
    copy = pltpu.make_async_copy(natural, out, sem)
    copy.start()
    copy.wait()


IN_VMEM = pl.BlockSpec(memory_space=pltpu.VMEM)
IN_SMEM = pl.BlockSpec(memory_space=pltpu.SMEM)
IN_HBM = pl.BlockSpec(memory_space=pltpu.HBM)


def in_smem(a):
    return pltpu.with_memory_space_constraint(a, pltpu.SMEM)


def cost(size):
    return pl.CostEstimate(flops=0, bytes_accessed=size, transcendentals=0)


def per_device(source, pool, near_mask, layer_count):
    depth_n = lax.axis_size("depth")
    planes = lax.axis_size("plane")
    here = lax.axis_index("depth")
    plane = lax.axis_index("plane")
    cap = pool.shape[0]
    block = pool.shape[-1]
    sources = source.shape[2]
    tile = source.shape[3] // block
    blocks = tile * planes
    halo = min(4 * depth_n, tile) if planes == 2 else 4 * depth_n
    window = tile + halo if planes == 2 else min(blocks, tile + 2 * halo)
    start = jnp.clip(plane * tile - halo, 0, blocks - window)
    own = plane * tile - start
    chunks = sources
    rows = 2 * window
    params = pltpu.CompilerParams(vmem_limit_bytes=VMEM_LIMIT)
    bf16, f32 = jnp.bfloat16, jnp.float32

    sc = jnp.stack([here, layer_count[0], own]).astype(jnp.int32)
    cells = source[0]
    weights = pool.reshape(cap, 3, 2 * block, block)
    wide = pltpu.VMEM((2, 2, sources * window, LANES), f32)
    if planes == 2:
        columns = near_mask.transpose(1, 0, 2).reshape(tile, cap * 3).astype(bf16)
        columns = jnp.pad(columns, ((0, 0), (0, LANES - cap * 3)))
        sent = jnp.where(
            plane == 0,
            jnp.concatenate([cells[:, :, (tile - halo) * block :], beside(columns[tile - halo :], sources)], axis=2),
            jnp.concatenate([cells[:, :, : halo * block], beside(columns[:halo], sources)], axis=2),
        )
        arrived = lax.ppermute(sent, "plane", [(0, 1), (1, 0)])
        src, mask, w = pl.pallas_call(
            enter_kernel,
            out_shape=(
                pltpu.VMEM((chunks, rows, block), bf16),
                pltpu.VMEM((cap, 2, window, LANES), f32),
                pltpu.VMEM(weights.shape, bf16),
            ),
            in_specs=[IN_HBM, IN_HBM, IN_VMEM, IN_SMEM],
            out_specs=(IN_VMEM,) * 3,
            scratch_shapes=[pltpu.VMEM(cells.shape, bf16), wide, pltpu.SemaphoreType.DMA((2,))],
            compiler_params=params,
            cost_estimate=cost(1 << 23),
        )(cells, weights, columns, in_smem(sc))
        src, mask = pl.pallas_call(
            join_kernel,
            out_shape=(pltpu.VMEM(src.shape, bf16), pltpu.VMEM(mask.shape, f32)),
            in_specs=[IN_VMEM, IN_SMEM, IN_VMEM, IN_VMEM],
            out_specs=(IN_VMEM,) * 2,
            input_output_aliases={2: 0, 3: 1},
            scratch_shapes=[wide],
            compiler_params=params,
            cost_estimate=cost(1 << 20),
        )(held(arrived), in_smem(sc), held(src), held(mask))
    else:
        whole = lax.all_gather(cells, "plane", axis=2, tiled=True)
        src = lax.dynamic_slice_in_dim(whole, start * block, window * block, axis=2)
        src = src.reshape(2, sources, window, block).transpose(1, 0, 2, 3).reshape(chunks, rows, block)
        present = lax.all_gather(near_mask, "plane", axis=1, tiled=True)
        present = lax.dynamic_slice_in_dim(present, start, window, axis=1).astype(f32)
        place = jnp.arange(window)[None, :]
        before = jnp.where(place == 0, 0.0, present[:, :, 0])
        after = jnp.where(place == window - 1, 0.0, present[:, :, 2])
        mask = jnp.broadcast_to(jnp.stack([before, after], axis=1)[..., None], (cap, 2, window, LANES))
        w = weights

    def swaps(first):
        pairs = [(i, i + 1) for i in range(first, depth_n - 1, 2)]
        return pairs + [(j, i) for i, j in pairs]

    last_down = chunks + LAG * (depth_n - 1)
    first_up = LAG * (depth_n - 1)
    steps = chunks + 2 * LAG * (depth_n - 1)
    queue = [{}] * LAG
    kept = {}
    for step in range(steps):
        sends = {}
        if step < steps - LAG:
            sends["o1"] = ("r1", swaps(0))
        if LAG <= step < steps - 2 * LAG:
            sends["o2"] = ("r2", swaps(1))
        held_now = {"state": kept.get("state")}
        if step < last_down:
            held_now["bottom"] = kept.get("bottom")
        if step >= first_up:
            held_now["top"] = kept.get("top")
        out = section(depth_n, step, sc, dict(src=src, w=w, mask=mask), queue.pop(0), held_now, sends)
        queue.append({to: lax.ppermute(out.pop(name), "depth", pairs) for name, (to, pairs) in sends.items()})
        kept.update(out)

    def leave(result):
        return pl.pallas_call(
            leave_kernel,
            out_shape=jax.ShapeDtypeStruct(cells.shape, bf16),
            in_specs=[IN_VMEM, IN_SMEM],
            out_specs=IN_HBM,
            scratch_shapes=[wide, pltpu.VMEM(cells.shape, bf16), pltpu.SemaphoreType.DMA],
            compiler_params=params,
            cost_estimate=cost(1 << 23),
        )(held(result), in_smem(sc))[None]

    return (leave(kept["top"]), leave(kept["bottom"]))


def beside(columns, sources):
    lines = 2 * sources
    folds = -(-columns.shape[0] // lines)
    columns = jnp.pad(columns, ((0, folds * lines - columns.shape[0]), (0, 0)))
    return columns.reshape(folds, 2, sources, LANES).transpose(1, 2, 0, 3).reshape(2, sources, folds * LANES)


def solution(mesh):
    return jax.shard_map(
        per_device,
        mesh=mesh,
        in_specs=(
            P("depth", None, ("group", "batch"), "plane"),
            P("depth", None, None, None, None),
            P("depth", "plane", None),
            P("depth"),
        ),
        out_specs=(
            P("depth", None, ("group", "batch"), "plane"),
            P("depth", None, ("group", "batch"), "plane"),
        ),
        check_vma=False,
    )
```

time: 109 us -> 106 us (0.972)
  local copies, waits for them, and re-layouts: 8.31 us -> 2.84 us
  Pallas kernels: 37 us -> 41.4 us
  waiting for transfers between devices: 6.62 us -> 4.22 us
    pallas_call x20 -> x24, Pallas kernels: 37 us -> 41.4 us  [the longest x20 33.3 us: section(): pl.pallas_call(functools.partial(section_kernel, depth_n, chunks, step, p...]
    transpose x4 -> x0, local copies, waits for them, and re-layouts: 3.87 us -> none  [leave(): return held.transpose(1, 0, 2, 3, 4).reshape(1, 2, sources, tile * block)]
    ppermute x34 -> x33, waiting for transfers between devices: 6.62 us -> 4.22 us  [the longest x32 4.21 us: per_device(): lax.ppermute(out.pop(name), 'depth', pairs)]
    concatenate x1 -> x0, local copies, waits for them, and re-layouts: 1.45 us -> none  [windowed(): first = jnp.concatenate([cells, arrived], axis=dim)]
    select_n x4 -> x1, other arithmetic: 1.33 us -> 0.04 us  [per_device(): jnp.where(plane == 0, jnp.concatenate([cells[:, :, (tile - halo) * block:...]
    ppermute x34 -> x33, starting transfers between devices: 52.9 us -> 52.9 us  [the longest x32 49.9 us: per_device(): lax.ppermute(out.pop(name), 'depth', pairs)]
  transfers between devices with their start and end apart: 34 -> 33, of which waited for: 4 -> 2; matrix products, arithmetic and copies ran while one was open for 3% -> 0% of each run, Pallas kernels for 29% -> 33%
where the time goes in v2:
time: 106 us; the launch traced here: 104 us
  starting transfers between devices  52.9 us (50%)
  Pallas kernels  41.4 us (39%)
  waiting for transfers between devices  4.22 us (4%)
  local copies, waits for them, and re-layouts  2.84 us (3%)
  between operations  2.01 us (2%)
    ppermute x32, starting transfers between devices, per_device(): lax.ppermute(out.pop(name), 'depth', pairs)  49.9 us
    pallas_call x20, Pallas kernels, section(): pl.pallas_call(functools.partial(section_kernel, depth_n, chunks, step, p...  33.3 us
    pallas_call x2, Pallas kernels, leave(): pl.pallas_call(leave_kernel, out_shape=jax.ShapeDtypeStruct(cells.shape,...  5.29 us
    ppermute x32, waiting for transfers between devices, per_device(): lax.ppermute(out.pop(name), 'depth', pairs)  4.21 us
    ppermute x1, starting transfers between devices, per_device(): arrived = lax.ppermute(sent, 'plane', [(0, 1), (1, 0)])  3 us
  transfers between devices with their start and end apart: 33, of which 2 were waited for; matrix products, arithmetic and copies ran while one was open for 0% of the time, Pallas kernels for 33%

profile of v2, /device:TPU:0, one launch (start us, length us, event | category | flops | bytes accessed | tf_op | source)
XLA Modules:
  0.0 104.3 jit_solution(13194074955628557779)
XLA Ops:
  2.6 3.0 %collective-permute-start = (bf16[2,8,4224]{2,1,0:T(8,128)(2,1)S(1)}, bf16[2,8,4224]{2,1,0:T(8,128)(2,1)S(1)}, u32[]{:S(2)}, u32[]{:S(2)}) collective-permute-start(bf16[2,8,4224]{2,1,0:T(8,128)(2,1)S(1)} %maximum_select_fusion), channel_id=1, source_target_pairs={{0,2},{2,0},{1,3},{3,1},{4,6},{6,4},{5,7},{7,5},{8,10},{10,8},{9,1... | collective-permute-start | bytes 405512 | tf_op jit(solution)/shard_map/ppermute | solution.py:261
  8.1 2.1 %shard_map.59 = (bf16[8,288,256]{2,1,0:T(8,128)(2,1)S(1)}, f32[3,2,144,128]{3,2,1,0:T(8,128)S(1)}, bf16[3,3,512,256]{3,2,1,0:T(8,128)(2,1)S(1)}) custom-call(bf16[2,8,32768]{2,1,0:T(8,128)(2,1)S(1)} %bitcast.16, bf16[3,3,512,256]{3,2,1,0:T(8,128)(2,1)S(1)} %bitcast.14, bf16[128,128]{1,0:T(8,128)(2,1)S(1)} %pad.4.own_mask, s32[3]{0:T(128)S(1)} %pad_add_fusion.sc.refs_0_), custom_call_target="tpu_custom_call" | custom-call | bytes 8388608 | tf_op jit(solution)/shard_map/pallas_call | solution.py:262
  15.5 3.9 %collective-permute-done.2.refs_4_ = bf16[288,256]{1,0:T(8,128)(2,1)S(1)} collective-permute-done((bf16[288,256]{1,0:T(8,128)(2,1)S(1)}, bf16[288,256]{1,0:T(8,128)(2,1)S(1)}, u32[]{:S(2)}, u32[]{:S(2)}) %collective-permute-start.2) | collective-permute-done | bytes 147488 | tf_op jit(solution)/shard_map/ppermute | solution.py:318
  24.0 3.1 %collective-permute-start.3 = (bf16[288,256]{1,0:T(8,128)(2,1)S(1)}, bf16[288,256]{1,0:T(8,128)(2,1)S(1)}, u32[]{:S(2)}, u32[]{:S(2)}) collective-permute-start(bf16[288,256]{1,0:T(8,128)(2,1)S(1)} %get-tuple-element.92), channel_id=1, source_target_pairs={{0,4},{8,12},{4,0},{12,8},{1,5},{9,13},{5,1},{13,9},{2,6},{10,14},... | collective-permute-start | bytes 442376 | tf_op jit(solution)/shard_map/ppermute | solution.py:318
  30.0 3.3 %collective-permute-start.9 = (bf16[288,256]{1,0:T(8,128)(2,1)S(1)}, bf16[288,256]{1,0:T(8,128)(2,1)S(1)}, u32[]{:S(2)}, u32[]{:S(2)}) collective-permute-start(bf16[288,256]{1,0:T(8,128)(2,1)S(1)} %get-tuple-element.102), channel_id=1, source_target_pairs={{0,4},{8,12},{4,0},{12,8},{1,5},{9,13},{5,1},{13,9},{2,6},{10,14},... | collective-permute-start | bytes 442376 | tf_op jit(solution)/shard_map/ppermute | solution.py:318
  39.9 2.5 %collective-permute-start.13 = (bf16[288,256]{1,0:T(8,128)(2,1)S(1)}, bf16[288,256]{1,0:T(8,128)(2,1)S(1)}, u32[]{:S(2)}, u32[]{:S(2)}) collective-permute-start(bf16[288,256]{1,0:T(8,128)(2,1)S(1)} %get-tuple-element.111), channel_id=1, source_target_pairs={{0,4},{8,12},{4,0},{12,8},{1,5},{9,13},{5,1},{13,9},{2,6},{10,14},... | collective-permute-start | bytes 442376 | tf_op jit(solution)/shard_map/ppermute | solution.py:318
  44.9 2.1 %collective-permute-start.11 = (bf16[288,256]{1,0:T(8,128)(2,1)S(1)}, bf16[288,256]{1,0:T(8,128)(2,1)S(1)}, u32[]{:S(2)}, u32[]{:S(2)}) collective-permute-start(bf16[288,256]{1,0:T(8,128)(2,1)S(1)} %get-tuple-element.109), channel_id=1, source_target_pairs={{0,4},{8,12},{4,0},{12,8},{1,5},{9,13},{5,1},{13,9},{2,6},{10,14},... | collective-permute-start | bytes 442376 | tf_op jit(solution)/shard_map/ppermute | solution.py:318
  48.3 3.1 %collective-permute-start.17 = (bf16[288,256]{1,0:T(8,128)(2,1)S(1)}, bf16[288,256]{1,0:T(8,128)(2,1)S(1)}, u32[]{:S(2)}, u32[]{:S(2)}) collective-permute-start(bf16[288,256]{1,0:T(8,128)(2,1)S(1)} %get-tuple-element.121), channel_id=1, source_target_pairs={{0,4},{8,12},{4,0},{12,8},{1,5},{9,13},{5,1},{13,9},{2,6},{10,14},... | collective-permute-start | bytes 442376 | tf_op jit(solution)/shard_map/ppermute | solution.py:318
  52.6 4.4 %collective-permute-start.15 = (bf16[288,256]{1,0:T(8,128)(2,1)S(1)}, bf16[288,256]{1,0:T(8,128)(2,1)S(1)}, u32[]{:S(2)}, u32[]{:S(2)}) collective-permute-start(bf16[288,256]{1,0:T(8,128)(2,1)S(1)} %get-tuple-element.119), channel_id=1, source_target_pairs={{0,4},{8,12},{4,0},{12,8},{1,5},{9,13},{5,1},{13,9},{2,6},{10,14},... | collective-permute-start | bytes 442376 | tf_op jit(solution)/shard_map/ppermute | solution.py:318
  58.3 3.2 %collective-permute-start.21 = (bf16[288,256]{1,0:T(8,128)(2,1)S(1)}, bf16[288,256]{1,0:T(8,128)(2,1)S(1)}, u32[]{:S(2)}, u32[]{:S(2)}) collective-permute-start(bf16[288,256]{1,0:T(8,128)(2,1)S(1)} %get-tuple-element.131), channel_id=1, source_target_pairs={{0,4},{8,12},{4,0},{12,8},{1,5},{9,13},{5,1},{13,9},{2,6},{10,14},... | collective-permute-start | bytes 442376 | tf_op jit(solution)/shard_map/ppermute | solution.py:318
  62.8 4.3 %collective-permute-start.19 = (bf16[288,256]{1,0:T(8,128)(2,1)S(1)}, bf16[288,256]{1,0:T(8,128)(2,1)S(1)}, u32[]{:S(2)}, u32[]{:S(2)}) collective-permute-start(bf16[288,256]{1,0:T(8,128)(2,1)S(1)} %get-tuple-element.129), channel_id=1, source_target_pairs={{0,4},{8,12},{4,0},{12,8},{1,5},{9,13},{5,1},{13,9},{2,6},{10,14},... | collective-permute-start | bytes 442376 | tf_op jit(solution)/shard_map/ppermute | solution.py:318
  67.7 2.0 %shard_map.73 = (bf16[8,4,288,256]{3,2,1,0:T(8,128)(2,1)S(1)}, bf16[8,288,256]{2,1,0:T(8,128)(2,1)S(1)}, bf16[8,288,256]{2,1,0:T(8,128)(2,1)S(1)}, bf16[288,256]{1,0:T(8,128)(2,1)S(1)}, bf16[288,256]{1,0:T(8,128)(2,1)S(1)}) custom-call(s32[3]{0:T(128)S(1)} %pad_add_fusion.sc.refs_0_, ...), custom_call_target="tpu_custom_call", output_to_operand_aliasing={{0}: (6, {}), {1}: (7, {}), {2}: (8, {})} | custom-call | flops 1358954496 | bytes 589824 | tf_op jit(solution)/shard_map/pallas_call | solution.py:114
  72.2 2.1 %shard_map.74 = (bf16[8,4,288,256]{3,2,1,0:T(8,128)(2,1)S(1)}, bf16[8,288,256]{2,1,0:T(8,128)(2,1)S(1)}, bf16[8,288,256]{2,1,0:T(8,128)(2,1)S(1)}, bf16[288,256]{1,0:T(8,128)(2,1)S(1)}, bf16[288,256]{1,0:T(8,128)(2,1)S(1)}) custom-call(s32[3]{0:T(128)S(1)} %pad_add_fusion.sc.refs_0_, ...), custom_call_target="tpu_custom_call", output_to_operand_aliasing={{0}: (6, {}), {1}: (7, {}), {2}: (8, {})} | custom-call | flops 1358954496 | bytes 589824 | tf_op jit(solution)/shard_map/pallas_call | solution.py:114
  77.0 2.0 %shard_map.75 = (bf16[8,288,256]{2,1,0:T(8,128)(2,1)S(1)}, bf16[288,256]{1,0:T(8,128)(2,1)S(1)}, bf16[288,256]{1,0:T(8,128)(2,1)S(1)}) custom-call(s32[3]{0:T(128)S(1)} %pad_add_fusion.sc.refs_0_, bf16[8,288,256]{2,1,0:T(8,128)(2,1)S(1)} %get-tuple-element.81.refs_1_, ...), custom_call_target="tpu_custom_call", output_to_operand_aliasing={{0}: (7, {})} | custom-call | flops 1358954496 | bytes 589824 | tf_op jit(solution)/shard_map/pallas_call | solution.py:114
  78.9 2.1 %collective-permute-start.29 = (bf16[288,256]{1,0:T(8,128)(2,1)S(1)}, bf16[288,256]{1,0:T(8,128)(2,1)S(1)}, u32[]{:S(2)}, u32[]{:S(2)}) collective-permute-start(bf16[288,256]{1,0:T(8,128)(2,1)S(1)} %get-tuple-element.148), channel_id=1, source_target_pairs={{0,4},{8,12},{4,0},{12,8},{1,5},{9,13},{5,1},{13,9},{2,6},{10,14},... | collective-permute-start | bytes 442376 | tf_op jit(solution)/shard_map/ppermute | solution.py:318
  81.7 2.0 %shard_map.76 = (bf16[8,288,256]{2,1,0:T(8,128)(2,1)S(1)}, bf16[288,256]{1,0:T(8,128)(2,1)S(1)}, bf16[288,256]{1,0:T(8,128)(2,1)S(1)}) custom-call(s32[3]{0:T(128)S(1)} %pad_add_fusion.sc.refs_0_, bf16[8,288,256]{2,1,0:T(8,128)(2,1)S(1)} %get-tuple-element.81.refs_1_, ...), custom_call_target="tpu_custom_call", output_to_operand_aliasing={{0}: (7, {})} | custom-call | flops 1358954496 | bytes 589824 | tf_op jit(solution)/shard_map/pallas_call | solution.py:114
  83.7 2.6 %collective-permute-start.27 = (bf16[288,256]{1,0:T(8,128)(2,1)S(1)}, bf16[288,256]{1,0:T(8,128)(2,1)S(1)}, u32[]{:S(2)}, u32[]{:S(2)}) collective-permute-start(bf16[288,256]{1,0:T(8,128)(2,1)S(1)} %get-tuple-element.146), channel_id=1, source_target_pairs={{0,4},{8,12},{4,0},{12,8},{1,5},{9,13},{5,1},{13,9},{2,6},{10,14},... | collective-permute-start | bytes 442376 | tf_op jit(solution)/shard_map/ppermute | solution.py:318
  87.0 1.9 %shard_map.77 = (bf16[8,288,256]{2,1,0:T(8,128)(2,1)S(1)}, bf16[288,256]{1,0:T(8,128)(2,1)S(1)}) custom-call(s32[3]{0:T(128)S(1)} %pad_add_fusion.sc.refs_0_, bf16[8,288,256]{2,1,0:T(8,128)(2,1)S(1)} %get-tuple-element.81.refs_1_, bf16[3,3,512,256]{3,2,1,0:T(8,128)(2,1)S(1)} %get-tuple-element.82.refs_2_, ...), custom_call_target="tpu_custom_call", output_to_operand_aliasing={{0}: (7, {})} | custom-call | flops 1358954496 | bytes 589824 | tf_op jit(solution)/shard_map/pallas_call | solution.py:114
  90.8 1.9 %shard_map.78 = (bf16[8,288,256]{2,1,0:T(8,128)(2,1)S(1)}, bf16[288,256]{1,0:T(8,128)(2,1)S(1)}) custom-call(s32[3]{0:T(128)S(1)} %pad_add_fusion.sc.refs_0_, bf16[8,288,256]{2,1,0:T(8,128)(2,1)S(1)} %get-tuple-element.81.refs_1_, bf16[3,3,512,256]{3,2,1,0:T(8,128)(2,1)S(1)} %get-tuple-element.82.refs_2_, ...), custom_call_target="tpu_custom_call", output_to_operand_aliasing={{0}: (7, {})} | custom-call | flops 1358954496 | bytes 589824 | tf_op jit(solution)/shard_map/pallas_call | solution.py:114
  92.8 2.1 %collective-permute-start.31 = (bf16[288,256]{1,0:T(8,128)(2,1)S(1)}, bf16[288,256]{1,0:T(8,128)(2,1)S(1)}, u32[]{:S(2)}, u32[]{:S(2)}) collective-permute-start(bf16[288,256]{1,0:T(8,128)(2,1)S(1)} %get-tuple-element.152), channel_id=1, source_target_pairs={{0,4},{8,12},{4,0},{12,8},{1,5},{9,13},{5,1},{13,9},{2,6},{10,14},... | collective-permute-start | bytes 442376 | tf_op jit(solution)/shard_map/ppermute | solution.py:318
  94.9 2.6 %shard_map.82 = bf16[2,8,32768]{2,1,0:T(8,128)(2,1)} custom-call(bf16[8,288,256]{2,1,0:T(8,128)(2,1)S(1)} %get-tuple-element.155.result, s32[3]{0:T(128)S(1)} %pad_add_fusion.sc.refs_0_), custom_call_target="tpu_custom_call" | custom-call | bytes 8388608 | tf_op jit(solution)/shard_map/pallas_call | solution.py:322
  97.6 1.9 %shard_map.79.refs_6_ = bf16[8,288,256]{2,1,0:T(8,128)(2,1)S(1)} custom-call(s32[3]{0:T(128)S(1)} %pad_add_fusion.sc.refs_0_, bf16[8,288,256]{2,1,0:T(8,128)(2,1)S(1)} %get-tuple-element.81.refs_1_, bf16[3,3,512,256]{3,2,1,0:T(8,128)(2,1)S(1)} %get-tuple-element.82.refs_2_, ...), custom_call_target="tpu_custom_call", output_to_operand_aliasing={{}: (6, {})} | custom-call | flops 1358954496 | bytes 589824 | tf_op jit(solution)/shard_map/pallas_call | solution.py:114
  99.5 1.9 %shard_map.80.result = bf16[8,288,256]{2,1,0:T(8,128)(2,1)S(1)} custom-call(s32[3]{0:T(128)S(1)} %pad_add_fusion.sc.refs_0_, bf16[8,288,256]{2,1,0:T(8,128)(2,1)S(1)} %get-tuple-element.81.refs_1_, bf16[3,3,512,256]{3,2,1,0:T(8,128)(2,1)S(1)} %get-tuple-element.82.refs_2_, ...), custom_call_target="tpu_custom_call", output_to_operand_aliasing={{}: (6, {})} | custom-call | flops 1358954496 | bytes 589824 | tf_op jit(solution)/shard_map/pallas_call | solution.py:114
  101.5 2.6 %shard_map.81 = bf16[2,8,32768]{2,1,0:T(8,128)(2,1)} custom-call(bf16[8,288,256]{2,1,0:T(8,128)(2,1)S(1)} %shard_map.80.result, s32[3]{0:T(128)S(1)} %pad_add_fusion.sc.refs_0_), custom_call_target="tpu_custom_call" | custom-call | bytes 8388608 | tf_op jit(solution)/shard_map/pallas_call | solution.py:322
  (78 shorter events, 39.5 us)
Async XLA Ops:
  2.6 7.5 %collective-permute-start = (bf16[2,8,4224]{2,1,0:T(8,128)(2,1)S(1)}, bf16[2,8,4224]{2,1,0:T(8,128)(2,1)S(1)}, u32[]{:S(2)}, u32[]{:S(2)}) collective-permute-start(bf16[2,8,4224]{2,1,0:T(8,128)(2,1)S(1)} %maximum_select_fusion), channel_id=1, source_target_pairs={{0,2},{2,0},{1,3},{3,1},{4,6},{6,4},{5,7},{7,5},{8,10},{10,8},{9,1... | collective-permute-start | bytes 405512 | tf_op jit(solution)/shard_map/ppermute | solution.py:261
  12.8 6.6 %collective-permute-start.2 = (bf16[288,256]{1,0:T(8,128)(2,1)S(1)}, bf16[288,256]{1,0:T(8,128)(2,1)S(1)}, u32[]{:S(2)}, u32[]{:S(2)}) collective-permute-start(bf16[288,256]{1,0:T(8,128)(2,1)S(1)} %get-tuple-element.87), channel_id=1, source_target_pairs={{0,4},{8,12},{4,0},{12,8},{1,5},{9,13},{5,1},{13,9},{2,6},{10,14},... | collective-permute-start | bytes 442376 | tf_op jit(solution)/shard_map/ppermute | solution.py:318
  15.0 7.1 %collective-permute-start.1 = (bf16[288,256]{1,0:T(8,128)(2,1)S(1)}, bf16[288,256]{1,0:T(8,128)(2,1)S(1)}, u32[]{:S(2)}, u32[]{:S(2)}) collective-permute-start(bf16[288,256]{1,0:T(8,128)(2,1)S(1)} %get-tuple-element.86), channel_id=1, source_target_pairs={{0,4},{8,12},{4,0},{12,8},{1,5},{9,13},{5,1},{13,9},{2,6},{10,14},... | collective-permute-start | bytes 442376 | tf_op jit(solution)/shard_map/ppermute | solution.py:318
  21.3 6.7 %collective-permute-start.5 = (bf16[288,256]{1,0:T(8,128)(2,1)S(1)}, bf16[288,256]{1,0:T(8,128)(2,1)S(1)}, u32[]{:S(2)}, u32[]{:S(2)}) collective-permute-start(bf16[288,256]{1,0:T(8,128)(2,1)S(1)} %get-tuple-element.94), channel_id=1, source_target_pairs={{0,4},{8,12},{4,0},{12,8},{1,5},{9,13},{5,1},{13,9},{2,6},{10,14},... | collective-permute-start | bytes 442376 | tf_op jit(solution)/shard_map/ppermute | solution.py:318
  21.4 6.6 %collective-permute-start.6 = (bf16[288,256]{1,0:T(8,128)(2,1)S(1)}, bf16[288,256]{1,0:T(8,128)(2,1)S(1)}, u32[]{:S(2)}, u32[]{:S(2)}) collective-permute-start(bf16[288,256]{1,0:T(8,128)(2,1)S(1)} %get-tuple-element.95), channel_id=1, source_target_pairs={{4,8},{8,4},{5,9},{9,5},{6,10},{10,6},{7,11},{11,7},{20,24},{24,20... | collective-permute-start | bytes 442376 | tf_op jit(solution)/shard_map/ppermute | solution.py:318
  24.0 9.9 %collective-permute-start.3 = (bf16[288,256]{1,0:T(8,128)(2,1)S(1)}, bf16[288,256]{1,0:T(8,128)(2,1)S(1)}, u32[]{:S(2)}, u32[]{:S(2)}) collective-permute-start(bf16[288,256]{1,0:T(8,128)(2,1)S(1)} %get-tuple-element.92), channel_id=1, source_target_pairs={{0,4},{8,12},{4,0},{12,8},{1,5},{9,13},{5,1},{13,9},{2,6},{10,14},... | collective-permute-start | bytes 442376 | tf_op jit(solution)/shard_map/ppermute | solution.py:318
  27.1 6.8 %collective-permute-start.4 = (bf16[288,256]{1,0:T(8,128)(2,1)S(1)}, bf16[288,256]{1,0:T(8,128)(2,1)S(1)}, u32[]{:S(2)}, u32[]{:S(2)}) collective-permute-start(bf16[288,256]{1,0:T(8,128)(2,1)S(1)} %get-tuple-element.93), channel_id=1, source_target_pairs={{4,8},{8,4},{5,9},{9,5},{6,10},{10,6},{7,11},{11,7},{20,24},{24,20... | collective-permute-start | bytes 442376 | tf_op jit(solution)/shard_map/ppermute | solution.py:318
  30.0 7.9 %collective-permute-start.9 = (bf16[288,256]{1,0:T(8,128)(2,1)S(1)}, bf16[288,256]{1,0:T(8,128)(2,1)S(1)}, u32[]{:S(2)}, u32[]{:S(2)}) collective-permute-start(bf16[288,256]{1,0:T(8,128)(2,1)S(1)} %get-tuple-element.102), channel_id=1, source_target_pairs={{0,4},{8,12},{4,0},{12,8},{1,5},{9,13},{5,1},{13,9},{2,6},{10,14},... | collective-permute-start | bytes 442376 | tf_op jit(solution)/shard_map/ppermute | solution.py:318
  35.9 7.1 %collective-permute-start.7 = (bf16[288,256]{1,0:T(8,128)(2,1)S(1)}, bf16[288,256]{1,0:T(8,128)(2,1)S(1)}, u32[]{:S(2)}, u32[]{:S(2)}) collective-permute-start(bf16[288,256]{1,0:T(8,128)(2,1)S(1)} %get-tuple-element.100), channel_id=1, source_target_pairs={{0,4},{8,12},{4,0},{12,8},{1,5},{9,13},{5,1},{13,9},{2,6},{10,14},... | collective-permute-start | bytes 442376 | tf_op jit(solution)/shard_map/ppermute | solution.py:318
  39.9 7.8 %collective-permute-start.13 = (bf16[288,256]{1,0:T(8,128)(2,1)S(1)}, bf16[288,256]{1,0:T(8,128)(2,1)S(1)}, u32[]{:S(2)}, u32[]{:S(2)}) collective-permute-start(bf16[288,256]{1,0:T(8,128)(2,1)S(1)} %get-tuple-element.111), channel_id=1, source_target_pairs={{0,4},{8,12},{4,0},{12,8},{1,5},{9,13},{5,1},{13,9},{2,6},{10,14},... | collective-permute-start | bytes 442376 | tf_op jit(solution)/shard_map/ppermute | solution.py:318
  44.9 7.1 %collective-permute-start.11 = (bf16[288,256]{1,0:T(8,128)(2,1)S(1)}, bf16[288,256]{1,0:T(8,128)(2,1)S(1)}, u32[]{:S(2)}, u32[]{:S(2)}) collective-permute-start(bf16[288,256]{1,0:T(8,128)(2,1)S(1)} %get-tuple-element.109), channel_id=1, source_target_pairs={{0,4},{8,12},{4,0},{12,8},{1,5},{9,13},{5,1},{13,9},{2,6},{10,14},... | collective-permute-start | bytes 442376 | tf_op jit(solution)/shard_map/ppermute | solution.py:318
  48.3 9.4 %collective-permute-start.17 = (bf16[288,256]{1,0:T(8,128)(2,1)S(1)}, bf16[288,256]{1,0:T(8,128)(2,1)S(1)}, u32[]{:S(2)}, u32[]{:S(2)}) collective-permute-start(bf16[288,256]{1,0:T(8,128)(2,1)S(1)} %get-tuple-element.121), channel_id=1, source_target_pairs={{0,4},{8,12},{4,0},{12,8},{1,5},{9,13},{5,1},{13,9},{2,6},{10,14},... | collective-permute-start | bytes 442376 | tf_op jit(solution)/shard_map/ppermute | solution.py:318
  51.4 6.3 %collective-permute-start.18 = (bf16[288,256]{1,0:T(8,128)(2,1)S(1)}, bf16[288,256]{1,0:T(8,128)(2,1)S(1)}, u32[]{:S(2)}, u32[]{:S(2)}) collective-permute-start(bf16[288,256]{1,0:T(8,128)(2,1)S(1)} %get-tuple-element.122), channel_id=1, source_target_pairs={{4,8},{8,4},{5,9},{9,5},{6,10},{10,6},{7,11},{11,7},{20,24},{24,20... | collective-permute-start | bytes 442376 | tf_op jit(solution)/shard_map/ppermute | solution.py:318
  52.6 9.5 %collective-permute-start.15 = (bf16[288,256]{1,0:T(8,128)(2,1)S(1)}, bf16[288,256]{1,0:T(8,128)(2,1)S(1)}, u32[]{:S(2)}, u32[]{:S(2)}) collective-permute-start(bf16[288,256]{1,0:T(8,128)(2,1)S(1)} %get-tuple-element.119), channel_id=1, source_target_pairs={{0,4},{8,12},{4,0},{12,8},{1,5},{9,13},{5,1},{13,9},{2,6},{10,14},... | collective-permute-start | bytes 442376 | tf_op jit(solution)/shard_map/ppermute | solution.py:318
  58.3 9.4 %collective-permute-start.21 = (bf16[288,256]{1,0:T(8,128)(2,1)S(1)}, bf16[288,256]{1,0:T(8,128)(2,1)S(1)}, u32[]{:S(2)}, u32[]{:S(2)}) collective-permute-start(bf16[288,256]{1,0:T(8,128)(2,1)S(1)} %get-tuple-element.131), channel_id=1, source_target_pairs={{0,4},{8,12},{4,0},{12,8},{1,5},{9,13},{5,1},{13,9},{2,6},{10,14},... | collective-permute-start | bytes 442376 | tf_op jit(solution)/shard_map/ppermute | solution.py:318
  61.5 6.2 %collective-permute-start.22 = (bf16[288,256]{1,0:T(8,128)(2,1)S(1)}, bf16[288,256]{1,0:T(8,128)(2,1)S(1)}, u32[]{:S(2)}, u32[]{:S(2)}) collective-permute-start(bf16[288,256]{1,0:T(8,128)(2,1)S(1)} %get-tuple-element.132), channel_id=1, source_target_pairs={{4,8},{8,4},{5,9},{9,5},{6,10},{10,6},{7,11},{11,7},{20,24},{24,20... | collective-permute-start | bytes 442376 | tf_op jit(solution)/shard_map/ppermute | solution.py:318
  62.8 9.4 %collective-permute-start.19 = (bf16[288,256]{1,0:T(8,128)(2,1)S(1)}, bf16[288,256]{1,0:T(8,128)(2,1)S(1)}, u32[]{:S(2)}, u32[]{:S(2)}) collective-permute-start(bf16[288,256]{1,0:T(8,128)(2,1)S(1)} %get-tuple-element.129), channel_id=1, source_target_pairs={{0,4},{8,12},{4,0},{12,8},{1,5},{9,13},{5,1},{13,9},{2,6},{10,14},... | collective-permute-start | bytes 442376 | tf_op jit(solution)/shard_map/ppermute | solution.py:318
  69.7 7.3 %collective-permute-start.25 = (bf16[288,256]{1,0:T(8,128)(2,1)S(1)}, bf16[288,256]{1,0:T(8,128)(2,1)S(1)}, u32[]{:S(2)}, u32[]{:S(2)}) collective-permute-start(bf16[288,256]{1,0:T(8,128)(2,1)S(1)} %get-tuple-element.142), channel_id=1, source_target_pairs={{0,4},{8,12},{4,0},{12,8},{1,5},{9,13},{5,1},{13,9},{2,6},{10,14},... | collective-permute-start | bytes 442376 | tf_op jit(solution)/shard_map/ppermute | solution.py:318
  74.4 7.3 %collective-permute-start.23 = (bf16[288,256]{1,0:T(8,128)(2,1)S(1)}, bf16[288,256]{1,0:T(8,128)(2,1)S(1)}, u32[]{:S(2)}, u32[]{:S(2)}) collective-permute-start(bf16[288,256]{1,0:T(8,128)(2,1)S(1)} %get-tuple-element.139), channel_id=1, source_target_pairs={{0,4},{8,12},{4,0},{12,8},{1,5},{9,13},{5,1},{13,9},{2,6},{10,14},... | collective-permute-start | bytes 442376 | tf_op jit(solution)/shard_map/ppermute | solution.py:318
  78.9 8.0 %collective-permute-start.29 = (bf16[288,256]{1,0:T(8,128)(2,1)S(1)}, bf16[288,256]{1,0:T(8,128)(2,1)S(1)}, u32[]{:S(2)}, u32[]{:S(2)}) collective-permute-start(bf16[288,256]{1,0:T(8,128)(2,1)S(1)} %get-tuple-element.148), channel_id=1, source_target_pairs={{0,4},{8,12},{4,0},{12,8},{1,5},{9,13},{5,1},{13,9},{2,6},{10,14},... | collective-permute-start | bytes 442376 | tf_op jit(solution)/shard_map/ppermute | solution.py:318
  81.0 6.0 %collective-permute-start.30 = (bf16[288,256]{1,0:T(8,128)(2,1)S(1)}, bf16[288,256]{1,0:T(8,128)(2,1)S(1)}, u32[]{:S(2)}, u32[]{:S(2)}) collective-permute-start(bf16[288,256]{1,0:T(8,128)(2,1)S(1)} %get-tuple-element.149), channel_id=1, source_target_pairs={{4,8},{8,4},{5,9},{9,5},{6,10},{10,6},{7,11},{11,7},{20,24},{24,20... | collective-permute-start | bytes 442376 | tf_op jit(solution)/shard_map/ppermute | solution.py:318
  83.7 7.1 %collective-permute-start.27 = (bf16[288,256]{1,0:T(8,128)(2,1)S(1)}, bf16[288,256]{1,0:T(8,128)(2,1)S(1)}, u32[]{:S(2)}, u32[]{:S(2)}) collective-permute-start(bf16[288,256]{1,0:T(8,128)(2,1)S(1)} %get-tuple-element.146), channel_id=1, source_target_pairs={{0,4},{8,12},{4,0},{12,8},{1,5},{9,13},{5,1},{13,9},{2,6},{10,14},... | collective-permute-start | bytes 442376 | tf_op jit(solution)/shard_map/ppermute | solution.py:318
  88.9 8.6 %collective-permute-start.32 = (bf16[288,256]{1,0:T(8,128)(2,1)S(1)}, bf16[288,256]{1,0:T(8,128)(2,1)S(1)}, u32[]{:S(2)}, u32[]{:S(2)}) collective-permute-start(bf16[288,256]{1,0:T(8,128)(2,1)S(1)} %get-tuple-element.153), channel_id=1, source_target_pairs={{0,4},{8,12},{4,0},{12,8},{1,5},{9,13},{5,1},{13,9},{2,6},{10,14},... | collective-permute-start | bytes 442376 | tf_op jit(solution)/shard_map/ppermute | solution.py:318
  92.8 6.8 %collective-permute-start.31 = (bf16[288,256]{1,0:T(8,128)(2,1)S(1)}, bf16[288,256]{1,0:T(8,128)(2,1)S(1)}, u32[]{:S(2)}, u32[]{:S(2)}) collective-permute-start(bf16[288,256]{1,0:T(8,128)(2,1)S(1)} %get-tuple-element.152), channel_id=1, source_target_pairs={{0,4},{8,12},{4,0},{12,8},{1,5},{9,13},{5,1},{13,9},{2,6},{10,14},... | collective-permute-start | bytes 442376 | tf_op jit(solution)/shard_map/ppermute | solution.py:318
  (11 other events, 54.0 us)

commit v3 on v2

--- a/solution.py
+++ b/solution.py
@@ -45,9 +45,17 @@
     def down():
         def enter(arrived):
             x = src[down_at]
-            if arrived is not None:
-                x = (arrived[...].astype(jnp.float32) + x.astype(jnp.float32)).astype(jnp.bfloat16)
-            state[down_at, 0] = x
+            if arrived is None:
+                state[down_at, 0] = x
+                return
+
+            @pl.when(here == 0)
+            def _():
+                state[down_at, 0] = x
+
+            @pl.when(here > 0)
+            def _():
+                state[down_at, 0] = (arrived[...].astype(jnp.float32) + x.astype(jnp.float32)).astype(jnp.bfloat16)
 
         choose("r2", "r1", enter)
 
@@ -70,7 +78,15 @@
         up = refs["up"]
 
         def enter(arrived):
-            up[...] = jnp.zeros_like(up) if arrived is None else arrived[...]
+            if arrived is not None:
+
+                @pl.when(here < depth_n - 1)
+                def _():
+                    up[...] = arrived[...]
+
+            @pl.when(here == depth_n - 1)
+            def _():
+                up[...] = jnp.zeros_like(up)
 
         choose("r1", "r2", enter)
 
@@ -214,6 +230,11 @@
     copy.wait()
 
 
+def scalars_kernel(facts, sc):
+    for i in range(sc.shape[0]):
+        sc[i] = facts[i, 0]
+
+
 IN_VMEM = pl.BlockSpec(memory_space=pltpu.VMEM)
 IN_SMEM = pl.BlockSpec(memory_space=pltpu.SMEM)
 IN_HBM = pl.BlockSpec(memory_space=pltpu.HBM)
@@ -232,6 +253,7 @@
     planes = lax.axis_size("plane")
     here = lax.axis_index("depth")
     plane = lax.axis_index("plane")
+    cores = lax.axis_size("batch")
     cap = pool.shape[0]
     block = pool.shape[-1]
     sources = source.shape[2]
@@ -246,7 +268,14 @@
     params = pltpu.CompilerParams(vmem_limit_bytes=VMEM_LIMIT)
     bf16, f32 = jnp.bfloat16, jnp.float32
 
-    sc = jnp.stack([here, layer_count[0], own]).astype(jnp.int32)
+    facts = jnp.stack([here, layer_count[0], own]).astype(jnp.int32)
+    facts = jnp.broadcast_to(jnp.pad(facts, (0, 5))[:, None], (8, LANES))
+    sc = pl.pallas_call(
+        scalars_kernel,
+        out_shape=pltpu.SMEM((3,), jnp.int32),
+        in_specs=[IN_VMEM],
+        out_specs=IN_SMEM,
+    )(held(facts))
     cells = source[0]
     weights = pool.reshape(cap, 3, 2 * block, block)
     wide = pltpu.VMEM((2, 2, sources * window, LANES), f32)
@@ -296,7 +325,10 @@
 
     def swaps(first):
         pairs = [(i, i + 1) for i in range(first, depth_n - 1, 2)]
-        return pairs + [(j, i) for i, j in pairs]
+        alone = sorted(set(range(depth_n)) - {i for pair in pairs for i in pair})
+        moves = [(i * cores + c, j * cores + c) for i, j in pairs for c in range(cores)]
+        moves += [(i * cores + c, i * cores + c + 1) for i in alone for c in range(0, cores - 1, 2)]
+        return moves + [(j, i) for i, j in moves]
 
     last_down = chunks + LAG * (depth_n - 1)
     first_up = LAG * (depth_n - 1)
@@ -315,7 +347,7 @@
         if step >= first_up:
             held_now["top"] = kept.get("top")
         out = section(depth_n, step, sc, dict(src=src, w=w, mask=mask), queue.pop(0), held_now, sends)
-        queue.append({to: lax.ppermute(out.pop(name), "depth", pairs) for name, (to, pairs) in sends.items()})
+        queue.append({to: lax.ppermute(out.pop(name), ("depth", "batch"), pairs) for name, (to, pairs) in sends.items()})
         kept.update(out)
 
     def leave(result):

time: 106 us -> 82.8 us (0.78)
  starting transfers between devices: 52.9 us -> 31.9 us
  Pallas kernels: 41.4 us -> 27.9 us
  waiting for transfers between devices: 4.22 us -> 16.8 us
    ppermute x32, starting transfers between devices: 49.9 us -> 28.9 us  [per_device(): lax.ppermute(out.pop(name), ('depth', 'batch'), pairs)]
    ppermute x32, waiting for transfers between devices: 4.21 us -> 16.8 us  [per_device(): lax.ppermute(out.pop(name), ('depth', 'batch'), pairs)]
    pallas_call x20, Pallas kernels: 33.3 us -> 21.9 us  [section(): pl.pallas_call(functools.partial(section_kernel, depth_n, chunks, step, p...]
    pallas_call x2, Pallas kernels: 5.29 us -> 4.21 us  [leave(): pl.pallas_call(leave_kernel, out_shape=jax.ShapeDtypeStruct(cells.shape,...]
  transfers between devices with their start and end apart: 33 -> 33, of which waited for: 2 -> 14; matrix products, arithmetic and copies ran while one was open for 0% -> 0% of each run, Pallas kernels for 33% -> 28%
where the time goes in v3:
time: 82.8 us; the launch traced here: 82.1 us
  starting transfers between devices  31.9 us (39%)
  Pallas kernels  27.9 us (34%)
  waiting for transfers between devices  16.8 us (20%)
  local copies, waits for them, and re-layouts  2.91 us (4%)
  between operations  1.72 us (2%)
  other arithmetic  0.89 us (1%)
    ppermute x32, starting transfers between devices, per_device(): lax.ppermute(out.pop(name), ('depth', 'batch'), pairs)  28.9 us
    pallas_call x20, Pallas kernels, section(): pl.pallas_call(functools.partial(section_kernel, depth_n, chunks, step, p...  21.9 us
    ppermute x32, waiting for transfers between devices, per_device(): lax.ppermute(out.pop(name), ('depth', 'batch'), pairs)  16.8 us
    pallas_call x2, Pallas kernels, leave(): pl.pallas_call(leave_kernel, out_shape=jax.ShapeDtypeStruct(cells.shape,...  4.21 us
    ppermute x1, starting transfers between devices, per_device(): arrived = lax.ppermute(sent, 'plane', [(0, 1), (1, 0)])  3 us
    unnamed x4, local copies, waits for them, and re-layouts  1.67 us
  transfers between devices with their start and end apart: 33, of which 14 were waited for; matrix products, arithmetic and copies ran while one was open for 0% of the time, Pallas kernels for 28%

profile of v3, /device:TPU:0, one launch (start us, length us, event | category | flops | bytes accessed | tf_op | source)
XLA Modules:
  0.0 82.1 jit_solution(5370400880622877995)
XLA Ops:
  2.6 3.0 %collective-permute-start = (bf16[2,8,4224]{2,1,0:T(8,128)(2,1)S(1)}, bf16[2,8,4224]{2,1,0:T(8,128)(2,1)S(1)}, u32[]{:S(2)}, u32[]{:S(2)}) collective-permute-start(bf16[2,8,4224]{2,1,0:T(8,128)(2,1)S(1)} %maximum_select_fusion), channel_id=1, source_target_pairs={{0,2},{2,0},{1,3},{3,1},{4,6},{6,4},{5,7},{7,5},{8,10},{10,8},{9,1... | collective-permute-start | bytes 405512 | tf_op jit(solution)/shard_map/ppermute | solution.py:290
  6.5 1.7 %copy-done = bf16[3,3,2,256,256]{4,3,2,1,0:T(8,128)(2,1)S(1)} copy-done((bf16[3,3,2,256,256]{4,3,2,1,0:T(8,128)(2,1)S(1)}, bf16[3,3,2,256,256]{4,3,2,1,0:T(8,128)(2,1)}, u32[]{:S(2)}) %copy-start) | copy-done | bytes 2359320
  8.2 1.5 %shard_map.60 = (bf16[8,288,256]{2,1,0:T(8,128)(2,1)S(1)}, f32[3,2,144,128]{3,2,1,0:T(8,128)S(1)}, bf16[3,3,512,256]{3,2,1,0:T(8,128)(2,1)S(1)}) custom-call(bf16[2,8,32768]{2,1,0:T(8,128)(2,1)S(1)} %bitcast.16, bf16[3,3,512,256]{3,2,1,0:T(8,128)(2,1)S(1)} %bitcast.14, bf16[128,128]{1,0:T(8,128)(2,1)S(1)} %pad.9.own_mask, s32[3]{0:T(128)S(4)} %shard_map.59.sc.refs_0_), custom_call_target="tpu_custom_call" | custom-call | bytes 8388608 | tf_op jit(solution)/shard_map/pallas_call | solution.py:291
  13.4 4.7 %collective-permute-done.2.refs_4_ = bf16[288,256]{1,0:T(8,128)(2,1)S(1)} collective-permute-done((bf16[288,256]{1,0:T(8,128)(2,1)S(1)}, bf16[288,256]{1,0:T(8,128)(2,1)S(1)}, u32[]{:S(2)}, u32[]{:S(2)}) %collective-permute-start.2) | collective-permute-done | bytes 147488 | tf_op jit(solution)/shard_map/ppermute | solution.py:350
  22.6 2.6 %collective-permute-done.5.refs_4_ = bf16[288,256]{1,0:T(8,128)(2,1)S(1)} collective-permute-done((bf16[288,256]{1,0:T(8,128)(2,1)S(1)}, bf16[288,256]{1,0:T(8,128)(2,1)S(1)}, u32[]{:S(2)}, u32[]{:S(2)}) %collective-permute-start.5) | collective-permute-done | bytes 147488 | tf_op jit(solution)/shard_map/ppermute | solution.py:350
  26.6 2.0 %collective-permute-start.9 = (bf16[288,256]{1,0:T(8,128)(2,1)S(1)}, bf16[288,256]{1,0:T(8,128)(2,1)S(1)}, u32[]{:S(2)}, u32[]{:S(2)}) collective-permute-start(bf16[288,256]{1,0:T(8,128)(2,1)S(1)} %get-tuple-element.102), channel_id=1, source_target_pairs={{0,4},{1,5},{8,12},{9,13},{4,0},{5,1},{12,8},{13,9},{2,6},{3,7},{1... | collective-permute-start | bytes 442376 | tf_op jit(solution)/shard_map/ppermute | solution.py:350
  28.6 1.4 %shard_map.67 = (bf16[8,4,288,256]{3,2,1,0:T(8,128)(2,1)S(1)}, bf16[8,288,256]{2,1,0:T(8,128)(2,1)S(1)}, bf16[288,256]{1,0:T(8,128)(2,1)S(1)}, bf16[288,256]{1,0:T(8,128)(2,1)S(1)}) custom-call(s32[3]{0:T(128)S(4)} %shard_map.59.sc.refs_0_, bf16[8,288,256]{2,1,0:T(8,128)(2,1)S(1)} %get-tuple-element.81.refs_1_, ...), custom_call_target="tpu_custom_call", output_to_operand_aliasing={{0}: (6, {}), {1}: (7, {})} | custom-call | flops 1358954496 | bytes 589824 | tf_op jit(solution)/shard_map/pallas_call | solution.py:130
  30.0 1.8 %collective-permute-start.7 = (bf16[288,256]{1,0:T(8,128)(2,1)S(1)}, bf16[288,256]{1,0:T(8,128)(2,1)S(1)}, u32[]{:S(2)}, u32[]{:S(2)}) collective-permute-start(bf16[288,256]{1,0:T(8,128)(2,1)S(1)} %get-tuple-element.100), channel_id=1, source_target_pairs={{0,4},{1,5},{8,12},{9,13},{4,0},{5,1},{12,8},{13,9},{2,6},{3,7},{1... | collective-permute-start | bytes 442376 | tf_op jit(solution)/shard_map/ppermute | solution.py:350
  33.2 1.9 %collective-permute-start.13 = (bf16[288,256]{1,0:T(8,128)(2,1)S(1)}, bf16[288,256]{1,0:T(8,128)(2,1)S(1)}, u32[]{:S(2)}, u32[]{:S(2)}) collective-permute-start(bf16[288,256]{1,0:T(8,128)(2,1)S(1)} %get-tuple-element.111), channel_id=1, source_target_pairs={{0,4},{1,5},{8,12},{9,13},{4,0},{5,1},{12,8},{13,9},{2,6},{3,7},{1... | collective-permute-start | bytes 442376 | tf_op jit(solution)/shard_map/ppermute | solution.py:350
  37.7 1.4 %collective-permute-start.11 = (bf16[288,256]{1,0:T(8,128)(2,1)S(1)}, bf16[288,256]{1,0:T(8,128)(2,1)S(1)}, u32[]{:S(2)}, u32[]{:S(2)}) collective-permute-start(bf16[288,256]{1,0:T(8,128)(2,1)S(1)} %get-tuple-element.109), channel_id=1, source_target_pairs={{0,4},{1,5},{8,12},{9,13},{4,0},{5,1},{12,8},{13,9},{2,6},{3,7},{1... | collective-permute-start | bytes 442376 | tf_op jit(solution)/shard_map/ppermute | solution.py:350
  39.5 2.8 %collective-permute-start.17 = (bf16[288,256]{1,0:T(8,128)(2,1)S(1)}, bf16[288,256]{1,0:T(8,128)(2,1)S(1)}, u32[]{:S(2)}, u32[]{:S(2)}) collective-permute-start(bf16[288,256]{1,0:T(8,128)(2,1)S(1)} %get-tuple-element.121), channel_id=1, source_target_pairs={{0,4},{1,5},{8,12},{9,13},{4,0},{5,1},{12,8},{13,9},{2,6},{3,7},{1... | collective-permute-start | bytes 442376 | tf_op jit(solution)/shard_map/ppermute | solution.py:350
  42.3 1.6 %collective-permute-done.11.refs_4_ = bf16[288,256]{1,0:T(8,128)(2,1)S(1)} collective-permute-done((bf16[288,256]{1,0:T(8,128)(2,1)S(1)}, bf16[288,256]{1,0:T(8,128)(2,1)S(1)}, u32[]{:S(2)}, u32[]{:S(2)}) %collective-permute-start.11) | collective-permute-done | bytes 147488 | tf_op jit(solution)/shard_map/ppermute | solution.py:350
  43.9 2.7 %collective-permute-start.15 = (bf16[288,256]{1,0:T(8,128)(2,1)S(1)}, bf16[288,256]{1,0:T(8,128)(2,1)S(1)}, u32[]{:S(2)}, u32[]{:S(2)}) collective-permute-start(bf16[288,256]{1,0:T(8,128)(2,1)S(1)} %get-tuple-element.119), channel_id=1, source_target_pairs={{0,4},{1,5},{8,12},{9,13},{4,0},{5,1},{12,8},{13,9},{2,6},{3,7},{1... | collective-permute-start | bytes 442376 | tf_op jit(solution)/shard_map/ppermute | solution.py:350
  47.1 2.1 %collective-permute-start.21 = (bf16[288,256]{1,0:T(8,128)(2,1)S(1)}, bf16[288,256]{1,0:T(8,128)(2,1)S(1)}, u32[]{:S(2)}, u32[]{:S(2)}) collective-permute-start(bf16[288,256]{1,0:T(8,128)(2,1)S(1)} %get-tuple-element.131), channel_id=1, source_target_pairs={{0,4},{1,5},{8,12},{9,13},{4,0},{5,1},{12,8},{13,9},{2,6},{3,7},{1... | collective-permute-start | bytes 442376 | tf_op jit(solution)/shard_map/ppermute | solution.py:350
  50.3 3.5 %collective-permute-start.19 = (bf16[288,256]{1,0:T(8,128)(2,1)S(1)}, bf16[288,256]{1,0:T(8,128)(2,1)S(1)}, u32[]{:S(2)}, u32[]{:S(2)}) collective-permute-start(bf16[288,256]{1,0:T(8,128)(2,1)S(1)} %get-tuple-element.129), channel_id=1, source_target_pairs={{0,4},{1,5},{8,12},{9,13},{4,0},{5,1},{12,8},{13,9},{2,6},{3,7},{1... | collective-permute-start | bytes 442376 | tf_op jit(solution)/shard_map/ppermute | solution.py:350
  53.8 1.4 %shard_map.74 = (bf16[8,4,288,256]{3,2,1,0:T(8,128)(2,1)S(1)}, bf16[8,288,256]{2,1,0:T(8,128)(2,1)S(1)}, bf16[8,288,256]{2,1,0:T(8,128)(2,1)S(1)}, bf16[288,256]{1,0:T(8,128)(2,1)S(1)}, bf16[288,256]{1,0:T(8,128)(2,1)S(1)}) custom-call(s32[3]{0:T(128)S(4)} %shard_map.59.sc.refs_0_, ...), custom_call_target="tpu_custom_call", output_to_operand_aliasing={{0}: (6, {}), {1}: (7, {}), {2}: (8, {})} | custom-call | flops 1358954496 | bytes 589824 | tf_op jit(solution)/shard_map/pallas_call | solution.py:130
  55.2 1.7 %collective-permute-start.25 = (bf16[288,256]{1,0:T(8,128)(2,1)S(1)}, bf16[288,256]{1,0:T(8,128)(2,1)S(1)}, u32[]{:S(2)}, u32[]{:S(2)}) collective-permute-start(bf16[288,256]{1,0:T(8,128)(2,1)S(1)} %get-tuple-element.142), channel_id=1, source_target_pairs={{0,4},{1,5},{8,12},{9,13},{4,0},{5,1},{12,8},{13,9},{2,6},{3,7},{1... | collective-permute-start | bytes 442376 | tf_op jit(solution)/shard_map/ppermute | solution.py:350
  57.0 1.6 %shard_map.75 = (bf16[8,4,288,256]{3,2,1,0:T(8,128)(2,1)S(1)}, bf16[8,288,256]{2,1,0:T(8,128)(2,1)S(1)}, bf16[8,288,256]{2,1,0:T(8,128)(2,1)S(1)}, bf16[288,256]{1,0:T(8,128)(2,1)S(1)}, bf16[288,256]{1,0:T(8,128)(2,1)S(1)}) custom-call(s32[3]{0:T(128)S(4)} %shard_map.59.sc.refs_0_, ...), custom_call_target="tpu_custom_call", output_to_operand_aliasing={{0}: (6, {}), {1}: (7, {}), {2}: (8, {})} | custom-call | flops 1358954496 | bytes 589824 | tf_op jit(solution)/shard_map/pallas_call | solution.py:130
  58.5 1.7 %collective-permute-start.23 = (bf16[288,256]{1,0:T(8,128)(2,1)S(1)}, bf16[288,256]{1,0:T(8,128)(2,1)S(1)}, u32[]{:S(2)}, u32[]{:S(2)}) collective-permute-start(bf16[288,256]{1,0:T(8,128)(2,1)S(1)} %get-tuple-element.139), channel_id=1, source_target_pairs={{0,4},{1,5},{8,12},{9,13},{4,0},{5,1},{12,8},{13,9},{2,6},{3,7},{1... | collective-permute-start | bytes 442376 | tf_op jit(solution)/shard_map/ppermute | solution.py:350
  64.7 1.4 %shard_map.77 = (bf16[8,288,256]{2,1,0:T(8,128)(2,1)S(1)}, bf16[288,256]{1,0:T(8,128)(2,1)S(1)}, bf16[288,256]{1,0:T(8,128)(2,1)S(1)}) custom-call(s32[3]{0:T(128)S(4)} %shard_map.59.sc.refs_0_, bf16[8,288,256]{2,1,0:T(8,128)(2,1)S(1)} %get-tuple-element.81.refs_1_, ...), custom_call_target="tpu_custom_call", output_to_operand_aliasing={{0}: (7, {})} | custom-call | flops 1358954496 | bytes 589824 | tf_op jit(solution)/shard_map/pallas_call | solution.py:130
  69.7 1.4 %collective-permute-start.32 = (bf16[288,256]{1,0:T(8,128)(2,1)S(1)}, bf16[288,256]{1,0:T(8,128)(2,1)S(1)}, u32[]{:S(2)}, u32[]{:S(2)}) collective-permute-start(bf16[288,256]{1,0:T(8,128)(2,1)S(1)} %get-tuple-element.153), channel_id=1, source_target_pairs={{0,4},{1,5},{8,12},{9,13},{4,0},{5,1},{12,8},{13,9},{2,6},{3,7},{1... | collective-permute-start | bytes 442376 | tf_op jit(solution)/shard_map/ppermute | solution.py:350
  73.3 1.4 %collective-permute-start.31 = (bf16[288,256]{1,0:T(8,128)(2,1)S(1)}, bf16[288,256]{1,0:T(8,128)(2,1)S(1)}, u32[]{:S(2)}, u32[]{:S(2)}) collective-permute-start(bf16[288,256]{1,0:T(8,128)(2,1)S(1)} %get-tuple-element.152), channel_id=1, source_target_pairs={{0,4},{1,5},{8,12},{9,13},{4,0},{5,1},{12,8},{13,9},{2,6},{3,7},{1... | collective-permute-start | bytes 442376 | tf_op jit(solution)/shard_map/ppermute | solution.py:350
  74.7 2.1 %shard_map.83 = bf16[2,8,32768]{2,1,0:T(8,128)(2,1)} custom-call(bf16[8,288,256]{2,1,0:T(8,128)(2,1)S(1)} %get-tuple-element.155.result, s32[3]{0:T(128)S(4)} %shard_map.59.sc.refs_0_), custom_call_target="tpu_custom_call" | custom-call | bytes 8388608 | tf_op jit(solution)/shard_map/pallas_call | solution.py:354
  79.9 2.1 %shard_map.82 = bf16[2,8,32768]{2,1,0:T(8,128)(2,1)} custom-call(bf16[8,288,256]{2,1,0:T(8,128)(2,1)S(1)} %shard_map.81.result, s32[3]{0:T(128)S(4)} %shard_map.59.sc.refs_0_), custom_call_target="tpu_custom_call" | custom-call | bytes 8388608 | tf_op jit(solution)/shard_map/pallas_call | solution.py:354
  (81 shorter events, 31.0 us)
Async XLA Ops:
  2.6 7.1 %collective-permute-start = (bf16[2,8,4224]{2,1,0:T(8,128)(2,1)S(1)}, bf16[2,8,4224]{2,1,0:T(8,128)(2,1)S(1)}, u32[]{:S(2)}, u32[]{:S(2)}) collective-permute-start(bf16[2,8,4224]{2,1,0:T(8,128)(2,1)S(1)} %maximum_select_fusion), channel_id=1, source_target_pairs={{0,2},{2,0},{1,3},{3,1},{4,6},{6,4},{5,7},{7,5},{8,10},{10,8},{9,1... | collective-permute-start | bytes 405512 | tf_op jit(solution)/shard_map/ppermute | solution.py:290
  11.3 6.8 %collective-permute-start.2 = (bf16[288,256]{1,0:T(8,128)(2,1)S(1)}, bf16[288,256]{1,0:T(8,128)(2,1)S(1)}, u32[]{:S(2)}, u32[]{:S(2)}) collective-permute-start(bf16[288,256]{1,0:T(8,128)(2,1)S(1)} %get-tuple-element.87), channel_id=1, source_target_pairs={{0,4},{1,5},{8,12},{9,13},{4,0},{5,1},{12,8},{13,9},{2,6},{3,7},{1... | collective-permute-start | bytes 442376 | tf_op jit(solution)/shard_map/ppermute | solution.py:350
  13.0 7.3 %collective-permute-start.1 = (bf16[288,256]{1,0:T(8,128)(2,1)S(1)}, bf16[288,256]{1,0:T(8,128)(2,1)S(1)}, u32[]{:S(2)}, u32[]{:S(2)}) collective-permute-start(bf16[288,256]{1,0:T(8,128)(2,1)S(1)} %get-tuple-element.86), channel_id=1, source_target_pairs={{0,4},{1,5},{8,12},{9,13},{4,0},{5,1},{12,8},{13,9},{2,6},{3,7},{1... | collective-permute-start | bytes 442376 | tf_op jit(solution)/shard_map/ppermute | solution.py:350
  19.5 5.8 %collective-permute-start.5 = (bf16[288,256]{1,0:T(8,128)(2,1)S(1)}, bf16[288,256]{1,0:T(8,128)(2,1)S(1)}, u32[]{:S(2)}, u32[]{:S(2)}) collective-permute-start(bf16[288,256]{1,0:T(8,128)(2,1)S(1)} %get-tuple-element.94), channel_id=1, source_target_pairs={{0,4},{1,5},{8,12},{9,13},{4,0},{5,1},{12,8},{13,9},{2,6},{3,7},{1... | collective-permute-start | bytes 442376 | tf_op jit(solution)/shard_map/ppermute | solution.py:350
  19.6 5.7 %collective-permute-start.6 = (bf16[288,256]{1,0:T(8,128)(2,1)S(1)}, bf16[288,256]{1,0:T(8,128)(2,1)S(1)}, u32[]{:S(2)}, u32[]{:S(2)}) collective-permute-start(bf16[288,256]{1,0:T(8,128)(2,1)S(1)} %get-tuple-element.95), channel_id=1, source_target_pairs={{4,8},{5,9},{0,1},{12,13},{8,4},{9,5},{1,0},{13,12},{6,10},{7,11},... | collective-permute-start | bytes 442376 | tf_op jit(solution)/shard_map/ppermute | solution.py:350
  21.6 7.0 %collective-permute-start.3 = (bf16[288,256]{1,0:T(8,128)(2,1)S(1)}, bf16[288,256]{1,0:T(8,128)(2,1)S(1)}, u32[]{:S(2)}, u32[]{:S(2)}) collective-permute-start(bf16[288,256]{1,0:T(8,128)(2,1)S(1)} %get-tuple-element.92), channel_id=1, source_target_pairs={{0,4},{1,5},{8,12},{9,13},{4,0},{5,1},{12,8},{13,9},{2,6},{3,7},{1... | collective-permute-start | bytes 442376 | tf_op jit(solution)/shard_map/ppermute | solution.py:350
  22.6 6.0 %collective-permute-start.4 = (bf16[288,256]{1,0:T(8,128)(2,1)S(1)}, bf16[288,256]{1,0:T(8,128)(2,1)S(1)}, u32[]{:S(2)}, u32[]{:S(2)}) collective-permute-start(bf16[288,256]{1,0:T(8,128)(2,1)S(1)} %get-tuple-element.93), channel_id=1, source_target_pairs={{4,8},{5,9},{0,1},{12,13},{8,4},{9,5},{1,0},{13,12},{6,10},{7,11},... | collective-permute-start | bytes 442376 | tf_op jit(solution)/shard_map/ppermute | solution.py:350
  26.6 5.2 %collective-permute-start.9 = (bf16[288,256]{1,0:T(8,128)(2,1)S(1)}, bf16[288,256]{1,0:T(8,128)(2,1)S(1)}, u32[]{:S(2)}, u32[]{:S(2)}) collective-permute-start(bf16[288,256]{1,0:T(8,128)(2,1)S(1)} %get-tuple-element.102), channel_id=1, source_target_pairs={{0,4},{1,5},{8,12},{9,13},{4,0},{5,1},{12,8},{13,9},{2,6},{3,7},{1... | collective-permute-start | bytes 442376 | tf_op jit(solution)/shard_map/ppermute | solution.py:350
  30.0 6.3 %collective-permute-start.7 = (bf16[288,256]{1,0:T(8,128)(2,1)S(1)}, bf16[288,256]{1,0:T(8,128)(2,1)S(1)}, u32[]{:S(2)}, u32[]{:S(2)}) collective-permute-start(bf16[288,256]{1,0:T(8,128)(2,1)S(1)} %get-tuple-element.100), channel_id=1, source_target_pairs={{0,4},{1,5},{8,12},{9,13},{4,0},{5,1},{12,8},{13,9},{2,6},{3,7},{1... | collective-permute-start | bytes 442376 | tf_op jit(solution)/shard_map/ppermute | solution.py:350
  33.2 6.3 %collective-permute-start.13 = (bf16[288,256]{1,0:T(8,128)(2,1)S(1)}, bf16[288,256]{1,0:T(8,128)(2,1)S(1)}, u32[]{:S(2)}, u32[]{:S(2)}) collective-permute-start(bf16[288,256]{1,0:T(8,128)(2,1)S(1)} %get-tuple-element.111), channel_id=1, source_target_pairs={{0,4},{1,5},{8,12},{9,13},{4,0},{5,1},{12,8},{13,9},{2,6},{3,7},{1... | collective-permute-start | bytes 442376 | tf_op jit(solution)/shard_map/ppermute | solution.py:350
  37.7 6.2 %collective-permute-start.11 = (bf16[288,256]{1,0:T(8,128)(2,1)S(1)}, bf16[288,256]{1,0:T(8,128)(2,1)S(1)}, u32[]{:S(2)}, u32[]{:S(2)}) collective-permute-start(bf16[288,256]{1,0:T(8,128)(2,1)S(1)} %get-tuple-element.109), channel_id=1, source_target_pairs={{0,4},{1,5},{8,12},{9,13},{4,0},{5,1},{12,8},{13,9},{2,6},{3,7},{1... | collective-permute-start | bytes 442376 | tf_op jit(solution)/shard_map/ppermute | solution.py:350
  39.1 4.8 %collective-permute-start.12 = (bf16[288,256]{1,0:T(8,128)(2,1)S(1)}, bf16[288,256]{1,0:T(8,128)(2,1)S(1)}, u32[]{:S(2)}, u32[]{:S(2)}) collective-permute-start(bf16[288,256]{1,0:T(8,128)(2,1)S(1)} %get-tuple-element.110), channel_id=1, source_target_pairs={{4,8},{5,9},{0,1},{12,13},{8,4},{9,5},{1,0},{13,12},{6,10},{7,11},... | collective-permute-start | bytes 442376 | tf_op jit(solution)/shard_map/ppermute | solution.py:350
  39.5 7.6 %collective-permute-start.17 = (bf16[288,256]{1,0:T(8,128)(2,1)S(1)}, bf16[288,256]{1,0:T(8,128)(2,1)S(1)}, u32[]{:S(2)}, u32[]{:S(2)}) collective-permute-start(bf16[288,256]{1,0:T(8,128)(2,1)S(1)} %get-tuple-element.121), channel_id=1, source_target_pairs={{0,4},{1,5},{8,12},{9,13},{4,0},{5,1},{12,8},{13,9},{2,6},{3,7},{1... | collective-permute-start | bytes 442376 | tf_op jit(solution)/shard_map/ppermute | solution.py:350
  42.3 4.8 %collective-permute-start.18 = (bf16[288,256]{1,0:T(8,128)(2,1)S(1)}, bf16[288,256]{1,0:T(8,128)(2,1)S(1)}, u32[]{:S(2)}, u32[]{:S(2)}) collective-permute-start(bf16[288,256]{1,0:T(8,128)(2,1)S(1)} %get-tuple-element.122), channel_id=1, source_target_pairs={{4,8},{5,9},{0,1},{12,13},{8,4},{9,5},{1,0},{13,12},{6,10},{7,11},... | collective-permute-start | bytes 442376 | tf_op jit(solution)/shard_map/ppermute | solution.py:350
  43.9 6.4 %collective-permute-start.15 = (bf16[288,256]{1,0:T(8,128)(2,1)S(1)}, bf16[288,256]{1,0:T(8,128)(2,1)S(1)}, u32[]{:S(2)}, u32[]{:S(2)}) collective-permute-start(bf16[288,256]{1,0:T(8,128)(2,1)S(1)} %get-tuple-element.119), channel_id=1, source_target_pairs={{0,4},{1,5},{8,12},{9,13},{4,0},{5,1},{12,8},{13,9},{2,6},{3,7},{1... | collective-permute-start | bytes 442376 | tf_op jit(solution)/shard_map/ppermute | solution.py:350
  47.1 6.8 %collective-permute-start.21 = (bf16[288,256]{1,0:T(8,128)(2,1)S(1)}, bf16[288,256]{1,0:T(8,128)(2,1)S(1)}, u32[]{:S(2)}, u32[]{:S(2)}) collective-permute-start(bf16[288,256]{1,0:T(8,128)(2,1)S(1)} %get-tuple-element.131), channel_id=1, source_target_pairs={{0,4},{1,5},{8,12},{9,13},{4,0},{5,1},{12,8},{13,9},{2,6},{3,7},{1... | collective-permute-start | bytes 442376 | tf_op jit(solution)/shard_map/ppermute | solution.py:350
  49.2 4.6 %collective-permute-start.22 = (bf16[288,256]{1,0:T(8,128)(2,1)S(1)}, bf16[288,256]{1,0:T(8,128)(2,1)S(1)}, u32[]{:S(2)}, u32[]{:S(2)}) collective-permute-start(bf16[288,256]{1,0:T(8,128)(2,1)S(1)} %get-tuple-element.132), channel_id=1, source_target_pairs={{4,8},{5,9},{0,1},{12,13},{8,4},{9,5},{1,0},{13,12},{6,10},{7,11},... | collective-permute-start | bytes 442376 | tf_op jit(solution)/shard_map/ppermute | solution.py:350
  50.3 6.6 %collective-permute-start.19 = (bf16[288,256]{1,0:T(8,128)(2,1)S(1)}, bf16[288,256]{1,0:T(8,128)(2,1)S(1)}, u32[]{:S(2)}, u32[]{:S(2)}) collective-permute-start(bf16[288,256]{1,0:T(8,128)(2,1)S(1)} %get-tuple-element.129), channel_id=1, source_target_pairs={{0,4},{1,5},{8,12},{9,13},{4,0},{5,1},{12,8},{13,9},{2,6},{3,7},{1... | collective-permute-start | bytes 442376 | tf_op jit(solution)/shard_map/ppermute | solution.py:350
  55.2 6.3 %collective-permute-start.25 = (bf16[288,256]{1,0:T(8,128)(2,1)S(1)}, bf16[288,256]{1,0:T(8,128)(2,1)S(1)}, u32[]{:S(2)}, u32[]{:S(2)}) collective-permute-start(bf16[288,256]{1,0:T(8,128)(2,1)S(1)} %get-tuple-element.142), channel_id=1, source_target_pairs={{0,4},{1,5},{8,12},{9,13},{4,0},{5,1},{12,8},{13,9},{2,6},{3,7},{1... | collective-permute-start | bytes 442376 | tf_op jit(solution)/shard_map/ppermute | solution.py:350
  58.5 6.1 %collective-permute-start.23 = (bf16[288,256]{1,0:T(8,128)(2,1)S(1)}, bf16[288,256]{1,0:T(8,128)(2,1)S(1)}, u32[]{:S(2)}, u32[]{:S(2)}) collective-permute-start(bf16[288,256]{1,0:T(8,128)(2,1)S(1)} %get-tuple-element.139), channel_id=1, source_target_pairs={{0,4},{1,5},{8,12},{9,13},{4,0},{5,1},{12,8},{13,9},{2,6},{3,7},{1... | collective-permute-start | bytes 442376 | tf_op jit(solution)/shard_map/ppermute | solution.py:350
  62.9 5.5 %collective-permute-start.29 = (bf16[288,256]{1,0:T(8,128)(2,1)S(1)}, bf16[288,256]{1,0:T(8,128)(2,1)S(1)}, u32[]{:S(2)}, u32[]{:S(2)}) collective-permute-start(bf16[288,256]{1,0:T(8,128)(2,1)S(1)} %get-tuple-element.148), channel_id=1, source_target_pairs={{0,4},{1,5},{8,12},{9,13},{4,0},{5,1},{12,8},{13,9},{2,6},{3,7},{1... | collective-permute-start | bytes 442376 | tf_op jit(solution)/shard_map/ppermute | solution.py:350
  66.0 5.9 %collective-permute-start.27 = (bf16[288,256]{1,0:T(8,128)(2,1)S(1)}, bf16[288,256]{1,0:T(8,128)(2,1)S(1)}, u32[]{:S(2)}, u32[]{:S(2)}) collective-permute-start(bf16[288,256]{1,0:T(8,128)(2,1)S(1)} %get-tuple-element.146), channel_id=1, source_target_pairs={{0,4},{1,5},{8,12},{9,13},{4,0},{5,1},{12,8},{13,9},{2,6},{3,7},{1... | collective-permute-start | bytes 442376 | tf_op jit(solution)/shard_map/ppermute | solution.py:350
  69.7 7.0 %collective-permute-start.32 = (bf16[288,256]{1,0:T(8,128)(2,1)S(1)}, bf16[288,256]{1,0:T(8,128)(2,1)S(1)}, u32[]{:S(2)}, u32[]{:S(2)}) collective-permute-start(bf16[288,256]{1,0:T(8,128)(2,1)S(1)} %get-tuple-element.153), channel_id=1, source_target_pairs={{0,4},{1,5},{8,12},{9,13},{4,0},{5,1},{12,8},{13,9},{2,6},{3,7},{1... | collective-permute-start | bytes 442376 | tf_op jit(solution)/shard_map/ppermute | solution.py:350
  73.3 5.2 %collective-permute-start.31 = (bf16[288,256]{1,0:T(8,128)(2,1)S(1)}, bf16[288,256]{1,0:T(8,128)(2,1)S(1)}, u32[]{:S(2)}, u32[]{:S(2)}) collective-permute-start(bf16[288,256]{1,0:T(8,128)(2,1)S(1)} %get-tuple-element.152), channel_id=1, source_target_pairs={{0,4},{1,5},{8,12},{9,13},{4,0},{5,1},{12,8},{13,9},{2,6},{3,7},{1... | collective-permute-start | bytes 442376 | tf_op jit(solution)/shard_map/ppermute | solution.py:350
  (11 other events, 44.3 us)

commit v4 on v3

--- a/solution.py
+++ b/solution.py
@@ -7,7 +7,7 @@
 from jax.experimental.pallas import tpu as pltpu
 from jax.sharding import PartitionSpec as P
 
-NT = (((1,), (1,)), ((), ()))
+NN = (((1,), (0,)), ((), ()))
 CHUNKS = 8
 LAG = 2
 VMEM_LIMIT = 16 * 1024 * 1024
@@ -19,9 +19,9 @@
     wide = x.astype(jnp.float32)
     before = pltpu.roll(wide, 1, 0) * jnp.tile(mask[slot, 0], (rows // window, 2))
     after = pltpu.roll(wide, rows - 1, 0) * jnp.tile(mask[slot, 1], (rows // window, 2))
-    total = lax.dot_general(before.astype(jnp.bfloat16), w[slot, 0], NT, preferred_element_type=jnp.float32)
-    total = total + lax.dot_general(x, w[slot, 1], NT, preferred_element_type=jnp.float32)
-    total = total + lax.dot_general(after.astype(jnp.bfloat16), w[slot, 2], NT, preferred_element_type=jnp.float32)
+    total = lax.dot_general(before.astype(jnp.bfloat16), w[slot, 0], NN, preferred_element_type=jnp.float32)
+    total = total + lax.dot_general(x, w[slot, 1], NN, preferred_element_type=jnp.float32)
+    total = total + lax.dot_general(after.astype(jnp.bfloat16), w[slot, 2], NN, preferred_element_type=jnp.float32)
     block = total.shape[1] // 2
     real = total[:half, :block] - total[half:, block:]
     imag = total[half:, :block] + total[:half, block:]
@@ -145,29 +145,57 @@
 LANES = 128
 
 
-def enter_kernel(source, pool, own_mask, sc, src, mask, w, natural, wide, sems):
+def offer_kernel(source, near, facts, payload, sc, lines, sem):
+    for i in range(sc.shape[0]):
+        sc[i] = facts[i, 0]
+    sources, width = payload.shape[1], payload.shape[2] - LANES
+    first = jnp.where(facts[2, 0] == 0, source.shape[2] - width, 0)
+    copy = pltpu.make_async_copy(
+        source.at[:, :, pl.ds(pl.multiple_of(first, LANES), width)], payload.at[:, :, pl.ds(0, width)], sem
+    )
+    copy.start()
+    lines[...] = jnp.zeros_like(lines)
+    for slot in range(near.shape[0]):
+        for side in range(2):
+            at = slot * 2 + side
+            lines[at : at + 1, :] = near[slot, 2 * side : 2 * side + 1, :].astype(jnp.float32)
+    for part in range(2):
+        payload[part, :, width:] = lines[part * sources : (part + 1) * sources].astype(payload.dtype)
+    copy.wait()
+
+
+def column(line):
+    return jnp.broadcast_to(line, (LANES, LANES)).T
+
+
+def enter_kernel(source, pool, near, sc, src, mask, w, natural, wide, raw, sems):
     own = pl.multiple_of(sc[2], 16)
-    bring = pltpu.make_async_copy(pool, w, sems.at[0])
+    bring = pltpu.make_async_copy(pool, raw, sems.at[0])
     load = pltpu.make_async_copy(source, natural, sems.at[1])
     load.start()
     bring.start()
-    sources, window = src.shape[0], wide.shape[2] // src.shape[0]
-    tile = own_mask.shape[0]
-    cap = mask.shape[0]
-    columns = own_mask[...].astype(jnp.float32)
-    for slot in range(cap):
+    sources = src.shape[0]
+    window = mask.shape[2]
+    tile = near.shape[2]
+    for slot in range(mask.shape[0]):
         for side in range(2):
-            at = slot * 3 + 2 * side
-            mask[slot, side, pl.ds(own, tile), :] = jnp.broadcast_to(columns[:, at : at + 1], (tile, LANES))
+            mask[slot, side, pl.ds(own, tile), :] = column(near[slot, 2 * side : 2 * side + 1, :].astype(jnp.float32))
     load.wait()
     spread(natural, wide, own, tile, sources, window)
     for part in range(2):
         for s in range(sources):
             for h in range(2):
                 src[s, pl.ds(part * window + own, tile), h * LANES : (h + 1) * LANES] = wide[
-                    part, h, pl.ds(s * window + own, tile), :
+                    part, h, pl.ds(s * (window + 1) + own, tile), :
                 ].astype(src.dtype)
     bring.wait()
+
+    def turn(i, _):
+        slot, offset = i // 3, lax.rem(i, 3)
+        w[slot, offset] = raw[slot, offset].T
+        return 0
+
+    lax.fori_loop(0, raw.shape[0] * 3, turn, 0)
 
 
 def spread(natural, wide, first, count, sources, window):
@@ -175,45 +203,49 @@
         for part in range(2):
             for h in range(2):
                 lanes = pl.ds(pl.multiple_of((2 * n + h) * LANES, LANES), LANES)
-                wide[part, h, pl.ds(first + n, sources, stride=window), :] = natural[part, :, lanes].astype(jnp.float32)
+                wide[part, h, pl.ds(first + n, sources, stride=window + 1), :] = natural[part, :, lanes].astype(
+                    jnp.float32
+                )
         return 0
 
-    lax.fori_loop(0, count, block, 0, unroll=4)
+    lax.fori_loop(0, count, block, 0, unroll=8)
 
 
 def join_kernel(arrived, sc, src_in, mask_in, src, mask, wide):
     own = sc[2]
-    sources, window = src.shape[0], wide.shape[2] // src.shape[0]
-    cap = mask.shape[0]
+    sources, window = src.shape[0], mask.shape[2]
     halo = arrived.shape[2] // (2 * LANES)
+    width = 2 * halo * LANES
     at = pl.multiple_of(jnp.where(own == 0, window - halo, 0), 16)
     spread(arrived, wide, at, halo, sources, window)
     for part in range(2):
         for s in range(sources):
             for h in range(2):
                 src[s, pl.ds(part * window + at, halo), h * LANES : (h + 1) * LANES] = wide[
-                    part, h, pl.ds(s * window + at, halo), :
+                    part, h, pl.ds(s * (window + 1) + at, halo), :
                 ].astype(src.dtype)
-    columns = arrived[:, :, 2 * halo * LANES :].astype(jnp.float32).reshape(-1, LANES)[:halo]
-    place = lax.broadcasted_iota(jnp.int32, (window, LANES), 0)
-    for slot in range(cap):
+    for slot in range(mask.shape[0]):
         for side in range(2):
-            j = slot * 3 + 2 * side
-            mask[slot, side, pl.ds(at, halo), :] = jnp.broadcast_to(
-                columns[:, j : j + 1], (halo, LANES)
-            )
+            r = slot * 2 + side
+            line = arrived[r // sources, r % sources : r % sources + 1, width:].astype(jnp.float32)
+            rows = column(line)
+            mask[slot, side, pl.ds(at, halo), :] = jnp.where(own == 0, rows[:halo], rows[LANES - halo :])
             end = 0 if side == 0 else window - 1
-            mask[slot, side] = jnp.where(place == end, 0.0, mask[slot, side])
-
-
-def leave_kernel(result, sc, out, wide, natural, sem):
+            mask[slot, side, end : end + 1, :] = jnp.zeros((1, LANES), jnp.float32)
+
+
+PIECES = 4
+
+
+def leave_kernel(result, sc, out, wide, natural, sems):
     own = sc[2]
     sources, window = result.shape[0], result.shape[1] // 2
     tile = out.shape[2] // (2 * LANES)
+    stride = window + 1
     for part in range(2):
         for s in range(sources):
             for h in range(2):
-                wide[part, h, pl.ds(s * window, window), :] = result[
+                wide[part, h, pl.ds(s * stride, window), :] = result[
                     s, pl.ds(part * window, window), h * LANES : (h + 1) * LANES
                 ].astype(jnp.float32)
 
@@ -221,13 +253,19 @@
         for part in range(2):
             for h in range(2):
                 lanes = pl.ds(pl.multiple_of((2 * n + h) * LANES, LANES), LANES)
-                natural[part, :, lanes] = wide[part, h, pl.ds(own + n, sources, stride=window), :].astype(out.dtype)
+                natural[part, :, lanes] = wide[part, h, pl.ds(own + n, sources, stride=stride), :].astype(out.dtype)
         return 0
 
-    lax.fori_loop(0, tile, block, 0, unroll=4)
-    copy = pltpu.make_async_copy(natural, out, sem)
-    copy.start()
-    copy.wait()
+    pieces = PIECES if tile % PIECES == 0 else 1
+    each = tile // pieces
+    copies = []
+    for piece in range(pieces):
+        lax.fori_loop(piece * each, (piece + 1) * each, block, 0, unroll=8)
+        lanes = pl.ds(piece * each * 2 * LANES, each * 2 * LANES)
+        copies.append(pltpu.make_async_copy(natural.at[:, :, lanes], out.at[:, :, lanes], sems.at[piece]))
+        copies[-1].start()
+    for copy in copies:
+        copy.wait()
 
 
 def scalars_kernel(facts, sc):
@@ -270,37 +308,37 @@
 
     facts = jnp.stack([here, layer_count[0], own]).astype(jnp.int32)
     facts = jnp.broadcast_to(jnp.pad(facts, (0, 5))[:, None], (8, LANES))
-    sc = pl.pallas_call(
-        scalars_kernel,
-        out_shape=pltpu.SMEM((3,), jnp.int32),
-        in_specs=[IN_VMEM],
-        out_specs=IN_SMEM,
-    )(held(facts))
-    cells = source[0]
-    weights = pool.reshape(cap, 3, 2 * block, block)
-    wide = pltpu.VMEM((2, 2, sources * window, LANES), f32)
-    if planes == 2:
-        columns = near_mask.transpose(1, 0, 2).reshape(tile, cap * 3).astype(bf16)
-        columns = jnp.pad(columns, ((0, 0), (0, LANES - cap * 3)))
-        sent = jnp.where(
-            plane == 0,
-            jnp.concatenate([cells[:, :, (tile - halo) * block :], beside(columns[tile - halo :], sources)], axis=2),
-            jnp.concatenate([cells[:, :, : halo * block], beside(columns[:halo], sources)], axis=2),
-        )
-        arrived = lax.ppermute(sent, "plane", [(0, 1), (1, 0)])
+    cells = pltpu.with_memory_space_constraint(source[0], pltpu.HBM)
+    weights = pltpu.with_memory_space_constraint(pool.reshape(cap, 3, 2 * block, block), pltpu.HBM)
+    wide = pltpu.VMEM((2, 2, sources * (window + 1) + 8, LANES), f32)
+    scalars = pltpu.SMEM((3,), jnp.int32)
+    if planes == 2 and tile == LANES and 2 * cap <= sources:
+        near = near_mask.transpose(0, 2, 1)
+        payload, sc = pl.pallas_call(
+            offer_kernel,
+            out_shape=(pltpu.VMEM((2, sources, halo * block + LANES), bf16), scalars),
+            in_specs=[IN_HBM, IN_VMEM, IN_VMEM],
+            out_specs=(IN_VMEM, IN_SMEM),
+            scratch_shapes=[pltpu.VMEM((2 * sources, LANES), f32), pltpu.SemaphoreType.DMA],
+            compiler_params=params,
+            cost_estimate=cost(1 << 20),
+        )(cells, held(near), held(facts))
+        arrived = lax.ppermute(payload, "plane", [(0, 1), (1, 0)])
         src, mask, w = pl.pallas_call(
             enter_kernel,
             out_shape=(
                 pltpu.VMEM((chunks, rows, block), bf16),
                 pltpu.VMEM((cap, 2, window, LANES), f32),
-                pltpu.VMEM(weights.shape, bf16),
+                pltpu.VMEM((cap, 3, block, 2 * block), bf16),
             ),
             in_specs=[IN_HBM, IN_HBM, IN_VMEM, IN_SMEM],
             out_specs=(IN_VMEM,) * 3,
-            scratch_shapes=[pltpu.VMEM(cells.shape, bf16), wide, pltpu.SemaphoreType.DMA((2,))],
+            scratch_shapes=[
+                pltpu.VMEM(source.shape[1:], bf16), wide, pltpu.VMEM(weights.shape, bf16), pltpu.SemaphoreType.DMA((2,))
+            ],
             compiler_params=params,
             cost_estimate=cost(1 << 23),
-        )(cells, weights, columns, in_smem(sc))
+        )(cells, weights, held(near), in_smem(sc))
         src, mask = pl.pallas_call(
             join_kernel,
             out_shape=(pltpu.VMEM(src.shape, bf16), pltpu.VMEM(mask.shape, f32)),
@@ -312,7 +350,8 @@
             cost_estimate=cost(1 << 20),
         )(held(arrived), in_smem(sc), held(src), held(mask))
     else:
-        whole = lax.all_gather(cells, "plane", axis=2, tiled=True)
+        sc = pl.pallas_call(scalars_kernel, out_shape=scalars, in_specs=[IN_VMEM], out_specs=IN_SMEM)(held(facts))
+        whole = lax.all_gather(source[0], "plane", axis=2, tiled=True)
         src = lax.dynamic_slice_in_dim(whole, start * block, window * block, axis=2)
         src = src.reshape(2, sources, window, block).transpose(1, 0, 2, 3).reshape(chunks, rows, block)
         present = lax.all_gather(near_mask, "plane", axis=1, tiled=True)
@@ -321,7 +360,7 @@
         before = jnp.where(place == 0, 0.0, present[:, :, 0])
         after = jnp.where(place == window - 1, 0.0, present[:, :, 2])
         mask = jnp.broadcast_to(jnp.stack([before, after], axis=1)[..., None], (cap, 2, window, LANES))
-        w = weights
+        w = pool.reshape(cap, 3, 2 * block, block).swapaxes(2, 3)
 
     def swaps(first):
         pairs = [(i, i + 1) for i in range(first, depth_n - 1, 2)]
@@ -335,7 +374,23 @@
     steps = chunks + 2 * LAG * (depth_n - 1)
     queue = [{}] * LAG
     kept = {}
+
+    def leave(result):
+        return pl.pallas_call(
+            leave_kernel,
+            out_shape=jax.ShapeDtypeStruct(source.shape[1:], bf16),
+            in_specs=[IN_VMEM, IN_SMEM],
+            out_specs=IN_HBM,
+            scratch_shapes=[wide, pltpu.VMEM(source.shape[1:], bf16), pltpu.SemaphoreType.DMA((PIECES,))],
+            compiler_params=params,
+            cost_estimate=cost(1 << 22),
+        )(held(result), in_smem(sc))[None]
+
     for step in range(steps):
+        if step == steps - 1:
+            kept["bottom"], kept["top"] = lax.optimization_barrier((kept["bottom"], kept["top"]))
+            bottom = leave(kept["bottom"])
+            bottom, kept["top"] = lax.optimization_barrier((bottom, kept["top"]))
         sends = {}
         if step < steps - LAG:
             sends["o1"] = ("r1", swaps(0))
@@ -350,25 +405,7 @@
         queue.append({to: lax.ppermute(out.pop(name), ("depth", "batch"), pairs) for name, (to, pairs) in sends.items()})
         kept.update(out)
 
-    def leave(result):
-        return pl.pallas_call(
-            leave_kernel,
-            out_shape=jax.ShapeDtypeStruct(cells.shape, bf16),
-            in_specs=[IN_VMEM, IN_SMEM],
-            out_specs=IN_HBM,
-            scratch_shapes=[wide, pltpu.VMEM(cells.shape, bf16), pltpu.SemaphoreType.DMA],
-            compiler_params=params,
-            cost_estimate=cost(1 << 23),
-        )(held(result), in_smem(sc))[None]
-
-    return (leave(kept["top"]), leave(kept["bottom"]))
-
-
-def beside(columns, sources):
-    lines = 2 * sources
-    folds = -(-columns.shape[0] // lines)
-    columns = jnp.pad(columns, ((0, folds * lines - columns.shape[0]), (0, 0)))
-    return columns.reshape(folds, 2, sources, LANES).transpose(1, 2, 0, 3).reshape(2, sources, folds * LANES)
+    return (leave(kept["top"]), bottom)
 
 
 def solution(mesh):

time: 82.8 us -> 82.2 us (level)
  local copies, waits for them, and re-layouts: 2.91 us -> 0.77 us
  starting transfers between devices: 31.9 us -> 33.9 us
    ppermute x32, starting transfers between devices: 28.9 us -> 30.9 us  [per_device(): lax.ppermute(out.pop(name), ('depth', 'batch'), pairs)]
    pallas_call x1, Pallas kernels: 1.54 us -> 3.15 us  [per_device(): pl.pallas_call(enter_kernel, out_shape=(pltpu.VMEM((chunks, rows, block),...]
    pallas_call x20, Pallas kernels: 21.9 us -> 20.5 us  [section(): pl.pallas_call(functools.partial(section_kernel, depth_n, chunks, step, p...]
    slice x1 -> x0, local copies, waits for them, and re-layouts: 0.99 us -> none  [per_device(): cells[:, :, :halo * block]]
    unnamed x4 -> x2, local copies, waits for them, and re-layouts: 1.67 us -> 0.69 us
  transfers between devices with their start and end apart: 33 -> 33, of which waited for: 14 -> 15; matrix products, arithmetic and copies ran while one was open for 0% -> 0% of each run, Pallas kernels for 28% -> 28%
where the time goes in v4:
time: 82.2 us; the launch traced here: 81 us
  starting transfers between devices  33.9 us (41%)
  Pallas kernels  27.3 us (33%)
  waiting for transfers between devices  17.3 us (21%)
  between operations  1.67 us (2%)
    ppermute x32, starting transfers between devices, per_device(): lax.ppermute(out.pop(name), ('depth', 'batch'), pairs)  30.9 us
    pallas_call x20, Pallas kernels, section(): pl.pallas_call(functools.partial(section_kernel, depth_n, chunks, step, p...  20.5 us
    ppermute x32, waiting for transfers between devices, per_device(): lax.ppermute(out.pop(name), ('depth', 'batch'), pairs)  16.9 us
    pallas_call x1, Pallas kernels, per_device(): pl.pallas_call(enter_kernel, out_shape=(pltpu.VMEM((chunks, rows, block),...  3.15 us
    ppermute x1, starting transfers between devices, per_device(): arrived = lax.ppermute(payload, 'plane', [(0, 1), (1, 0)])  3 us
    pallas_call x2, Pallas kernels, leave(): pl.pallas_call(leave_kernel, out_shape=jax.ShapeDtypeStruct(source.shape[...  2.53 us
  transfers between devices with their start and end apart: 33, of which 15 were waited for; matrix products, arithmetic and copies ran while one was open for 0% of the time, Pallas kernels for 28%

profile of v4, /device:TPU:0, one launch (start us, length us, event | category | flops | bytes accessed | tf_op | source)
XLA Modules:
  0.0 81.0 jit_solution(17486508215082755792)
XLA Ops:
  3.1 3.0 %collective-permute-start = (bf16[2,8,4224]{2,1,0:T(8,128)(2,1)S(1)}, bf16[2,8,4224]{2,1,0:T(8,128)(2,1)S(1)}, u32[]{:S(2)}, u32[]{:S(2)}) collective-permute-start(bf16[2,8,4224]{2,1,0:T(8,128)(2,1)S(1)} %get-tuple-element.86), channel_id=1, source_target_pairs={{0,2},{2,0},{1,3},{3,1},{4,6},{6,4},{5,7},{7,5},{8,10},{10,8},{9,1... | collective-permute-start | bytes 405512 | tf_op jit(solution)/shard_map/ppermute | solution.py:326
  6.1 3.2 %shard_map.60 = (bf16[8,288,256]{2,1,0:T(8,128)(2,1)S(1)}, f32[3,2,144,128]{3,2,1,0:T(8,128)S(1)}, bf16[3,3,256,512]{3,2,1,0:T(8,128)(2,1)S(1)}) custom-call(bf16[2,8,32768]{2,1,0:T(8,128)(2,1)} %bitcast.10, bf16[3,3,512,256]{3,2,1,0:T(8,128)(2,1)} %bitcast.11, s32[3,3,128]{2,1,0:T(4,128)S(1)} %bitcast.8, s32[3]{0:T(128)S(4)} %get-tuple-element.85.sc.refs_0_), custom_call_target="tpu_custom_call" | custom-call | bytes 8388608 | tf_op jit(solution)/shard_map/pallas_call | solution.py:327
  13.2 4.6 %collective-permute-done.2.refs_4_ = bf16[288,256]{1,0:T(8,128)(2,1)S(1)} collective-permute-done((bf16[288,256]{1,0:T(8,128)(2,1)S(1)}, bf16[288,256]{1,0:T(8,128)(2,1)S(1)}, u32[]{:S(2)}, u32[]{:S(2)}) %collective-permute-start.2) | collective-permute-done | bytes 147488 | tf_op jit(solution)/shard_map/ppermute | solution.py:405
  22.7 2.3 %collective-permute-done.5.refs_4_ = bf16[288,256]{1,0:T(8,128)(2,1)S(1)} collective-permute-done((bf16[288,256]{1,0:T(8,128)(2,1)S(1)}, bf16[288,256]{1,0:T(8,128)(2,1)S(1)}, u32[]{:S(2)}, u32[]{:S(2)}) %collective-permute-start.5) | collective-permute-done | bytes 147488 | tf_op jit(solution)/shard_map/ppermute | solution.py:405
  26.2 2.0 %collective-permute-start.9 = (bf16[288,256]{1,0:T(8,128)(2,1)S(1)}, bf16[288,256]{1,0:T(8,128)(2,1)S(1)}, u32[]{:S(2)}, u32[]{:S(2)}) collective-permute-start(bf16[288,256]{1,0:T(8,128)(2,1)S(1)} %get-tuple-element.110), channel_id=1, source_target_pairs={{0,4},{1,5},{8,12},{9,13},{4,0},{5,1},{12,8},{13,9},{2,6},{3,7},{1... | collective-permute-start | bytes 442376 | tf_op jit(solution)/shard_map/ppermute | solution.py:405
  28.2 1.3 %shard_map.67 = (bf16[8,4,288,256]{3,2,1,0:T(8,128)(2,1)S(1)}, bf16[8,288,256]{2,1,0:T(8,128)(2,1)S(1)}, bf16[288,256]{1,0:T(8,128)(2,1)S(1)}, bf16[288,256]{1,0:T(8,128)(2,1)S(1)}) custom-call(s32[3]{0:T(128)S(4)} %get-tuple-element.85.sc.refs_0_, bf16[8,288,256]{2,1,0:T(8,128)(2,1)S(1)} %get-tuple-element.89.refs_1_, ...), custom_call_target="tpu_custom_call", output_to_operand_aliasing={{0}: (6, {}), {1}: (7, {})} | custom-call | flops 1358954496 | bytes 589824 | tf_op jit(solution)/shard_map/pallas_call | solution.py:130
  29.5 1.4 %collective-permute-start.7 = (bf16[288,256]{1,0:T(8,128)(2,1)S(1)}, bf16[288,256]{1,0:T(8,128)(2,1)S(1)}, u32[]{:S(2)}, u32[]{:S(2)}) collective-permute-start(bf16[288,256]{1,0:T(8,128)(2,1)S(1)} %get-tuple-element.108), channel_id=1, source_target_pairs={{0,4},{1,5},{8,12},{9,13},{4,0},{5,1},{12,8},{13,9},{2,6},{3,7},{1... | collective-permute-start | bytes 442376 | tf_op jit(solution)/shard_map/ppermute | solution.py:405
  32.7 2.0 %collective-permute-start.13 = (bf16[288,256]{1,0:T(8,128)(2,1)S(1)}, bf16[288,256]{1,0:T(8,128)(2,1)S(1)}, u32[]{:S(2)}, u32[]{:S(2)}) collective-permute-start(bf16[288,256]{1,0:T(8,128)(2,1)S(1)} %get-tuple-element.119), channel_id=1, source_target_pairs={{0,4},{1,5},{8,12},{9,13},{4,0},{5,1},{12,8},{13,9},{2,6},{3,7},{1... | collective-permute-start | bytes 442376 | tf_op jit(solution)/shard_map/ppermute | solution.py:405
  34.7 1.4 %collective-permute-done.7.refs_4_ = bf16[288,256]{1,0:T(8,128)(2,1)S(1)} collective-permute-done((bf16[288,256]{1,0:T(8,128)(2,1)S(1)}, bf16[288,256]{1,0:T(8,128)(2,1)S(1)}, u32[]{:S(2)}, u32[]{:S(2)}) %collective-permute-start.7) | collective-permute-done | bytes 147488 | tf_op jit(solution)/shard_map/ppermute | solution.py:405
  37.4 1.4 %collective-permute-start.11 = (bf16[288,256]{1,0:T(8,128)(2,1)S(1)}, bf16[288,256]{1,0:T(8,128)(2,1)S(1)}, u32[]{:S(2)}, u32[]{:S(2)}) collective-permute-start(bf16[288,256]{1,0:T(8,128)(2,1)S(1)} %get-tuple-element.117), channel_id=1, source_target_pairs={{0,4},{1,5},{8,12},{9,13},{4,0},{5,1},{12,8},{13,9},{2,6},{3,7},{1... | collective-permute-start | bytes 442376 | tf_op jit(solution)/shard_map/ppermute | solution.py:405
  39.0 2.7 %collective-permute-start.17 = (bf16[288,256]{1,0:T(8,128)(2,1)S(1)}, bf16[288,256]{1,0:T(8,128)(2,1)S(1)}, u32[]{:S(2)}, u32[]{:S(2)}) collective-permute-start(bf16[288,256]{1,0:T(8,128)(2,1)S(1)} %get-tuple-element.129), channel_id=1, source_target_pairs={{0,4},{1,5},{8,12},{9,13},{4,0},{5,1},{12,8},{13,9},{2,6},{3,7},{1... | collective-permute-start | bytes 442376 | tf_op jit(solution)/shard_map/ppermute | solution.py:405
  41.7 1.6 %collective-permute-done.11.refs_4_ = bf16[288,256]{1,0:T(8,128)(2,1)S(1)} collective-permute-done((bf16[288,256]{1,0:T(8,128)(2,1)S(1)}, bf16[288,256]{1,0:T(8,128)(2,1)S(1)}, u32[]{:S(2)}, u32[]{:S(2)}) %collective-permute-start.11) | collective-permute-done | bytes 147488 | tf_op jit(solution)/shard_map/ppermute | solution.py:405
  43.3 3.3 %collective-permute-start.15 = (bf16[288,256]{1,0:T(8,128)(2,1)S(1)}, bf16[288,256]{1,0:T(8,128)(2,1)S(1)}, u32[]{:S(2)}, u32[]{:S(2)}) collective-permute-start(bf16[288,256]{1,0:T(8,128)(2,1)S(1)} %get-tuple-element.127), channel_id=1, source_target_pairs={{0,4},{1,5},{8,12},{9,13},{4,0},{5,1},{12,8},{13,9},{2,6},{3,7},{1... | collective-permute-start | bytes 442376 | tf_op jit(solution)/shard_map/ppermute | solution.py:405
  46.7 2.5 %collective-permute-start.21 = (bf16[288,256]{1,0:T(8,128)(2,1)S(1)}, bf16[288,256]{1,0:T(8,128)(2,1)S(1)}, u32[]{:S(2)}, u32[]{:S(2)}) collective-permute-start(bf16[288,256]{1,0:T(8,128)(2,1)S(1)} %get-tuple-element.139), channel_id=1, source_target_pairs={{0,4},{1,5},{8,12},{9,13},{4,0},{5,1},{12,8},{13,9},{2,6},{3,7},{1... | collective-permute-start | bytes 442376 | tf_op jit(solution)/shard_map/ppermute | solution.py:405
  50.2 3.4 %collective-permute-start.19 = (bf16[288,256]{1,0:T(8,128)(2,1)S(1)}, bf16[288,256]{1,0:T(8,128)(2,1)S(1)}, u32[]{:S(2)}, u32[]{:S(2)}) collective-permute-start(bf16[288,256]{1,0:T(8,128)(2,1)S(1)} %get-tuple-element.137), channel_id=1, source_target_pairs={{0,4},{1,5},{8,12},{9,13},{4,0},{5,1},{12,8},{13,9},{2,6},{3,7},{1... | collective-permute-start | bytes 442376 | tf_op jit(solution)/shard_map/ppermute | solution.py:405
  53.6 1.3 %shard_map.74 = (bf16[8,4,288,256]{3,2,1,0:T(8,128)(2,1)S(1)}, bf16[8,288,256]{2,1,0:T(8,128)(2,1)S(1)}, bf16[8,288,256]{2,1,0:T(8,128)(2,1)S(1)}, bf16[288,256]{1,0:T(8,128)(2,1)S(1)}, bf16[288,256]{1,0:T(8,128)(2,1)S(1)}) custom-call(s32[3]{0:T(128)S(4)} %get-tuple-element.85.sc.refs_0_, ...), custom_call_target="tpu_custom_call", output_to_operand_aliasing={{0}: (6, {}), {1}: (7, {}), {2}: (8, {})} | custom-call | flops 1358954496 | bytes 589824 | tf_op jit(solution)/shard_map/pallas_call | solution.py:130
  54.9 2.0 %collective-permute-start.25 = (bf16[288,256]{1,0:T(8,128)(2,1)S(1)}, bf16[288,256]{1,0:T(8,128)(2,1)S(1)}, u32[]{:S(2)}, u32[]{:S(2)}) collective-permute-start(bf16[288,256]{1,0:T(8,128)(2,1)S(1)} %get-tuple-element.150), channel_id=1, source_target_pairs={{0,4},{1,5},{8,12},{9,13},{4,0},{5,1},{12,8},{13,9},{2,6},{3,7},{1... | collective-permute-start | bytes 442376 | tf_op jit(solution)/shard_map/ppermute | solution.py:405
  56.9 1.5 %shard_map.75 = (bf16[8,4,288,256]{3,2,1,0:T(8,128)(2,1)S(1)}, bf16[8,288,256]{2,1,0:T(8,128)(2,1)S(1)}, bf16[8,288,256]{2,1,0:T(8,128)(2,1)S(1)}, bf16[288,256]{1,0:T(8,128)(2,1)S(1)}, bf16[288,256]{1,0:T(8,128)(2,1)S(1)}) custom-call(s32[3]{0:T(128)S(4)} %get-tuple-element.85.sc.refs_0_, ...), custom_call_target="tpu_custom_call", output_to_operand_aliasing={{0}: (6, {}), {1}: (7, {}), {2}: (8, {})} | custom-call | flops 1358954496 | bytes 589824 | tf_op jit(solution)/shard_map/pallas_call | solution.py:130
  58.4 1.9 %collective-permute-start.23 = (bf16[288,256]{1,0:T(8,128)(2,1)S(1)}, bf16[288,256]{1,0:T(8,128)(2,1)S(1)}, u32[]{:S(2)}, u32[]{:S(2)}) collective-permute-start(bf16[288,256]{1,0:T(8,128)(2,1)S(1)} %get-tuple-element.147), channel_id=1, source_target_pairs={{0,4},{1,5},{8,12},{9,13},{4,0},{5,1},{12,8},{13,9},{2,6},{3,7},{1... | collective-permute-start | bytes 442376 | tf_op jit(solution)/shard_map/ppermute | solution.py:405
  61.3 1.3 %shard_map.76 = (bf16[8,288,256]{2,1,0:T(8,128)(2,1)S(1)}, bf16[288,256]{1,0:T(8,128)(2,1)S(1)}, bf16[288,256]{1,0:T(8,128)(2,1)S(1)}) custom-call(s32[3]{0:T(128)S(4)} %get-tuple-element.85.sc.refs_0_, bf16[8,288,256]{2,1,0:T(8,128)(2,1)S(1)} %get-tuple-element.89.refs_1_, ...), custom_call_target="tpu_custom_call", output_to_operand_aliasing={{0}: (7, {})} | custom-call | flops 1358954496 | bytes 589824 | tf_op jit(solution)/shard_map/pallas_call | solution.py:130
  62.5 1.6 %collective-permute-start.29 = (bf16[288,256]{1,0:T(8,128)(2,1)S(1)}, bf16[288,256]{1,0:T(8,128)(2,1)S(1)}, u32[]{:S(2)}, u32[]{:S(2)}) collective-permute-start(bf16[288,256]{1,0:T(8,128)(2,1)S(1)} %get-tuple-element.156), channel_id=1, source_target_pairs={{0,4},{1,5},{8,12},{9,13},{4,0},{5,1},{12,8},{13,9},{2,6},{3,7},{1... | collective-permute-start | bytes 442376 | tf_op jit(solution)/shard_map/ppermute | solution.py:405
  66.0 1.6 %collective-permute-start.27 = (bf16[288,256]{1,0:T(8,128)(2,1)S(1)}, bf16[288,256]{1,0:T(8,128)(2,1)S(1)}, u32[]{:S(2)}, u32[]{:S(2)}) collective-permute-start(bf16[288,256]{1,0:T(8,128)(2,1)S(1)} %get-tuple-element.154), channel_id=1, source_target_pairs={{0,4},{1,5},{8,12},{9,13},{4,0},{5,1},{12,8},{13,9},{2,6},{3,7},{1... | collective-permute-start | bytes 442376 | tf_op jit(solution)/shard_map/ppermute | solution.py:405
  69.3 1.6 %collective-permute-start.32 = (bf16[288,256]{1,0:T(8,128)(2,1)S(1)}, bf16[288,256]{1,0:T(8,128)(2,1)S(1)}, u32[]{:S(2)}, u32[]{:S(2)}) collective-permute-start(bf16[288,256]{1,0:T(8,128)(2,1)S(1)} %get-tuple-element.162), channel_id=1, source_target_pairs={{0,4},{1,5},{8,12},{9,13},{4,0},{5,1},{12,8},{13,9},{2,6},{3,7},{1... | collective-permute-start | bytes 442376 | tf_op jit(solution)/shard_map/ppermute | solution.py:405
  73.0 1.4 %collective-permute-start.31 = (bf16[288,256]{1,0:T(8,128)(2,1)S(1)}, bf16[288,256]{1,0:T(8,128)(2,1)S(1)}, u32[]{:S(2)}, u32[]{:S(2)}) collective-permute-start(bf16[288,256]{1,0:T(8,128)(2,1)S(1)} %get-tuple-element.160), channel_id=1, source_target_pairs={{0,4},{1,5},{8,12},{9,13},{4,0},{5,1},{12,8},{13,9},{2,6},{3,7},{1... | collective-permute-start | bytes 442376 | tf_op jit(solution)/shard_map/ppermute | solution.py:405
  (72 shorter events, 29.2 us)
Async XLA Ops:
  3.1 6.6 %collective-permute-start = (bf16[2,8,4224]{2,1,0:T(8,128)(2,1)S(1)}, bf16[2,8,4224]{2,1,0:T(8,128)(2,1)S(1)}, u32[]{:S(2)}, u32[]{:S(2)}) collective-permute-start(bf16[2,8,4224]{2,1,0:T(8,128)(2,1)S(1)} %get-tuple-element.86), channel_id=1, source_target_pairs={{0,2},{2,0},{1,3},{3,1},{4,6},{6,4},{5,7},{7,5},{8,10},{10,8},{9,1... | collective-permute-start | bytes 405512 | tf_op jit(solution)/shard_map/ppermute | solution.py:326
  11.2 6.7 %collective-permute-start.2 = (bf16[288,256]{1,0:T(8,128)(2,1)S(1)}, bf16[288,256]{1,0:T(8,128)(2,1)S(1)}, u32[]{:S(2)}, u32[]{:S(2)}) collective-permute-start(bf16[288,256]{1,0:T(8,128)(2,1)S(1)} %get-tuple-element.95), channel_id=1, source_target_pairs={{0,4},{1,5},{8,12},{9,13},{4,0},{5,1},{12,8},{13,9},{2,6},{3,7},{1... | collective-permute-start | bytes 442376 | tf_op jit(solution)/shard_map/ppermute | solution.py:405
  13.0 7.3 %collective-permute-start.1 = (bf16[288,256]{1,0:T(8,128)(2,1)S(1)}, bf16[288,256]{1,0:T(8,128)(2,1)S(1)}, u32[]{:S(2)}, u32[]{:S(2)}) collective-permute-start(bf16[288,256]{1,0:T(8,128)(2,1)S(1)} %get-tuple-element.94), channel_id=1, source_target_pairs={{0,4},{1,5},{8,12},{9,13},{4,0},{5,1},{12,8},{13,9},{2,6},{3,7},{1... | collective-permute-start | bytes 442376 | tf_op jit(solution)/shard_map/ppermute | solution.py:405
  19.1 5.9 %collective-permute-start.5 = (bf16[288,256]{1,0:T(8,128)(2,1)S(1)}, bf16[288,256]{1,0:T(8,128)(2,1)S(1)}, u32[]{:S(2)}, u32[]{:S(2)}) collective-permute-start(bf16[288,256]{1,0:T(8,128)(2,1)S(1)} %get-tuple-element.102), channel_id=1, source_target_pairs={{0,4},{1,5},{8,12},{9,13},{4,0},{5,1},{12,8},{13,9},{2,6},{3,7},{1... | collective-permute-start | bytes 442376 | tf_op jit(solution)/shard_map/ppermute | solution.py:405
  19.2 5.8 %collective-permute-start.6 = (bf16[288,256]{1,0:T(8,128)(2,1)S(1)}, bf16[288,256]{1,0:T(8,128)(2,1)S(1)}, u32[]{:S(2)}, u32[]{:S(2)}) collective-permute-start(bf16[288,256]{1,0:T(8,128)(2,1)S(1)} %get-tuple-element.103), channel_id=1, source_target_pairs={{4,8},{5,9},{0,1},{12,13},{8,4},{9,5},{1,0},{13,12},{6,10},{7,11},... | collective-permute-start | bytes 442376 | tf_op jit(solution)/shard_map/ppermute | solution.py:405
  21.6 6.6 %collective-permute-start.3 = (bf16[288,256]{1,0:T(8,128)(2,1)S(1)}, bf16[288,256]{1,0:T(8,128)(2,1)S(1)}, u32[]{:S(2)}, u32[]{:S(2)}) collective-permute-start(bf16[288,256]{1,0:T(8,128)(2,1)S(1)} %get-tuple-element.100), channel_id=1, source_target_pairs={{0,4},{1,5},{8,12},{9,13},{4,0},{5,1},{12,8},{13,9},{2,6},{3,7},{1... | collective-permute-start | bytes 442376 | tf_op jit(solution)/shard_map/ppermute | solution.py:405
  22.7 5.5 %collective-permute-start.4 = (bf16[288,256]{1,0:T(8,128)(2,1)S(1)}, bf16[288,256]{1,0:T(8,128)(2,1)S(1)}, u32[]{:S(2)}, u32[]{:S(2)}) collective-permute-start(bf16[288,256]{1,0:T(8,128)(2,1)S(1)} %get-tuple-element.101), channel_id=1, source_target_pairs={{4,8},{5,9},{0,1},{12,13},{8,4},{9,5},{1,0},{13,12},{6,10},{7,11},... | collective-permute-start | bytes 442376 | tf_op jit(solution)/shard_map/ppermute | solution.py:405
  26.2 5.2 %collective-permute-start.9 = (bf16[288,256]{1,0:T(8,128)(2,1)S(1)}, bf16[288,256]{1,0:T(8,128)(2,1)S(1)}, u32[]{:S(2)}, u32[]{:S(2)}) collective-permute-start(bf16[288,256]{1,0:T(8,128)(2,1)S(1)} %get-tuple-element.110), channel_id=1, source_target_pairs={{0,4},{1,5},{8,12},{9,13},{4,0},{5,1},{12,8},{13,9},{2,6},{3,7},{1... | collective-permute-start | bytes 442376 | tf_op jit(solution)/shard_map/ppermute | solution.py:405
  29.5 6.6 %collective-permute-start.7 = (bf16[288,256]{1,0:T(8,128)(2,1)S(1)}, bf16[288,256]{1,0:T(8,128)(2,1)S(1)}, u32[]{:S(2)}, u32[]{:S(2)}) collective-permute-start(bf16[288,256]{1,0:T(8,128)(2,1)S(1)} %get-tuple-element.108), channel_id=1, source_target_pairs={{0,4},{1,5},{8,12},{9,13},{4,0},{5,1},{12,8},{13,9},{2,6},{3,7},{1... | collective-permute-start | bytes 442376 | tf_op jit(solution)/shard_map/ppermute | solution.py:405
  31.0 5.2 %collective-permute-start.8 = (bf16[288,256]{1,0:T(8,128)(2,1)S(1)}, bf16[288,256]{1,0:T(8,128)(2,1)S(1)}, u32[]{:S(2)}, u32[]{:S(2)}) collective-permute-start(bf16[288,256]{1,0:T(8,128)(2,1)S(1)} %get-tuple-element.109), channel_id=1, source_target_pairs={{4,8},{5,9},{0,1},{12,13},{8,4},{9,5},{1,0},{13,12},{6,10},{7,11},... | collective-permute-start | bytes 442376 | tf_op jit(solution)/shard_map/ppermute | solution.py:405
  32.7 6.3 %collective-permute-start.13 = (bf16[288,256]{1,0:T(8,128)(2,1)S(1)}, bf16[288,256]{1,0:T(8,128)(2,1)S(1)}, u32[]{:S(2)}, u32[]{:S(2)}) collective-permute-start(bf16[288,256]{1,0:T(8,128)(2,1)S(1)} %get-tuple-element.119), channel_id=1, source_target_pairs={{0,4},{1,5},{8,12},{9,13},{4,0},{5,1},{12,8},{13,9},{2,6},{3,7},{1... | collective-permute-start | bytes 442376 | tf_op jit(solution)/shard_map/ppermute | solution.py:405
  37.4 5.9 %collective-permute-start.11 = (bf16[288,256]{1,0:T(8,128)(2,1)S(1)}, bf16[288,256]{1,0:T(8,128)(2,1)S(1)}, u32[]{:S(2)}, u32[]{:S(2)}) collective-permute-start(bf16[288,256]{1,0:T(8,128)(2,1)S(1)} %get-tuple-element.117), channel_id=1, source_target_pairs={{0,4},{1,5},{8,12},{9,13},{4,0},{5,1},{12,8},{13,9},{2,6},{3,7},{1... | collective-permute-start | bytes 442376 | tf_op jit(solution)/shard_map/ppermute | solution.py:405
  38.8 4.5 %collective-permute-start.12 = (bf16[288,256]{1,0:T(8,128)(2,1)S(1)}, bf16[288,256]{1,0:T(8,128)(2,1)S(1)}, u32[]{:S(2)}, u32[]{:S(2)}) collective-permute-start(bf16[288,256]{1,0:T(8,128)(2,1)S(1)} %get-tuple-element.118), channel_id=1, source_target_pairs={{4,8},{5,9},{0,1},{12,13},{8,4},{9,5},{1,0},{13,12},{6,10},{7,11},... | collective-permute-start | bytes 442376 | tf_op jit(solution)/shard_map/ppermute | solution.py:405
  39.0 7.6 %collective-permute-start.17 = (bf16[288,256]{1,0:T(8,128)(2,1)S(1)}, bf16[288,256]{1,0:T(8,128)(2,1)S(1)}, u32[]{:S(2)}, u32[]{:S(2)}) collective-permute-start(bf16[288,256]{1,0:T(8,128)(2,1)S(1)} %get-tuple-element.129), channel_id=1, source_target_pairs={{0,4},{1,5},{8,12},{9,13},{4,0},{5,1},{12,8},{13,9},{2,6},{3,7},{1... | collective-permute-start | bytes 442376 | tf_op jit(solution)/shard_map/ppermute | solution.py:405
  41.7 4.9 %collective-permute-start.18 = (bf16[288,256]{1,0:T(8,128)(2,1)S(1)}, bf16[288,256]{1,0:T(8,128)(2,1)S(1)}, u32[]{:S(2)}, u32[]{:S(2)}) collective-permute-start(bf16[288,256]{1,0:T(8,128)(2,1)S(1)} %get-tuple-element.130), channel_id=1, source_target_pairs={{4,8},{5,9},{0,1},{12,13},{8,4},{9,5},{1,0},{13,12},{6,10},{7,11},... | collective-permute-start | bytes 442376 | tf_op jit(solution)/shard_map/ppermute | solution.py:405
  43.3 6.9 %collective-permute-start.15 = (bf16[288,256]{1,0:T(8,128)(2,1)S(1)}, bf16[288,256]{1,0:T(8,128)(2,1)S(1)}, u32[]{:S(2)}, u32[]{:S(2)}) collective-permute-start(bf16[288,256]{1,0:T(8,128)(2,1)S(1)} %get-tuple-element.127), channel_id=1, source_target_pairs={{0,4},{1,5},{8,12},{9,13},{4,0},{5,1},{12,8},{13,9},{2,6},{3,7},{1... | collective-permute-start | bytes 442376 | tf_op jit(solution)/shard_map/ppermute | solution.py:405
  46.7 7.0 %collective-permute-start.21 = (bf16[288,256]{1,0:T(8,128)(2,1)S(1)}, bf16[288,256]{1,0:T(8,128)(2,1)S(1)}, u32[]{:S(2)}, u32[]{:S(2)}) collective-permute-start(bf16[288,256]{1,0:T(8,128)(2,1)S(1)} %get-tuple-element.139), channel_id=1, source_target_pairs={{0,4},{1,5},{8,12},{9,13},{4,0},{5,1},{12,8},{13,9},{2,6},{3,7},{1... | collective-permute-start | bytes 442376 | tf_op jit(solution)/shard_map/ppermute | solution.py:405
  50.2 6.7 %collective-permute-start.19 = (bf16[288,256]{1,0:T(8,128)(2,1)S(1)}, bf16[288,256]{1,0:T(8,128)(2,1)S(1)}, u32[]{:S(2)}, u32[]{:S(2)}) collective-permute-start(bf16[288,256]{1,0:T(8,128)(2,1)S(1)} %get-tuple-element.137), channel_id=1, source_target_pairs={{0,4},{1,5},{8,12},{9,13},{4,0},{5,1},{12,8},{13,9},{2,6},{3,7},{1... | collective-permute-start | bytes 442376 | tf_op jit(solution)/shard_map/ppermute | solution.py:405
  54.9 6.3 %collective-permute-start.25 = (bf16[288,256]{1,0:T(8,128)(2,1)S(1)}, bf16[288,256]{1,0:T(8,128)(2,1)S(1)}, u32[]{:S(2)}, u32[]{:S(2)}) collective-permute-start(bf16[288,256]{1,0:T(8,128)(2,1)S(1)} %get-tuple-element.150), channel_id=1, source_target_pairs={{0,4},{1,5},{8,12},{9,13},{4,0},{5,1},{12,8},{13,9},{2,6},{3,7},{1... | collective-permute-start | bytes 442376 | tf_op jit(solution)/shard_map/ppermute | solution.py:405
  58.4 6.3 %collective-permute-start.23 = (bf16[288,256]{1,0:T(8,128)(2,1)S(1)}, bf16[288,256]{1,0:T(8,128)(2,1)S(1)}, u32[]{:S(2)}, u32[]{:S(2)}) collective-permute-start(bf16[288,256]{1,0:T(8,128)(2,1)S(1)} %get-tuple-element.147), channel_id=1, source_target_pairs={{0,4},{1,5},{8,12},{9,13},{4,0},{5,1},{12,8},{13,9},{2,6},{3,7},{1... | collective-permute-start | bytes 442376 | tf_op jit(solution)/shard_map/ppermute | solution.py:405
  62.5 5.5 %collective-permute-start.29 = (bf16[288,256]{1,0:T(8,128)(2,1)S(1)}, bf16[288,256]{1,0:T(8,128)(2,1)S(1)}, u32[]{:S(2)}, u32[]{:S(2)}) collective-permute-start(bf16[288,256]{1,0:T(8,128)(2,1)S(1)} %get-tuple-element.156), channel_id=1, source_target_pairs={{0,4},{1,5},{8,12},{9,13},{4,0},{5,1},{12,8},{13,9},{2,6},{3,7},{1... | collective-permute-start | bytes 442376 | tf_op jit(solution)/shard_map/ppermute | solution.py:405
  66.0 5.7 %collective-permute-start.27 = (bf16[288,256]{1,0:T(8,128)(2,1)S(1)}, bf16[288,256]{1,0:T(8,128)(2,1)S(1)}, u32[]{:S(2)}, u32[]{:S(2)}) collective-permute-start(bf16[288,256]{1,0:T(8,128)(2,1)S(1)} %get-tuple-element.154), channel_id=1, source_target_pairs={{0,4},{1,5},{8,12},{9,13},{4,0},{5,1},{12,8},{13,9},{2,6},{3,7},{1... | collective-permute-start | bytes 442376 | tf_op jit(solution)/shard_map/ppermute | solution.py:405
  69.3 6.3 %collective-permute-start.32 = (bf16[288,256]{1,0:T(8,128)(2,1)S(1)}, bf16[288,256]{1,0:T(8,128)(2,1)S(1)}, u32[]{:S(2)}, u32[]{:S(2)}) collective-permute-start(bf16[288,256]{1,0:T(8,128)(2,1)S(1)} %get-tuple-element.162), channel_id=1, source_target_pairs={{0,4},{1,5},{8,12},{9,13},{4,0},{5,1},{12,8},{13,9},{2,6},{3,7},{1... | collective-permute-start | bytes 442376 | tf_op jit(solution)/shard_map/ppermute | solution.py:405
  73.0 5.4 %collective-permute-start.31 = (bf16[288,256]{1,0:T(8,128)(2,1)S(1)}, bf16[288,256]{1,0:T(8,128)(2,1)S(1)}, u32[]{:S(2)}, u32[]{:S(2)}) collective-permute-start(bf16[288,256]{1,0:T(8,128)(2,1)S(1)} %get-tuple-element.160), channel_id=1, source_target_pairs={{0,4},{1,5},{8,12},{9,13},{4,0},{5,1},{12,8},{13,9},{2,6},{3,7},{1... | collective-permute-start | bytes 442376 | tf_op jit(solution)/shard_map/ppermute | solution.py:405
  (10 other events, 36.4 us)

commit v5 on v4

--- a/solution.py
+++ b/solution.py
@@ -8,6 +8,7 @@
 from jax.sharding import PartitionSpec as P
 
 NN = (((1,), (0,)), ((), ()))
+NT = (((1,), (1,)), ((), ()))
 CHUNKS = 8
 LAG = 2
 VMEM_LIMIT = 16 * 1024 * 1024
@@ -16,12 +17,13 @@
 def apply_layer(x, w, mask, slot):
     rows, window = x.shape[0], mask.shape[2]
     half = rows // 2
+    how = NN if w.shape[2] < w.shape[3] else NT
     wide = x.astype(jnp.float32)
     before = pltpu.roll(wide, 1, 0) * jnp.tile(mask[slot, 0], (rows // window, 2))
     after = pltpu.roll(wide, rows - 1, 0) * jnp.tile(mask[slot, 1], (rows // window, 2))
-    total = lax.dot_general(before.astype(jnp.bfloat16), w[slot, 0], NN, preferred_element_type=jnp.float32)
-    total = total + lax.dot_general(x, w[slot, 1], NN, preferred_element_type=jnp.float32)
-    total = total + lax.dot_general(after.astype(jnp.bfloat16), w[slot, 2], NN, preferred_element_type=jnp.float32)
+    total = lax.dot_general(before.astype(jnp.bfloat16), w[slot, 0], how, preferred_element_type=jnp.float32)
+    total = total + lax.dot_general(x, w[slot, 1], how, preferred_element_type=jnp.float32)
+    total = total + lax.dot_general(after.astype(jnp.bfloat16), w[slot, 2], how, preferred_element_type=jnp.float32)
     block = total.shape[1] // 2
     real = total[:half, :block] - total[half:, block:]
     imag = total[half:, :block] + total[:half, block:]
@@ -145,32 +147,37 @@
 LANES = 128
 
 
-def offer_kernel(source, near, facts, payload, sc, lines, sem):
+def offer_kernel(source, near, facts, head, payload, sc, near_out, lines, sems):
     for i in range(sc.shape[0]):
         sc[i] = facts[i, 0]
-    sources, width = payload.shape[1], payload.shape[2] - LANES
+    width = payload.shape[2]
+    halo = width // (2 * LANES)
     first = jnp.where(facts[2, 0] == 0, source.shape[2] - width, 0)
-    copy = pltpu.make_async_copy(
-        source.at[:, :, pl.ds(pl.multiple_of(first, LANES), width)], payload.at[:, :, pl.ds(0, width)], sem
-    )
+    copy = pltpu.make_async_copy(source.at[:, :, pl.ds(pl.multiple_of(first, LANES), width)], payload, sems.at[0])
+    bring = pltpu.make_async_copy(near, near_out, sems.at[1])
     copy.start()
+    bring.start()
     lines[...] = jnp.zeros_like(lines)
+    bring.wait()
     for slot in range(near.shape[0]):
         for side in range(2):
-            at = slot * 2 + side
-            lines[at : at + 1, :] = near[slot, 2 * side : 2 * side + 1, :].astype(jnp.float32)
+            at = 2 * halo + slot * 2 + side
+            lines[at : at + 1, :LANES] = near_out[slot, 2 * side : 2 * side + 1, :].astype(jnp.float32)
+    copy.wait()
     for part in range(2):
-        payload[part, :, width:] = lines[part * sources : (part + 1) * sources].astype(payload.dtype)
-    copy.wait()
+        for n in range(halo):
+            at = part * halo + n
+            lines[at : at + 1, :] = payload[part, 0:1, 2 * n * LANES : 2 * (n + 1) * LANES].astype(jnp.float32)
+    head[...] = lines[...].astype(head.dtype)
 
 
 def column(line):
     return jnp.broadcast_to(line, (LANES, LANES)).T
 
 
-def enter_kernel(source, pool, near, sc, src, mask, w, natural, wide, raw, sems):
+def enter_kernel(source, pool, near, sc, src, mask, w, natural, wide, sems):
     own = pl.multiple_of(sc[2], 16)
-    bring = pltpu.make_async_copy(pool, raw, sems.at[0])
+    bring = pltpu.make_async_copy(pool, w, sems.at[0])
     load = pltpu.make_async_copy(source, natural, sems.at[1])
     load.start()
     bring.start()
@@ -190,12 +197,14 @@
                 ].astype(src.dtype)
     bring.wait()
 
+
+def turn_kernel(w, turned):
     def turn(i, _):
         slot, offset = i // 3, lax.rem(i, 3)
-        w[slot, offset] = raw[slot, offset].T
+        turned[slot, offset] = w[slot, offset].T
         return 0
 
-    lax.fori_loop(0, raw.shape[0] * 3, turn, 0)
+    lax.fori_loop(0, w.shape[0] * 3, turn, 0)
 
 
 def spread(natural, wide, first, count, sources, window):
@@ -211,27 +220,34 @@
     lax.fori_loop(0, count, block, 0, unroll=8)
 
 
-def join_kernel(arrived, sc, src_in, mask_in, src, mask, wide):
+def join_head_kernel(head, sc, src_in, mask_in, src, mask):
     own = sc[2]
-    sources, window = src.shape[0], mask.shape[2]
+    window = mask.shape[2]
+    halo = (head.shape[0] - 16) // 2
+    at = pl.multiple_of(jnp.where(own == 0, window - halo, 0), 16)
+    for part in range(2):
+        src[0, pl.ds(part * window + at, halo), :] = head[part * halo : (part + 1) * halo, :]
+    for slot in range(mask.shape[0]):
+        for side in range(2):
+            r = 2 * halo + slot * 2 + side
+            rows = column(head[r : r + 1, :LANES].astype(jnp.float32))
+            mask[slot, side, pl.ds(at, halo), :] = jnp.where(own == 0, rows[:halo], rows[LANES - halo :])
+            end = 0 if side == 0 else window - 1
+            mask[slot, side, end : end + 1, :] = jnp.zeros((1, LANES), jnp.float32)
+
+
+def join_kernel(arrived, sc, src_in, src, wide):
+    own = sc[2]
+    sources, window = src.shape[0], src.shape[1] // 2
     halo = arrived.shape[2] // (2 * LANES)
-    width = 2 * halo * LANES
     at = pl.multiple_of(jnp.where(own == 0, window - halo, 0), 16)
     spread(arrived, wide, at, halo, sources, window)
     for part in range(2):
-        for s in range(sources):
+        for s in range(1, sources):
             for h in range(2):
                 src[s, pl.ds(part * window + at, halo), h * LANES : (h + 1) * LANES] = wide[
                     part, h, pl.ds(s * (window + 1) + at, halo), :
                 ].astype(src.dtype)
-    for slot in range(mask.shape[0]):
-        for side in range(2):
-            r = slot * 2 + side
-            line = arrived[r // sources, r % sources : r % sources + 1, width:].astype(jnp.float32)
-            rows = column(line)
-            mask[slot, side, pl.ds(at, halo), :] = jnp.where(own == 0, rows[:halo], rows[LANES - halo :])
-            end = 0 if side == 0 else window - 1
-            mask[slot, side, end : end + 1, :] = jnp.zeros((1, LANES), jnp.float32)
 
 
 PIECES = 4
@@ -314,41 +330,57 @@
     scalars = pltpu.SMEM((3,), jnp.int32)
     if planes == 2 and tile == LANES and 2 * cap <= sources:
         near = near_mask.transpose(0, 2, 1)
-        payload, sc = pl.pallas_call(
+        head, payload, sc, near = pl.pallas_call(
             offer_kernel,
-            out_shape=(pltpu.VMEM((2, sources, halo * block + LANES), bf16), scalars),
-            in_specs=[IN_HBM, IN_VMEM, IN_VMEM],
-            out_specs=(IN_VMEM, IN_SMEM),
-            scratch_shapes=[pltpu.VMEM((2 * sources, LANES), f32), pltpu.SemaphoreType.DMA],
+            out_shape=(
+                pltpu.VMEM((2 * halo + 16, 2 * LANES), bf16),
+                pltpu.VMEM((2, sources, halo * block), bf16),
+                scalars,
+                pltpu.VMEM(near.shape, near.dtype),
+            ),
+            in_specs=[IN_HBM, IN_HBM, IN_VMEM],
+            out_specs=(IN_VMEM, IN_VMEM, IN_SMEM, IN_VMEM),
+            scratch_shapes=[pltpu.VMEM((2 * halo + 16, 2 * LANES), f32), pltpu.SemaphoreType.DMA((2,))],
             compiler_params=params,
             cost_estimate=cost(1 << 20),
-        )(cells, held(near), held(facts))
+        )(cells, pltpu.with_memory_space_constraint(near, pltpu.HBM), held(facts))
+        head = lax.ppermute(head, "plane", [(0, 1), (1, 0)])
         arrived = lax.ppermute(payload, "plane", [(0, 1), (1, 0)])
         src, mask, w = pl.pallas_call(
             enter_kernel,
             out_shape=(
                 pltpu.VMEM((chunks, rows, block), bf16),
                 pltpu.VMEM((cap, 2, window, LANES), f32),
-                pltpu.VMEM((cap, 3, block, 2 * block), bf16),
+                pltpu.VMEM(weights.shape, bf16),
             ),
             in_specs=[IN_HBM, IN_HBM, IN_VMEM, IN_SMEM],
             out_specs=(IN_VMEM,) * 3,
-            scratch_shapes=[
-                pltpu.VMEM(source.shape[1:], bf16), wide, pltpu.VMEM(weights.shape, bf16), pltpu.SemaphoreType.DMA((2,))
-            ],
+            scratch_shapes=[pltpu.VMEM(source.shape[1:], bf16), wide, pltpu.SemaphoreType.DMA((2,))],
             compiler_params=params,
             cost_estimate=cost(1 << 23),
         )(cells, weights, held(near), in_smem(sc))
         src, mask = pl.pallas_call(
-            join_kernel,
+            join_head_kernel,
             out_shape=(pltpu.VMEM(src.shape, bf16), pltpu.VMEM(mask.shape, f32)),
             in_specs=[IN_VMEM, IN_SMEM, IN_VMEM, IN_VMEM],
             out_specs=(IN_VMEM,) * 2,
             input_output_aliases={2: 0, 3: 1},
-            scratch_shapes=[wide],
             compiler_params=params,
-            cost_estimate=cost(1 << 20),
-        )(held(arrived), in_smem(sc), held(src), held(mask))
+            cost_estimate=cost(1 << 18),
+        )(held(head), in_smem(sc), held(src), held(mask))
+
+        def complete(src):
+            return pl.pallas_call(
+                join_kernel,
+                out_shape=pltpu.VMEM(src.shape, bf16),
+                in_specs=[IN_VMEM, IN_SMEM, IN_VMEM],
+                out_specs=IN_VMEM,
+                input_output_aliases={2: 0},
+                scratch_shapes=[wide],
+                compiler_params=params,
+                cost_estimate=cost(1 << 20),
+            )(held(arrived), in_smem(sc), held(src))
+
     else:
         sc = pl.pallas_call(scalars_kernel, out_shape=scalars, in_specs=[IN_VMEM], out_specs=IN_SMEM)(held(facts))
         whole = lax.all_gather(source[0], "plane", axis=2, tiled=True)
@@ -360,7 +392,8 @@
         before = jnp.where(place == 0, 0.0, present[:, :, 0])
         after = jnp.where(place == window - 1, 0.0, present[:, :, 2])
         mask = jnp.broadcast_to(jnp.stack([before, after], axis=1)[..., None], (cap, 2, window, LANES))
-        w = pool.reshape(cap, 3, 2 * block, block).swapaxes(2, 3)
+        w = pool.reshape(cap, 3, 2 * block, block)
+        complete = lambda src: src
 
     def swaps(first):
         pairs = [(i, i + 1) for i in range(first, depth_n - 1, 2)]
@@ -391,6 +424,17 @@
             kept["bottom"], kept["top"] = lax.optimization_barrier((kept["bottom"], kept["top"]))
             bottom = leave(kept["bottom"])
             bottom, kept["top"] = lax.optimization_barrier((bottom, kept["top"]))
+        if step == 1:
+            src = complete(src)
+        if step == LAG:
+            w = pl.pallas_call(
+                turn_kernel,
+                out_shape=pltpu.VMEM((cap, 3, block, 2 * block), bf16),
+                in_specs=[IN_VMEM],
+                out_specs=IN_VMEM,
+                compiler_params=params,
+                cost_estimate=cost(1 << 22),
+            )(held(w))
         sends = {}
         if step < steps - LAG:
             sends["o1"] = ("r1", swaps(0))

time: 82.2 us -> 81.3 us (0.989); the launches traced: 81 us -> 81.3 us
  starting transfers between devices: 33.9 us -> 49.3 us
  waiting for transfers between devices: 17.3 us -> 9.13 us
  Pallas kernels: 27.3 us -> 21 us
    ppermute x32, starting transfers between devices: 30.9 us -> 46.2 us  [per_device(): lax.ppermute(out.pop(name), ('depth', 'batch'), pairs)]
    ppermute x32, waiting for transfers between devices: 16.9 us -> 8.54 us  [per_device(): lax.ppermute(out.pop(name), ('depth', 'batch'), pairs)]
    pallas_call x20, Pallas kernels: 20.5 us -> 14.2 us  [section(): pl.pallas_call(functools.partial(section_kernel, depth_n, chunks, step, p...]
    ppermute x0 -> x1, starting transfers between devices: none -> 3 us  [per_device(): head = lax.ppermute(head, 'plane', [(0, 1), (1, 0)])]
    ppermute x1, starting transfers between devices: 3 us -> 0.08 us  [per_device(): arrived = lax.ppermute(payload, 'plane', [(0, 1), (1, 0)])]
    pallas_call x2 -> x4, Pallas kernels: 1.14 us -> 2.35 us  [the longest x1 1.13 us: per_device(): pl.pallas_call(turn_kernel, out_shape=pltpu.VMEM((cap, 3, block, 2 * bloc...]
    pallas_call x1, Pallas kernels: 3.15 us -> 2.01 us  [per_device(): pl.pallas_call(enter_kernel, out_shape=(pltpu.VMEM((chunks, rows, block),...]
  transfers between devices with their start and end apart: 33 -> 34, of which waited for: 15 -> 9; matrix products, arithmetic and copies ran while one was open for 0% -> 0% of each run, Pallas kernels for 28% -> 22%
where the time goes in v5:
time: 81.3 us
  starting transfers between devices  49.3 us (61%)
  Pallas kernels  21 us (26%)
  waiting for transfers between devices  9.13 us (11%)
  between operations  1.71 us (2%)
    ppermute x32, starting transfers between devices, per_device(): lax.ppermute(out.pop(name), ('depth', 'batch'), pairs)  46.2 us
    pallas_call x20, Pallas kernels, section(): pl.pallas_call(functools.partial(section_kernel, depth_n, chunks, step, p...  14.2 us
    ppermute x32, waiting for transfers between devices, per_device(): lax.ppermute(out.pop(name), ('depth', 'batch'), pairs)  8.54 us
    ppermute x1, starting transfers between devices, per_device(): head = lax.ppermute(head, 'plane', [(0, 1), (1, 0)])  3 us
    pallas_call x2, Pallas kernels, leave(): pl.pallas_call(leave_kernel, out_shape=jax.ShapeDtypeStruct(source.shape[...  2.53 us
    pallas_call x1, Pallas kernels, per_device(): pl.pallas_call(enter_kernel, out_shape=(pltpu.VMEM((chunks, rows, block),...  2.01 us
  transfers between devices with their start and end apart: 34, of which 9 were waited for; matrix products, arithmetic and copies ran while one was open for 0% of the time, Pallas kernels for 22%

profile of v5, /device:TPU:0, one launch (start us, length us, event | category | flops | bytes accessed | tf_op | source)
XLA Modules:
  0.0 81.3 jit_solution(2321012739694475906)
XLA Ops:
  2.5 3.0 %collective-permute-start.1 = (bf16[48,256]{1,0:T(8,128)(2,1)S(1)}, bf16[48,256]{1,0:T(8,128)(2,1)S(1)}, u32[]{:S(2)}, u32[]{:S(2)}) collective-permute-start(bf16[48,256]{1,0:T(8,128)(2,1)S(1)} %get-tuple-element.89), channel_id=1, source_target_pairs={{0,2},{2,0},{1,3},{3,1},{4,6},{6,4},{5,7},{7,5},{8,10},{10,8},{9,1... | collective-permute-start | bytes 73736 | tf_op jit(solution)/shard_map/ppermute | solution.py:347
  5.5 2.0 %shard_map.60 = (bf16[8,288,256]{2,1,0:T(8,128)(2,1)S(1)}, f32[3,2,144,128]{3,2,1,0:T(8,128)S(1)}, bf16[3,3,512,256]{3,2,1,0:T(8,128)(2,1)S(1)}) custom-call(bf16[2,8,32768]{2,1,0:T(8,128)(2,1)} %bitcast.8, bf16[3,3,512,256]{3,2,1,0:T(8,128)(2,1)} %bitcast.9, s32[3,3,128]{2,1,0:T(4,128)S(1)} %get-tuple-element.90.near, s32[3]{0:T(128)S(4)} %get-tuple-element.87.sc.refs_0_), custom_call_target="tpu_custom_call" | custom-call | bytes 8388608 | tf_op jit(solution)/shard_map/pallas_call | solution.py:349
  8.6 1.2 %collective-permute-start.3 = (bf16[288,256]{1,0:T(8,128)(2,1)S(1)}, bf16[288,256]{1,0:T(8,128)(2,1)S(1)}, u32[]{:S(2)}, u32[]{:S(2)}) collective-permute-start(bf16[288,256]{1,0:T(8,128)(2,1)S(1)} %get-tuple-element.99), channel_id=1, source_target_pairs={{0,4},{1,5},{8,12},{9,13},{4,0},{5,1},{12,8},{13,9},{2,6},{3,7},{1... | collective-permute-start | bytes 442376 | tf_op jit(solution)/shard_map/ppermute | solution.py:449
  12.3 1.1 %shard_map.63.refs_2_ = bf16[3,3,256,512]{3,2,1,0:T(8,128)(2,1)S(1)} custom-call(bf16[3,3,512,256]{3,2,1,0:T(8,128)(2,1)S(1)} %get-tuple-element.94.w.refs_2_), custom_call_target="tpu_custom_call" | custom-call | bytes 4194304 | tf_op jit(solution)/shard_map/pallas_call | solution.py:430
  13.5 2.0 %collective-permute-done.3.refs_4_ = bf16[288,256]{1,0:T(8,128)(2,1)S(1)} collective-permute-done((bf16[288,256]{1,0:T(8,128)(2,1)S(1)}, bf16[288,256]{1,0:T(8,128)(2,1)S(1)}, u32[]{:S(2)}, u32[]{:S(2)}) %collective-permute-start.3) | collective-permute-done | bytes 147488 | tf_op jit(solution)/shard_map/ppermute | solution.py:449
  16.9 1.3 %collective-permute-done.2.refs_4_ = bf16[288,256]{1,0:T(8,128)(2,1)S(1)} collective-permute-done((bf16[288,256]{1,0:T(8,128)(2,1)S(1)}, bf16[288,256]{1,0:T(8,128)(2,1)S(1)}, u32[]{:S(2)}, u32[]{:S(2)}) %collective-permute-start.2) | collective-permute-done | bytes 147488 | tf_op jit(solution)/shard_map/ppermute | solution.py:449
  20.0 2.2 %collective-permute-done.6.refs_4_ = bf16[288,256]{1,0:T(8,128)(2,1)S(1)} collective-permute-done((bf16[288,256]{1,0:T(8,128)(2,1)S(1)}, bf16[288,256]{1,0:T(8,128)(2,1)S(1)}, u32[]{:S(2)}, u32[]{:S(2)}) %collective-permute-start.6) | collective-permute-done | bytes 147488 | tf_op jit(solution)/shard_map/ppermute | solution.py:449
  23.1 2.0 %collective-permute-start.10 = (bf16[288,256]{1,0:T(8,128)(2,1)S(1)}, bf16[288,256]{1,0:T(8,128)(2,1)S(1)}, u32[]{:S(2)}, u32[]{:S(2)}) collective-permute-start(bf16[288,256]{1,0:T(8,128)(2,1)S(1)} %get-tuple-element.114), channel_id=1, source_target_pairs={{0,4},{1,5},{8,12},{9,13},{4,0},{5,1},{12,8},{13,9},{2,6},{3,7},{1... | collective-permute-start | bytes 442376 | tf_op jit(solution)/shard_map/ppermute | solution.py:449
  26.2 2.0 %collective-permute-start.8 = (bf16[288,256]{1,0:T(8,128)(2,1)S(1)}, bf16[288,256]{1,0:T(8,128)(2,1)S(1)}, u32[]{:S(2)}, u32[]{:S(2)}) collective-permute-start(bf16[288,256]{1,0:T(8,128)(2,1)S(1)} %get-tuple-element.112), channel_id=1, source_target_pairs={{0,4},{1,5},{8,12},{9,13},{4,0},{5,1},{12,8},{13,9},{2,6},{3,7},{1... | collective-permute-start | bytes 442376 | tf_op jit(solution)/shard_map/ppermute | solution.py:449
  29.5 2.2 %collective-permute-start.14 = (bf16[288,256]{1,0:T(8,128)(2,1)S(1)}, bf16[288,256]{1,0:T(8,128)(2,1)S(1)}, u32[]{:S(2)}, u32[]{:S(2)}) collective-permute-start(bf16[288,256]{1,0:T(8,128)(2,1)S(1)} %get-tuple-element.123), channel_id=1, source_target_pairs={{0,4},{1,5},{8,12},{9,13},{4,0},{5,1},{12,8},{13,9},{2,6},{3,7},{1... | collective-permute-start | bytes 442376 | tf_op jit(solution)/shard_map/ppermute | solution.py:449
  33.2 2.8 %collective-permute-start.12 = (bf16[288,256]{1,0:T(8,128)(2,1)S(1)}, bf16[288,256]{1,0:T(8,128)(2,1)S(1)}, u32[]{:S(2)}, u32[]{:S(2)}) collective-permute-start(bf16[288,256]{1,0:T(8,128)(2,1)S(1)} %get-tuple-element.121), channel_id=1, source_target_pairs={{0,4},{1,5},{8,12},{9,13},{4,0},{5,1},{12,8},{13,9},{2,6},{3,7},{1... | collective-permute-start | bytes 442376 | tf_op jit(solution)/shard_map/ppermute | solution.py:449
  36.0 3.8 %collective-permute-start.18 = (bf16[288,256]{1,0:T(8,128)(2,1)S(1)}, bf16[288,256]{1,0:T(8,128)(2,1)S(1)}, u32[]{:S(2)}, u32[]{:S(2)}) collective-permute-start(bf16[288,256]{1,0:T(8,128)(2,1)S(1)} %get-tuple-element.133), channel_id=1, source_target_pairs={{0,4},{1,5},{8,12},{9,13},{4,0},{5,1},{12,8},{13,9},{2,6},{3,7},{1... | collective-permute-start | bytes 442376 | tf_op jit(solution)/shard_map/ppermute | solution.py:449
  39.8 4.5 %collective-permute-start.16 = (bf16[288,256]{1,0:T(8,128)(2,1)S(1)}, bf16[288,256]{1,0:T(8,128)(2,1)S(1)}, u32[]{:S(2)}, u32[]{:S(2)}) collective-permute-start(bf16[288,256]{1,0:T(8,128)(2,1)S(1)} %get-tuple-element.131), channel_id=1, source_target_pairs={{0,4},{1,5},{8,12},{9,13},{4,0},{5,1},{12,8},{13,9},{2,6},{3,7},{1... | collective-permute-start | bytes 442376 | tf_op jit(solution)/shard_map/ppermute | solution.py:449
  44.4 4.4 %collective-permute-start.22 = (bf16[288,256]{1,0:T(8,128)(2,1)S(1)}, bf16[288,256]{1,0:T(8,128)(2,1)S(1)}, u32[]{:S(2)}, u32[]{:S(2)}) collective-permute-start(bf16[288,256]{1,0:T(8,128)(2,1)S(1)} %get-tuple-element.143), channel_id=1, source_target_pairs={{0,4},{1,5},{8,12},{9,13},{4,0},{5,1},{12,8},{13,9},{2,6},{3,7},{1... | collective-permute-start | bytes 442376 | tf_op jit(solution)/shard_map/ppermute | solution.py:449
  48.8 3.8 %collective-permute-start.20 = (bf16[288,256]{1,0:T(8,128)(2,1)S(1)}, bf16[288,256]{1,0:T(8,128)(2,1)S(1)}, u32[]{:S(2)}, u32[]{:S(2)}) collective-permute-start(bf16[288,256]{1,0:T(8,128)(2,1)S(1)} %get-tuple-element.141), channel_id=1, source_target_pairs={{0,4},{1,5},{8,12},{9,13},{4,0},{5,1},{12,8},{13,9},{2,6},{3,7},{1... | collective-permute-start | bytes 442376 | tf_op jit(solution)/shard_map/ppermute | solution.py:449
  53.4 3.5 %collective-permute-start.26 = (bf16[288,256]{1,0:T(8,128)(2,1)S(1)}, bf16[288,256]{1,0:T(8,128)(2,1)S(1)}, u32[]{:S(2)}, u32[]{:S(2)}) collective-permute-start(bf16[288,256]{1,0:T(8,128)(2,1)S(1)} %get-tuple-element.154), channel_id=1, source_target_pairs={{0,4},{1,5},{8,12},{9,13},{4,0},{5,1},{12,8},{13,9},{2,6},{3,7},{1... | collective-permute-start | bytes 442376 | tf_op jit(solution)/shard_map/ppermute | solution.py:449
  58.0 2.9 %collective-permute-start.24 = (bf16[288,256]{1,0:T(8,128)(2,1)S(1)}, bf16[288,256]{1,0:T(8,128)(2,1)S(1)}, u32[]{:S(2)}, u32[]{:S(2)}) collective-permute-start(bf16[288,256]{1,0:T(8,128)(2,1)S(1)} %get-tuple-element.151), channel_id=1, source_target_pairs={{0,4},{1,5},{8,12},{9,13},{4,0},{5,1},{12,8},{13,9},{2,6},{3,7},{1... | collective-permute-start | bytes 442376 | tf_op jit(solution)/shard_map/ppermute | solution.py:449
  61.8 2.8 %collective-permute-start.30 = (bf16[288,256]{1,0:T(8,128)(2,1)S(1)}, bf16[288,256]{1,0:T(8,128)(2,1)S(1)}, u32[]{:S(2)}, u32[]{:S(2)}) collective-permute-start(bf16[288,256]{1,0:T(8,128)(2,1)S(1)} %get-tuple-element.160), channel_id=1, source_target_pairs={{0,4},{1,5},{8,12},{9,13},{4,0},{5,1},{12,8},{13,9},{2,6},{3,7},{1... | collective-permute-start | bytes 442376 | tf_op jit(solution)/shard_map/ppermute | solution.py:449
  65.5 3.2 %collective-permute-start.28 = (bf16[288,256]{1,0:T(8,128)(2,1)S(1)}, bf16[288,256]{1,0:T(8,128)(2,1)S(1)}, u32[]{:S(2)}, u32[]{:S(2)}) collective-permute-start(bf16[288,256]{1,0:T(8,128)(2,1)S(1)} %get-tuple-element.158), channel_id=1, source_target_pairs={{0,4},{1,5},{8,12},{9,13},{4,0},{5,1},{12,8},{13,9},{2,6},{3,7},{1... | collective-permute-start | bytes 442376 | tf_op jit(solution)/shard_map/ppermute | solution.py:449
  69.6 2.5 %collective-permute-start.33 = (bf16[288,256]{1,0:T(8,128)(2,1)S(1)}, bf16[288,256]{1,0:T(8,128)(2,1)S(1)}, u32[]{:S(2)}, u32[]{:S(2)}) collective-permute-start(bf16[288,256]{1,0:T(8,128)(2,1)S(1)} %get-tuple-element.166), channel_id=1, source_target_pairs={{0,4},{1,5},{8,12},{9,13},{4,0},{5,1},{12,8},{13,9},{2,6},{3,7},{1... | collective-permute-start | bytes 442376 | tf_op jit(solution)/shard_map/ppermute | solution.py:449
  73.0 2.2 %collective-permute-start.32 = (bf16[288,256]{1,0:T(8,128)(2,1)S(1)}, bf16[288,256]{1,0:T(8,128)(2,1)S(1)}, u32[]{:S(2)}, u32[]{:S(2)}) collective-permute-start(bf16[288,256]{1,0:T(8,128)(2,1)S(1)} %get-tuple-element.164), channel_id=1, source_target_pairs={{0,4},{1,5},{8,12},{9,13},{4,0},{5,1},{12,8},{13,9},{2,6},{3,7},{1... | collective-permute-start | bytes 442376 | tf_op jit(solution)/shard_map/ppermute | solution.py:449
  75.2 1.6 %collective-permute-done.33.refs_4_ = bf16[288,256]{1,0:T(8,128)(2,1)S(1)} collective-permute-done((bf16[288,256]{1,0:T(8,128)(2,1)S(1)}, bf16[288,256]{1,0:T(8,128)(2,1)S(1)}, u32[]{:S(2)}, u32[]{:S(2)}) %collective-permute-start.33) | collective-permute-done | bytes 147488 | tf_op jit(solution)/shard_map/ppermute | solution.py:449
  77.7 1.3 %shard_map.83 = bf16[2,8,32768]{2,1,0:T(8,128)(2,1)} custom-call(bf16[8,288,256]{2,1,0:T(8,128)(2,1)S(1)} %get-tuple-element.168.result, s32[3]{0:T(128)S(4)} %get-tuple-element.87.sc.refs_0_), custom_call_target="tpu_custom_call" | custom-call | bytes 4194304 | tf_op jit(solution)/shard_map/pallas_call | solution.py:412
  79.9 1.3 %shard_map.85 = bf16[2,8,32768]{2,1,0:T(8,128)(2,1)} custom-call(bf16[8,288,256]{2,1,0:T(8,128)(2,1)S(1)} %shard_map.84.result, s32[3]{0:T(128)S(4)} %get-tuple-element.87.sc.refs_0_), custom_call_target="tpu_custom_call" | custom-call | bytes 4194304 | tf_op jit(solution)/shard_map/pallas_call | solution.py:412
  (74 shorter events, 20.2 us)
Async XLA Ops:
  2.5 5.1 %collective-permute-start.1 = (bf16[48,256]{1,0:T(8,128)(2,1)S(1)}, bf16[48,256]{1,0:T(8,128)(2,1)S(1)}, u32[]{:S(2)}, u32[]{:S(2)}) collective-permute-start(bf16[48,256]{1,0:T(8,128)(2,1)S(1)} %get-tuple-element.89), channel_id=1, source_target_pairs={{0,2},{2,0},{1,3},{3,1},{4,6},{6,4},{5,7},{7,5},{8,10},{10,8},{9,1... | collective-permute-start | bytes 73736 | tf_op jit(solution)/shard_map/ppermute | solution.py:347
  5.5 5.0 %collective-permute-start = (bf16[2,8,4096]{2,1,0:T(8,128)(2,1)S(1)}, bf16[2,8,4096]{2,1,0:T(8,128)(2,1)S(1)}, u32[]{:S(2)}, u32[]{:S(2)}) collective-permute-start(bf16[2,8,4096]{2,1,0:T(8,128)(2,1)S(1)} %get-tuple-element.88), channel_id=1, source_target_pairs={{0,2},{2,0},{1,3},{3,1},{4,6},{6,4},{5,7},{7,5},{8,10},{10,8},{9,1... | collective-permute-start | bytes 393224 | tf_op jit(solution)/shard_map/ppermute | solution.py:348
  8.6 6.8 %collective-permute-start.3 = (bf16[288,256]{1,0:T(8,128)(2,1)S(1)}, bf16[288,256]{1,0:T(8,128)(2,1)S(1)}, u32[]{:S(2)}, u32[]{:S(2)}) collective-permute-start(bf16[288,256]{1,0:T(8,128)(2,1)S(1)} %get-tuple-element.99), channel_id=1, source_target_pairs={{0,4},{1,5},{8,12},{9,13},{4,0},{5,1},{12,8},{13,9},{2,6},{3,7},{1... | collective-permute-start | bytes 442376 | tf_op jit(solution)/shard_map/ppermute | solution.py:449
  11.4 6.7 %collective-permute-start.2 = (bf16[288,256]{1,0:T(8,128)(2,1)S(1)}, bf16[288,256]{1,0:T(8,128)(2,1)S(1)}, u32[]{:S(2)}, u32[]{:S(2)}) collective-permute-start(bf16[288,256]{1,0:T(8,128)(2,1)S(1)} %get-tuple-element.98), channel_id=1, source_target_pairs={{0,4},{1,5},{8,12},{9,13},{4,0},{5,1},{12,8},{13,9},{2,6},{3,7},{1... | collective-permute-start | bytes 442376 | tf_op jit(solution)/shard_map/ppermute | solution.py:449
  16.3 5.9 %collective-permute-start.6 = (bf16[288,256]{1,0:T(8,128)(2,1)S(1)}, bf16[288,256]{1,0:T(8,128)(2,1)S(1)}, u32[]{:S(2)}, u32[]{:S(2)}) collective-permute-start(bf16[288,256]{1,0:T(8,128)(2,1)S(1)} %get-tuple-element.106), channel_id=1, source_target_pairs={{0,4},{1,5},{8,12},{9,13},{4,0},{5,1},{12,8},{13,9},{2,6},{3,7},{1... | collective-permute-start | bytes 442376 | tf_op jit(solution)/shard_map/ppermute | solution.py:449
  16.9 5.4 %collective-permute-start.7 = (bf16[288,256]{1,0:T(8,128)(2,1)S(1)}, bf16[288,256]{1,0:T(8,128)(2,1)S(1)}, u32[]{:S(2)}, u32[]{:S(2)}) collective-permute-start(bf16[288,256]{1,0:T(8,128)(2,1)S(1)} %get-tuple-element.107), channel_id=1, source_target_pairs={{4,8},{5,9},{0,1},{12,13},{8,4},{9,5},{1,0},{13,12},{6,10},{7,11},... | collective-permute-start | bytes 442376 | tf_op jit(solution)/shard_map/ppermute | solution.py:449
  19.0 6.3 %collective-permute-start.4 = (bf16[288,256]{1,0:T(8,128)(2,1)S(1)}, bf16[288,256]{1,0:T(8,128)(2,1)S(1)}, u32[]{:S(2)}, u32[]{:S(2)}) collective-permute-start(bf16[288,256]{1,0:T(8,128)(2,1)S(1)} %get-tuple-element.104), channel_id=1, source_target_pairs={{0,4},{1,5},{8,12},{9,13},{4,0},{5,1},{12,8},{13,9},{2,6},{3,7},{1... | collective-permute-start | bytes 442376 | tf_op jit(solution)/shard_map/ppermute | solution.py:449
  20.0 5.3 %collective-permute-start.5 = (bf16[288,256]{1,0:T(8,128)(2,1)S(1)}, bf16[288,256]{1,0:T(8,128)(2,1)S(1)}, u32[]{:S(2)}, u32[]{:S(2)}) collective-permute-start(bf16[288,256]{1,0:T(8,128)(2,1)S(1)} %get-tuple-element.105), channel_id=1, source_target_pairs={{4,8},{5,9},{0,1},{12,13},{8,4},{9,5},{1,0},{13,12},{6,10},{7,11},... | collective-permute-start | bytes 442376 | tf_op jit(solution)/shard_map/ppermute | solution.py:449
  23.1 5.5 %collective-permute-start.10 = (bf16[288,256]{1,0:T(8,128)(2,1)S(1)}, bf16[288,256]{1,0:T(8,128)(2,1)S(1)}, u32[]{:S(2)}, u32[]{:S(2)}) collective-permute-start(bf16[288,256]{1,0:T(8,128)(2,1)S(1)} %get-tuple-element.114), channel_id=1, source_target_pairs={{0,4},{1,5},{8,12},{9,13},{4,0},{5,1},{12,8},{13,9},{2,6},{3,7},{1... | collective-permute-start | bytes 442376 | tf_op jit(solution)/shard_map/ppermute | solution.py:449
  26.2 6.2 %collective-permute-start.8 = (bf16[288,256]{1,0:T(8,128)(2,1)S(1)}, bf16[288,256]{1,0:T(8,128)(2,1)S(1)}, u32[]{:S(2)}, u32[]{:S(2)}) collective-permute-start(bf16[288,256]{1,0:T(8,128)(2,1)S(1)} %get-tuple-element.112), channel_id=1, source_target_pairs={{0,4},{1,5},{8,12},{9,13},{4,0},{5,1},{12,8},{13,9},{2,6},{3,7},{1... | collective-permute-start | bytes 442376 | tf_op jit(solution)/shard_map/ppermute | solution.py:449
  29.5 6.5 %collective-permute-start.14 = (bf16[288,256]{1,0:T(8,128)(2,1)S(1)}, bf16[288,256]{1,0:T(8,128)(2,1)S(1)}, u32[]{:S(2)}, u32[]{:S(2)}) collective-permute-start(bf16[288,256]{1,0:T(8,128)(2,1)S(1)} %get-tuple-element.123), channel_id=1, source_target_pairs={{0,4},{1,5},{8,12},{9,13},{4,0},{5,1},{12,8},{13,9},{2,6},{3,7},{1... | collective-permute-start | bytes 442376 | tf_op jit(solution)/shard_map/ppermute | solution.py:449
  33.2 6.6 %collective-permute-start.12 = (bf16[288,256]{1,0:T(8,128)(2,1)S(1)}, bf16[288,256]{1,0:T(8,128)(2,1)S(1)}, u32[]{:S(2)}, u32[]{:S(2)}) collective-permute-start(bf16[288,256]{1,0:T(8,128)(2,1)S(1)} %get-tuple-element.121), channel_id=1, source_target_pairs={{0,4},{1,5},{8,12},{9,13},{4,0},{5,1},{12,8},{13,9},{2,6},{3,7},{1... | collective-permute-start | bytes 442376 | tf_op jit(solution)/shard_map/ppermute | solution.py:449
  36.0 8.3 %collective-permute-start.18 = (bf16[288,256]{1,0:T(8,128)(2,1)S(1)}, bf16[288,256]{1,0:T(8,128)(2,1)S(1)}, u32[]{:S(2)}, u32[]{:S(2)}) collective-permute-start(bf16[288,256]{1,0:T(8,128)(2,1)S(1)} %get-tuple-element.133), channel_id=1, source_target_pairs={{0,4},{1,5},{8,12},{9,13},{4,0},{5,1},{12,8},{13,9},{2,6},{3,7},{1... | collective-permute-start | bytes 442376 | tf_op jit(solution)/shard_map/ppermute | solution.py:449
  39.8 4.5 %collective-permute-start.19 = (bf16[288,256]{1,0:T(8,128)(2,1)S(1)}, bf16[288,256]{1,0:T(8,128)(2,1)S(1)}, u32[]{:S(2)}, u32[]{:S(2)}) collective-permute-start(bf16[288,256]{1,0:T(8,128)(2,1)S(1)} %get-tuple-element.134), channel_id=1, source_target_pairs={{4,8},{5,9},{0,1},{12,13},{8,4},{9,5},{1,0},{13,12},{6,10},{7,11},... | collective-permute-start | bytes 442376 | tf_op jit(solution)/shard_map/ppermute | solution.py:449
  39.8 8.9 %collective-permute-start.16 = (bf16[288,256]{1,0:T(8,128)(2,1)S(1)}, bf16[288,256]{1,0:T(8,128)(2,1)S(1)}, u32[]{:S(2)}, u32[]{:S(2)}) collective-permute-start(bf16[288,256]{1,0:T(8,128)(2,1)S(1)} %get-tuple-element.131), channel_id=1, source_target_pairs={{0,4},{1,5},{8,12},{9,13},{4,0},{5,1},{12,8},{13,9},{2,6},{3,7},{1... | collective-permute-start | bytes 442376 | tf_op jit(solution)/shard_map/ppermute | solution.py:449
  44.3 4.4 %collective-permute-start.17 = (bf16[288,256]{1,0:T(8,128)(2,1)S(1)}, bf16[288,256]{1,0:T(8,128)(2,1)S(1)}, u32[]{:S(2)}, u32[]{:S(2)}) collective-permute-start(bf16[288,256]{1,0:T(8,128)(2,1)S(1)} %get-tuple-element.132), channel_id=1, source_target_pairs={{4,8},{5,9},{0,1},{12,13},{8,4},{9,5},{1,0},{13,12},{6,10},{7,11},... | collective-permute-start | bytes 442376 | tf_op jit(solution)/shard_map/ppermute | solution.py:449
  44.4 8.2 %collective-permute-start.22 = (bf16[288,256]{1,0:T(8,128)(2,1)S(1)}, bf16[288,256]{1,0:T(8,128)(2,1)S(1)}, u32[]{:S(2)}, u32[]{:S(2)}) collective-permute-start(bf16[288,256]{1,0:T(8,128)(2,1)S(1)} %get-tuple-element.143), channel_id=1, source_target_pairs={{0,4},{1,5},{8,12},{9,13},{4,0},{5,1},{12,8},{13,9},{2,6},{3,7},{1... | collective-permute-start | bytes 442376 | tf_op jit(solution)/shard_map/ppermute | solution.py:449
  48.8 8.1 %collective-permute-start.20 = (bf16[288,256]{1,0:T(8,128)(2,1)S(1)}, bf16[288,256]{1,0:T(8,128)(2,1)S(1)}, u32[]{:S(2)}, u32[]{:S(2)}) collective-permute-start(bf16[288,256]{1,0:T(8,128)(2,1)S(1)} %get-tuple-element.141), channel_id=1, source_target_pairs={{0,4},{1,5},{8,12},{9,13},{4,0},{5,1},{12,8},{13,9},{2,6},{3,7},{1... | collective-permute-start | bytes 442376 | tf_op jit(solution)/shard_map/ppermute | solution.py:449
  53.4 7.5 %collective-permute-start.26 = (bf16[288,256]{1,0:T(8,128)(2,1)S(1)}, bf16[288,256]{1,0:T(8,128)(2,1)S(1)}, u32[]{:S(2)}, u32[]{:S(2)}) collective-permute-start(bf16[288,256]{1,0:T(8,128)(2,1)S(1)} %get-tuple-element.154), channel_id=1, source_target_pairs={{0,4},{1,5},{8,12},{9,13},{4,0},{5,1},{12,8},{13,9},{2,6},{3,7},{1... | collective-permute-start | bytes 442376 | tf_op jit(solution)/shard_map/ppermute | solution.py:449
  58.0 6.6 %collective-permute-start.24 = (bf16[288,256]{1,0:T(8,128)(2,1)S(1)}, bf16[288,256]{1,0:T(8,128)(2,1)S(1)}, u32[]{:S(2)}, u32[]{:S(2)}) collective-permute-start(bf16[288,256]{1,0:T(8,128)(2,1)S(1)} %get-tuple-element.151), channel_id=1, source_target_pairs={{0,4},{1,5},{8,12},{9,13},{4,0},{5,1},{12,8},{13,9},{2,6},{3,7},{1... | collective-permute-start | bytes 442376 | tf_op jit(solution)/shard_map/ppermute | solution.py:449
  61.8 6.9 %collective-permute-start.30 = (bf16[288,256]{1,0:T(8,128)(2,1)S(1)}, bf16[288,256]{1,0:T(8,128)(2,1)S(1)}, u32[]{:S(2)}, u32[]{:S(2)}) collective-permute-start(bf16[288,256]{1,0:T(8,128)(2,1)S(1)} %get-tuple-element.160), channel_id=1, source_target_pairs={{0,4},{1,5},{8,12},{9,13},{4,0},{5,1},{12,8},{13,9},{2,6},{3,7},{1... | collective-permute-start | bytes 442376 | tf_op jit(solution)/shard_map/ppermute | solution.py:449
  65.5 6.6 %collective-permute-start.28 = (bf16[288,256]{1,0:T(8,128)(2,1)S(1)}, bf16[288,256]{1,0:T(8,128)(2,1)S(1)}, u32[]{:S(2)}, u32[]{:S(2)}) collective-permute-start(bf16[288,256]{1,0:T(8,128)(2,1)S(1)} %get-tuple-element.158), channel_id=1, source_target_pairs={{0,4},{1,5},{8,12},{9,13},{4,0},{5,1},{12,8},{13,9},{2,6},{3,7},{1... | collective-permute-start | bytes 442376 | tf_op jit(solution)/shard_map/ppermute | solution.py:449
  69.6 7.2 %collective-permute-start.33 = (bf16[288,256]{1,0:T(8,128)(2,1)S(1)}, bf16[288,256]{1,0:T(8,128)(2,1)S(1)}, u32[]{:S(2)}, u32[]{:S(2)}) collective-permute-start(bf16[288,256]{1,0:T(8,128)(2,1)S(1)} %get-tuple-element.166), channel_id=1, source_target_pairs={{0,4},{1,5},{8,12},{9,13},{4,0},{5,1},{12,8},{13,9},{2,6},{3,7},{1... | collective-permute-start | bytes 442376 | tf_op jit(solution)/shard_map/ppermute | solution.py:449
  73.0 6.1 %collective-permute-start.32 = (bf16[288,256]{1,0:T(8,128)(2,1)S(1)}, bf16[288,256]{1,0:T(8,128)(2,1)S(1)}, u32[]{:S(2)}, u32[]{:S(2)}) collective-permute-start(bf16[288,256]{1,0:T(8,128)(2,1)S(1)} %get-tuple-element.164), channel_id=1, source_target_pairs={{0,4},{1,5},{8,12},{9,13},{4,0},{5,1},{12,8},{13,9},{2,6},{3,7},{1... | collective-permute-start | bytes 442376 | tf_op jit(solution)/shard_map/ppermute | solution.py:449
  (10 other events, 39.2 us)

commit v6 on v5

--- a/solution.py
+++ b/solution.py
@@ -17,20 +17,25 @@
 def apply_layer(x, w, mask, slot):
     rows, window = x.shape[0], mask.shape[2]
     half = rows // 2
-    how = NN if w.shape[2] < w.shape[3] else NT
     wide = x.astype(jnp.float32)
     before = pltpu.roll(wide, 1, 0) * jnp.tile(mask[slot, 0], (rows // window, 2))
     after = pltpu.roll(wide, rows - 1, 0) * jnp.tile(mask[slot, 1], (rows // window, 2))
-    total = lax.dot_general(before.astype(jnp.bfloat16), w[slot, 0], how, preferred_element_type=jnp.float32)
-    total = total + lax.dot_general(x, w[slot, 1], how, preferred_element_type=jnp.float32)
-    total = total + lax.dot_general(after.astype(jnp.bfloat16), w[slot, 2], how, preferred_element_type=jnp.float32)
-    block = total.shape[1] // 2
-    real = total[:half, :block] - total[half:, block:]
-    imag = total[half:, :block] + total[:half, block:]
-    return real, imag
-
-
-def section_kernel(depth_n, chunks, step, plan, *refs):
+    sides = (before.astype(jnp.bfloat16), x, after.astype(jnp.bfloat16))
+    block = x.shape[1]
+    if w.shape[2] == block:
+        together = jnp.concatenate(sides, axis=1)
+        turned = w[slot].reshape(3 * block, 2 * block)
+        by_real = lax.dot_general(together, turned[:, :block], NN, preferred_element_type=jnp.float32)
+        by_imag = lax.dot_general(together, turned[:, block:], NN, preferred_element_type=jnp.float32)
+    else:
+        total = sum(
+            lax.dot_general(side, w[slot, i], NT, preferred_element_type=jnp.float32) for i, side in enumerate(sides)
+        )
+        by_real, by_imag = total[:, :block], total[:, block:]
+    return by_real[:half] - by_imag[half:], by_real[half:] + by_imag[:half]
+
+
+def section_kernel(depth_n, chunks, step, descends, plan, *refs):
     refs = dict(zip(plan, refs))
     sc, src, w, mask, state = (refs[name] for name in ("sc", "src", "w", "mask", "state"))
     here, count = sc[0], sc[1]
@@ -68,7 +73,6 @@
             return 0
 
         lax.fori_loop(0, count, layer, 0)
-        refs["bottom"][down_at] = state[down_at, count]
 
         def send(out):
             if out is not None:
@@ -108,7 +112,7 @@
 
         choose("o2", "o1", send)
 
-    if "bottom" in refs:
+    if descends:
         pl.when((down_at >= 0) & (down_at < chunks))(down)
     if "top" in refs:
         pl.when((up_at >= 0) & (up_at < chunks))(rise)
@@ -118,19 +122,19 @@
     return pltpu.with_memory_space_constraint(a, pltpu.VMEM)
 
 
-def section(depth_n, step, sc, fixed, arrived, kept, sends):
+def section(depth_n, step, descends, sc, fixed, arrived, kept, sends):
     src = fixed["src"]
     chunks, rows, block = src.shape
     cap = fixed["w"].shape[0]
     in_vmem = pl.BlockSpec(memory_space=pltpu.VMEM)
-    shapes = {"state": (chunks, cap + 1, rows, block), "bottom": src.shape, "top": src.shape}
-    writes = ["state"] * ("bottom" in kept) + [name for name in ("bottom", "top") if name in kept]
+    shapes = {"state": (chunks, cap + 1, rows, block), "top": src.shape}
+    writes = ["state"] * descends + ["top"] * ("top" in kept)
     ins = {**fixed, **arrived, **{name: a for name, a in kept.items() if a is not None}}
     outs = writes + list(sends)
     aliases = {1 + list(ins).index(name): outs.index(name) for name in writes if name in ins}
     plan = ["sc"] + list(ins) + outs + ["up"]
     results = pl.pallas_call(
-        functools.partial(section_kernel, depth_n, chunks, step, plan),
+        functools.partial(section_kernel, depth_n, chunks, step, descends, plan),
         out_shape=tuple(pltpu.VMEM(shapes.get(name, (rows, block)), src.dtype) for name in outs),
         in_specs=[pl.BlockSpec(memory_space=pltpu.SMEM)] + [in_vmem] * len(ins),
         out_specs=(in_vmem,) * len(outs),
@@ -255,14 +259,15 @@
 
 def leave_kernel(result, sc, out, wide, natural, sems):
     own = sc[2]
-    sources, window = result.shape[0], result.shape[1] // 2
+    sources, window = result.shape[0], result.shape[-2] // 2
     tile = out.shape[2] // (2 * LANES)
     stride = window + 1
     for part in range(2):
         for s in range(sources):
             for h in range(2):
+                where = (s,) if len(result.shape) == 3 else (s, sc[1])
                 wide[part, h, pl.ds(s * stride, window), :] = result[
-                    s, pl.ds(part * window, window), h * LANES : (h + 1) * LANES
+                    (*where, pl.ds(part * window, window), slice(h * LANES, (h + 1) * LANES))
                 ].astype(jnp.float32)
 
     def block(n, _):
@@ -421,12 +426,13 @@
 
     for step in range(steps):
         if step == steps - 1:
-            kept["bottom"], kept["top"] = lax.optimization_barrier((kept["bottom"], kept["top"]))
-            bottom = leave(kept["bottom"])
+            kept = dict(zip(kept, lax.optimization_barrier(tuple(kept.values()))))
+            bottom = leave(kept["state"])
             bottom, kept["top"] = lax.optimization_barrier((bottom, kept["top"]))
         if step == 1:
             src = complete(src)
         if step == LAG:
+            w, kept["state"] = lax.optimization_barrier((w, kept["state"]))
             w = pl.pallas_call(
                 turn_kernel,
                 out_shape=pltpu.VMEM((cap, 3, block, 2 * block), bf16),
@@ -441,11 +447,9 @@
         if LAG <= step < steps - 2 * LAG:
             sends["o2"] = ("r2", swaps(1))
         held_now = {"state": kept.get("state")}
-        if step < last_down:
-            held_now["bottom"] = kept.get("bottom")
         if step >= first_up:
             held_now["top"] = kept.get("top")
-        out = section(depth_n, step, sc, dict(src=src, w=w, mask=mask), queue.pop(0), held_now, sends)
+        out = section(depth_n, step, step < last_down, sc, dict(src=src, w=w, mask=mask), queue.pop(0), held_now, sends)
         queue.append({to: lax.ppermute(out.pop(name), ("depth", "batch"), pairs) for name, (to, pairs) in sends.items()})
         kept.update(out)
 

time: 81.3 us -> 79.9 us (0.983); the launches traced: 81.3 us -> 78.4 us
  starting transfers between devices: 49.3 us -> 33.3 us
  waiting for transfers between devices: 9.13 us -> 16.1 us
  Pallas kernels: 21 us -> 27.2 us
    ppermute x32, starting transfers between devices: 46.2 us -> 30.2 us  [per_device(): lax.ppermute(out.pop(name), ('depth', 'batch'), pairs)]
    ppermute x32, waiting for transfers between devices: 8.54 us -> 15.5 us  [per_device(): lax.ppermute(out.pop(name), ('depth', 'batch'), pairs)]
    pallas_call x20, Pallas kernels: 14.2 us -> 20.3 us  [section(): pl.pallas_call(functools.partial(section_kernel, depth_n, chunks, step, d...]
  transfers between devices with their start and end apart: 34 -> 34, of which waited for: 9 -> 16; matrix products, arithmetic and copies ran while one was open for 0% -> 0% of each run, Pallas kernels for 22% -> 30%
where the time goes in v6:
time: 79.9 us; the launch traced here: 78.4 us
  starting transfers between devices  33.3 us (42%)
  Pallas kernels  27.2 us (34%)
  waiting for transfers between devices  16.1 us (20%)
  between operations  1.67 us (2%)
    ppermute x32, starting transfers between devices, per_device(): lax.ppermute(out.pop(name), ('depth', 'batch'), pairs)  30.2 us
    pallas_call x20, Pallas kernels, section(): pl.pallas_call(functools.partial(section_kernel, depth_n, chunks, step, d...  20.3 us
    ppermute x32, waiting for transfers between devices, per_device(): lax.ppermute(out.pop(name), ('depth', 'batch'), pairs)  15.5 us
    ppermute x1, starting transfers between devices, per_device(): head = lax.ppermute(head, 'plane', [(0, 1), (1, 0)])  3 us
    pallas_call x2, Pallas kernels, leave(): pl.pallas_call(leave_kernel, out_shape=jax.ShapeDtypeStruct(source.shape[...  2.53 us
    pallas_call x1, Pallas kernels, per_device(): pl.pallas_call(enter_kernel, out_shape=(pltpu.VMEM((chunks, rows, block),...  2.01 us
  transfers between devices with their start and end apart: 34, of which 16 were waited for; matrix products, arithmetic and copies ran while one was open for 0% of the time, Pallas kernels for 30%

profile of v6, /device:TPU:0, one launch (start us, length us, event | category | flops | bytes accessed | tf_op | source)
XLA Modules:
  0.0 78.4 jit_solution(17780650861458127021)
XLA Ops:
  2.5 3.0 %collective-permute-start.1 = (bf16[48,256]{1,0:T(8,128)(2,1)S(1)}, bf16[48,256]{1,0:T(8,128)(2,1)S(1)}, u32[]{:S(2)}, u32[]{:S(2)}) collective-permute-start(bf16[48,256]{1,0:T(8,128)(2,1)S(1)} %get-tuple-element.77), channel_id=1, source_target_pairs={{0,2},{2,0},{1,3},{3,1},{4,6},{6,4},{5,7},{7,5},{8,10},{10,8},{9,1... | collective-permute-start | bytes 73736 | tf_op jit(solution)/shard_map/ppermute | solution.py:352
  5.5 2.0 %shard_map.60 = (bf16[8,288,256]{2,1,0:T(8,128)(2,1)S(1)}, f32[3,2,144,128]{3,2,1,0:T(8,128)S(1)}, bf16[3,3,512,256]{3,2,1,0:T(8,128)(2,1)S(1)}) custom-call(bf16[2,8,32768]{2,1,0:T(8,128)(2,1)} %bitcast.8, bf16[3,3,512,256]{3,2,1,0:T(8,128)(2,1)} %bitcast.9, s32[3,3,128]{2,1,0:T(4,128)S(1)} %get-tuple-element.78.near, s32[3]{0:T(128)S(4)} %get-tuple-element.75.sc.refs_0_), custom_call_target="tpu_custom_call" | custom-call | bytes 8388608 | tf_op jit(solution)/shard_map/pallas_call | solution.py:354
  7.7 1.3 %shard_map.63 = (bf16[8,4,288,256]{3,2,1,0:T(8,128)(2,1)S(1)}, bf16[288,256]{1,0:T(8,128)(2,1)S(1)}) custom-call(s32[3]{0:T(128)S(4)} %get-tuple-element.75.sc.refs_0_, bf16[8,288,256]{2,1,0:T(8,128)(2,1)S(1)} %get-tuple-element.81.src_in.refs_1_, bf16[3,3,512,256]{3,2,1,0:T(8,128)(2,1)S(1)} %get-tuple-element.86.refs_2_.w, ...), custom_call_target="tpu_custom_call" | custom-call | flops 1358954496 | bytes 589824 | tf_op jit(solution)/shard_map/pallas_call | solution.py:136
  10.5 1.3 %shard_map.64 = (bf16[8,4,288,256]{3,2,1,0:T(8,128)(2,1)S(1)}, bf16[288,256]{1,0:T(8,128)(2,1)S(1)}) custom-call(s32[3]{0:T(128)S(4)} %get-tuple-element.75.sc.refs_0_, bf16[8,288,256]{2,1,0:T(8,128)(2,1)S(1)} %shard_map.62.refs_1_, bf16[3,3,512,256]{3,2,1,0:T(8,128)(2,1)S(1)} %get-tuple-element.86.refs_2_.w, ...), custom_call_target="tpu_custom_call", output_to_operand_aliasing={{0}: (4, {})} | custom-call | flops 1358954496 | bytes 589824 | tf_op jit(solution)/shard_map/pallas_call | solution.py:136
  13.5 2.4 %collective-permute-done.3.refs_4_ = bf16[288,256]{1,0:T(8,128)(2,1)S(1)} collective-permute-done((bf16[288,256]{1,0:T(8,128)(2,1)S(1)}, bf16[288,256]{1,0:T(8,128)(2,1)S(1)}, u32[]{:S(2)}, u32[]{:S(2)}) %collective-permute-start.3) | collective-permute-done | bytes 147488 | tf_op jit(solution)/shard_map/ppermute | solution.py:453
  20.4 2.6 %collective-permute-done.6.refs_4_ = bf16[288,256]{1,0:T(8,128)(2,1)S(1)} collective-permute-done((bf16[288,256]{1,0:T(8,128)(2,1)S(1)}, bf16[288,256]{1,0:T(8,128)(2,1)S(1)}, u32[]{:S(2)}, u32[]{:S(2)}) %collective-permute-start.6) | collective-permute-done | bytes 147488 | tf_op jit(solution)/shard_map/ppermute | solution.py:453
  24.3 2.0 %collective-permute-start.10 = (bf16[288,256]{1,0:T(8,128)(2,1)S(1)}, bf16[288,256]{1,0:T(8,128)(2,1)S(1)}, u32[]{:S(2)}, u32[]{:S(2)}) collective-permute-start(bf16[288,256]{1,0:T(8,128)(2,1)S(1)} %get-tuple-element.99), channel_id=1, source_target_pairs={{0,4},{1,5},{8,12},{9,13},{4,0},{5,1},{12,8},{13,9},{2,6},{3,7},{1... | collective-permute-start | bytes 442376 | tf_op jit(solution)/shard_map/ppermute | solution.py:453
  27.6 1.8 %collective-permute-start.8 = (bf16[288,256]{1,0:T(8,128)(2,1)S(1)}, bf16[288,256]{1,0:T(8,128)(2,1)S(1)}, u32[]{:S(2)}, u32[]{:S(2)}) collective-permute-start(bf16[288,256]{1,0:T(8,128)(2,1)S(1)} %get-tuple-element.97), channel_id=1, source_target_pairs={{0,4},{1,5},{8,12},{9,13},{4,0},{5,1},{12,8},{13,9},{2,6},{3,7},{1... | collective-permute-start | bytes 442376 | tf_op jit(solution)/shard_map/ppermute | solution.py:453
  30.7 2.1 %collective-permute-start.14 = (bf16[288,256]{1,0:T(8,128)(2,1)S(1)}, bf16[288,256]{1,0:T(8,128)(2,1)S(1)}, u32[]{:S(2)}, u32[]{:S(2)}) collective-permute-start(bf16[288,256]{1,0:T(8,128)(2,1)S(1)} %get-tuple-element.106), channel_id=1, source_target_pairs={{0,4},{1,5},{8,12},{9,13},{4,0},{5,1},{12,8},{13,9},{2,6},{3,7},{1... | collective-permute-start | bytes 442376 | tf_op jit(solution)/shard_map/ppermute | solution.py:453
  35.1 1.4 %collective-permute-start.12 = (bf16[288,256]{1,0:T(8,128)(2,1)S(1)}, bf16[288,256]{1,0:T(8,128)(2,1)S(1)}, u32[]{:S(2)}, u32[]{:S(2)}) collective-permute-start(bf16[288,256]{1,0:T(8,128)(2,1)S(1)} %get-tuple-element.104), channel_id=1, source_target_pairs={{0,4},{1,5},{8,12},{9,13},{4,0},{5,1},{12,8},{13,9},{2,6},{3,7},{1... | collective-permute-start | bytes 442376 | tf_op jit(solution)/shard_map/ppermute | solution.py:453
  37.0 2.7 %collective-permute-start.18 = (bf16[288,256]{1,0:T(8,128)(2,1)S(1)}, bf16[288,256]{1,0:T(8,128)(2,1)S(1)}, u32[]{:S(2)}, u32[]{:S(2)}) collective-permute-start(bf16[288,256]{1,0:T(8,128)(2,1)S(1)} %get-tuple-element.114), channel_id=1, source_target_pairs={{0,4},{1,5},{8,12},{9,13},{4,0},{5,1},{12,8},{13,9},{2,6},{3,7},{1... | collective-permute-start | bytes 442376 | tf_op jit(solution)/shard_map/ppermute | solution.py:453
  39.7 1.7 %collective-permute-done.12.refs_4_ = bf16[288,256]{1,0:T(8,128)(2,1)S(1)} collective-permute-done((bf16[288,256]{1,0:T(8,128)(2,1)S(1)}, bf16[288,256]{1,0:T(8,128)(2,1)S(1)}, u32[]{:S(2)}, u32[]{:S(2)}) %collective-permute-start.12) | collective-permute-done | bytes 147488 | tf_op jit(solution)/shard_map/ppermute | solution.py:453
  41.4 2.6 %collective-permute-start.16 = (bf16[288,256]{1,0:T(8,128)(2,1)S(1)}, bf16[288,256]{1,0:T(8,128)(2,1)S(1)}, u32[]{:S(2)}, u32[]{:S(2)}) collective-permute-start(bf16[288,256]{1,0:T(8,128)(2,1)S(1)} %get-tuple-element.112), channel_id=1, source_target_pairs={{0,4},{1,5},{8,12},{9,13},{4,0},{5,1},{12,8},{13,9},{2,6},{3,7},{1... | collective-permute-start | bytes 442376 | tf_op jit(solution)/shard_map/ppermute | solution.py:453
  44.6 2.3 %collective-permute-start.22 = (bf16[288,256]{1,0:T(8,128)(2,1)S(1)}, bf16[288,256]{1,0:T(8,128)(2,1)S(1)}, u32[]{:S(2)}, u32[]{:S(2)}) collective-permute-start(bf16[288,256]{1,0:T(8,128)(2,1)S(1)} %get-tuple-element.122), channel_id=1, source_target_pairs={{0,4},{1,5},{8,12},{9,13},{4,0},{5,1},{12,8},{13,9},{2,6},{3,7},{1... | collective-permute-start | bytes 442376 | tf_op jit(solution)/shard_map/ppermute | solution.py:453
  47.8 3.4 %collective-permute-start.20 = (bf16[288,256]{1,0:T(8,128)(2,1)S(1)}, bf16[288,256]{1,0:T(8,128)(2,1)S(1)}, u32[]{:S(2)}, u32[]{:S(2)}) collective-permute-start(bf16[288,256]{1,0:T(8,128)(2,1)S(1)} %get-tuple-element.120), channel_id=1, source_target_pairs={{0,4},{1,5},{8,12},{9,13},{4,0},{5,1},{12,8},{13,9},{2,6},{3,7},{1... | collective-permute-start | bytes 442376 | tf_op jit(solution)/shard_map/ppermute | solution.py:453
  51.2 1.3 %shard_map.76 = (bf16[8,4,288,256]{3,2,1,0:T(8,128)(2,1)S(1)}, bf16[8,288,256]{2,1,0:T(8,128)(2,1)S(1)}, bf16[288,256]{1,0:T(8,128)(2,1)S(1)}, bf16[288,256]{1,0:T(8,128)(2,1)S(1)}) custom-call(s32[3]{0:T(128)S(4)} %get-tuple-element.75.sc.refs_0_, bf16[8,288,256]{2,1,0:T(8,128)(2,1)S(1)} %shard_map.62.refs_1_, ...), custom_call_target="tpu_custom_call", output_to_operand_aliasing={{0}: (6, {}), {1}: (7, {})} | custom-call | flops 1358954496 | bytes 589824 | tf_op jit(solution)/shard_map/pallas_call | solution.py:136
  52.5 1.9 %collective-permute-start.26 = (bf16[288,256]{1,0:T(8,128)(2,1)S(1)}, bf16[288,256]{1,0:T(8,128)(2,1)S(1)}, u32[]{:S(2)}, u32[]{:S(2)}) collective-permute-start(bf16[288,256]{1,0:T(8,128)(2,1)S(1)} %get-tuple-element.131), channel_id=1, source_target_pairs={{0,4},{1,5},{8,12},{9,13},{4,0},{5,1},{12,8},{13,9},{2,6},{3,7},{1... | collective-permute-start | bytes 442376 | tf_op jit(solution)/shard_map/ppermute | solution.py:453
  54.5 1.3 %shard_map.77 = (bf16[8,4,288,256]{3,2,1,0:T(8,128)(2,1)S(1)}, bf16[8,288,256]{2,1,0:T(8,128)(2,1)S(1)}, bf16[288,256]{1,0:T(8,128)(2,1)S(1)}, bf16[288,256]{1,0:T(8,128)(2,1)S(1)}) custom-call(s32[3]{0:T(128)S(4)} %get-tuple-element.75.sc.refs_0_, bf16[8,288,256]{2,1,0:T(8,128)(2,1)S(1)} %shard_map.62.refs_1_, ...), custom_call_target="tpu_custom_call", output_to_operand_aliasing={{0}: (6, {}), {1}: (7, {})} | custom-call | flops 1358954496 | bytes 589824 | tf_op jit(solution)/shard_map/pallas_call | solution.py:136
  55.7 1.9 %collective-permute-start.24 = (bf16[288,256]{1,0:T(8,128)(2,1)S(1)}, bf16[288,256]{1,0:T(8,128)(2,1)S(1)}, u32[]{:S(2)}, u32[]{:S(2)}) collective-permute-start(bf16[288,256]{1,0:T(8,128)(2,1)S(1)} %get-tuple-element.128), channel_id=1, source_target_pairs={{0,4},{1,5},{8,12},{9,13},{4,0},{5,1},{12,8},{13,9},{2,6},{3,7},{1... | collective-permute-start | bytes 442376 | tf_op jit(solution)/shard_map/ppermute | solution.py:453
  58.8 1.4 %shard_map.78 = (bf16[8,288,256]{2,1,0:T(8,128)(2,1)S(1)}, bf16[288,256]{1,0:T(8,128)(2,1)S(1)}, bf16[288,256]{1,0:T(8,128)(2,1)S(1)}) custom-call(s32[3]{0:T(128)S(4)} %get-tuple-element.75.sc.refs_0_, bf16[8,288,256]{2,1,0:T(8,128)(2,1)S(1)} %shard_map.62.refs_1_, bf16[3,3,256,512]{3,2,1,0:T(8,128)(2,1)S(1)} %shard_map.65.refs_2_, ...), custom_call_target="tpu_custom_call", output_to_operand_aliasing={{0}: (7, {})} | custom-call | flops 1358954496 | bytes 589824 | tf_op jit(solution)/shard_map/pallas_call | solution.py:136
  60.2 1.4 %collective-permute-start.30 = (bf16[288,256]{1,0:T(8,128)(2,1)S(1)}, bf16[288,256]{1,0:T(8,128)(2,1)S(1)}, u32[]{:S(2)}, u32[]{:S(2)}) collective-permute-start(bf16[288,256]{1,0:T(8,128)(2,1)S(1)} %get-tuple-element.137), channel_id=1, source_target_pairs={{0,4},{1,5},{8,12},{9,13},{4,0},{5,1},{12,8},{13,9},{2,6},{3,7},{1... | collective-permute-start | bytes 442376 | tf_op jit(solution)/shard_map/ppermute | solution.py:453
  63.3 1.4 %collective-permute-start.28 = (bf16[288,256]{1,0:T(8,128)(2,1)S(1)}, bf16[288,256]{1,0:T(8,128)(2,1)S(1)}, u32[]{:S(2)}, u32[]{:S(2)}) collective-permute-start(bf16[288,256]{1,0:T(8,128)(2,1)S(1)} %get-tuple-element.135), channel_id=1, source_target_pairs={{0,4},{1,5},{8,12},{9,13},{4,0},{5,1},{12,8},{13,9},{2,6},{3,7},{1... | collective-permute-start | bytes 442376 | tf_op jit(solution)/shard_map/ppermute | solution.py:453
  67.0 1.4 %collective-permute-start.33 = (bf16[288,256]{1,0:T(8,128)(2,1)S(1)}, bf16[288,256]{1,0:T(8,128)(2,1)S(1)}, u32[]{:S(2)}, u32[]{:S(2)}) collective-permute-start(bf16[288,256]{1,0:T(8,128)(2,1)S(1)} %get-tuple-element.142), channel_id=1, source_target_pairs={{0,4},{1,5},{8,12},{9,13},{4,0},{5,1},{12,8},{13,9},{2,6},{3,7},{1... | collective-permute-start | bytes 442376 | tf_op jit(solution)/shard_map/ppermute | solution.py:453
  70.5 1.4 %collective-permute-start.32 = (bf16[288,256]{1,0:T(8,128)(2,1)S(1)}, bf16[288,256]{1,0:T(8,128)(2,1)S(1)}, u32[]{:S(2)}, u32[]{:S(2)}) collective-permute-start(bf16[288,256]{1,0:T(8,128)(2,1)S(1)} %get-tuple-element.141), channel_id=1, source_target_pairs={{0,4},{1,5},{8,12},{9,13},{4,0},{5,1},{12,8},{13,9},{2,6},{3,7},{1... | collective-permute-start | bytes 442376 | tf_op jit(solution)/shard_map/ppermute | solution.py:453
  (74 shorter events, 30.6 us)
Async XLA Ops:
  2.5 5.1 %collective-permute-start.1 = (bf16[48,256]{1,0:T(8,128)(2,1)S(1)}, bf16[48,256]{1,0:T(8,128)(2,1)S(1)}, u32[]{:S(2)}, u32[]{:S(2)}) collective-permute-start(bf16[48,256]{1,0:T(8,128)(2,1)S(1)} %get-tuple-element.77), channel_id=1, source_target_pairs={{0,2},{2,0},{1,3},{3,1},{4,6},{6,4},{5,7},{7,5},{8,10},{10,8},{9,1... | collective-permute-start | bytes 73736 | tf_op jit(solution)/shard_map/ppermute | solution.py:352
  5.5 5.0 %collective-permute-start = (bf16[2,8,4096]{2,1,0:T(8,128)(2,1)S(1)}, bf16[2,8,4096]{2,1,0:T(8,128)(2,1)S(1)}, u32[]{:S(2)}, u32[]{:S(2)}) collective-permute-start(bf16[2,8,4096]{2,1,0:T(8,128)(2,1)S(1)} %get-tuple-element.76), channel_id=1, source_target_pairs={{0,2},{2,0},{1,3},{3,1},{4,6},{6,4},{5,7},{7,5},{8,10},{10,8},{9,1... | collective-permute-start | bytes 393224 | tf_op jit(solution)/shard_map/ppermute | solution.py:353
  9.1 6.8 %collective-permute-start.3 = (bf16[288,256]{1,0:T(8,128)(2,1)S(1)}, bf16[288,256]{1,0:T(8,128)(2,1)S(1)}, u32[]{:S(2)}, u32[]{:S(2)}) collective-permute-start(bf16[288,256]{1,0:T(8,128)(2,1)S(1)} %get-tuple-element.88), channel_id=1, source_target_pairs={{0,4},{1,5},{8,12},{9,13},{4,0},{5,1},{12,8},{13,9},{2,6},{3,7},{1... | collective-permute-start | bytes 442376 | tf_op jit(solution)/shard_map/ppermute | solution.py:453
  11.8 6.3 %collective-permute-start.2 = (bf16[288,256]{1,0:T(8,128)(2,1)S(1)}, bf16[288,256]{1,0:T(8,128)(2,1)S(1)}, u32[]{:S(2)}, u32[]{:S(2)}) collective-permute-start(bf16[288,256]{1,0:T(8,128)(2,1)S(1)} %get-tuple-element.87), channel_id=1, source_target_pairs={{0,4},{1,5},{8,12},{9,13},{4,0},{5,1},{12,8},{13,9},{2,6},{3,7},{1... | collective-permute-start | bytes 442376 | tf_op jit(solution)/shard_map/ppermute | solution.py:453
  17.2 5.9 %collective-permute-start.6 = (bf16[288,256]{1,0:T(8,128)(2,1)S(1)}, bf16[288,256]{1,0:T(8,128)(2,1)S(1)}, u32[]{:S(2)}, u32[]{:S(2)}) collective-permute-start(bf16[288,256]{1,0:T(8,128)(2,1)S(1)} %get-tuple-element.93), channel_id=1, source_target_pairs={{0,4},{1,5},{8,12},{9,13},{4,0},{5,1},{12,8},{13,9},{2,6},{3,7},{1... | collective-permute-start | bytes 442376 | tf_op jit(solution)/shard_map/ppermute | solution.py:453
  17.2 5.8 %collective-permute-start.7 = (bf16[288,256]{1,0:T(8,128)(2,1)S(1)}, bf16[288,256]{1,0:T(8,128)(2,1)S(1)}, u32[]{:S(2)}, u32[]{:S(2)}) collective-permute-start(bf16[288,256]{1,0:T(8,128)(2,1)S(1)} %get-tuple-element.94), channel_id=1, source_target_pairs={{4,8},{5,9},{0,1},{12,13},{8,4},{9,5},{1,0},{13,12},{6,10},{7,11},... | collective-permute-start | bytes 442376 | tf_op jit(solution)/shard_map/ppermute | solution.py:453
  19.4 6.9 %collective-permute-start.4 = (bf16[288,256]{1,0:T(8,128)(2,1)S(1)}, bf16[288,256]{1,0:T(8,128)(2,1)S(1)}, u32[]{:S(2)}, u32[]{:S(2)}) collective-permute-start(bf16[288,256]{1,0:T(8,128)(2,1)S(1)} %get-tuple-element.91), channel_id=1, source_target_pairs={{0,4},{1,5},{8,12},{9,13},{4,0},{5,1},{12,8},{13,9},{2,6},{3,7},{1... | collective-permute-start | bytes 442376 | tf_op jit(solution)/shard_map/ppermute | solution.py:453
  20.4 5.9 %collective-permute-start.5 = (bf16[288,256]{1,0:T(8,128)(2,1)S(1)}, bf16[288,256]{1,0:T(8,128)(2,1)S(1)}, u32[]{:S(2)}, u32[]{:S(2)}) collective-permute-start(bf16[288,256]{1,0:T(8,128)(2,1)S(1)} %get-tuple-element.92), channel_id=1, source_target_pairs={{4,8},{5,9},{0,1},{12,13},{8,4},{9,5},{1,0},{13,12},{6,10},{7,11},... | collective-permute-start | bytes 442376 | tf_op jit(solution)/shard_map/ppermute | solution.py:453
  24.3 5.2 %collective-permute-start.10 = (bf16[288,256]{1,0:T(8,128)(2,1)S(1)}, bf16[288,256]{1,0:T(8,128)(2,1)S(1)}, u32[]{:S(2)}, u32[]{:S(2)}) collective-permute-start(bf16[288,256]{1,0:T(8,128)(2,1)S(1)} %get-tuple-element.99), channel_id=1, source_target_pairs={{0,4},{1,5},{8,12},{9,13},{4,0},{5,1},{12,8},{13,9},{2,6},{3,7},{1... | collective-permute-start | bytes 442376 | tf_op jit(solution)/shard_map/ppermute | solution.py:453
  27.6 6.3 %collective-permute-start.8 = (bf16[288,256]{1,0:T(8,128)(2,1)S(1)}, bf16[288,256]{1,0:T(8,128)(2,1)S(1)}, u32[]{:S(2)}, u32[]{:S(2)}) collective-permute-start(bf16[288,256]{1,0:T(8,128)(2,1)S(1)} %get-tuple-element.97), channel_id=1, source_target_pairs={{0,4},{1,5},{8,12},{9,13},{4,0},{5,1},{12,8},{13,9},{2,6},{3,7},{1... | collective-permute-start | bytes 442376 | tf_op jit(solution)/shard_map/ppermute | solution.py:453
  30.7 6.3 %collective-permute-start.14 = (bf16[288,256]{1,0:T(8,128)(2,1)S(1)}, bf16[288,256]{1,0:T(8,128)(2,1)S(1)}, u32[]{:S(2)}, u32[]{:S(2)}) collective-permute-start(bf16[288,256]{1,0:T(8,128)(2,1)S(1)} %get-tuple-element.106), channel_id=1, source_target_pairs={{0,4},{1,5},{8,12},{9,13},{4,0},{5,1},{12,8},{13,9},{2,6},{3,7},{1... | collective-permute-start | bytes 442376 | tf_op jit(solution)/shard_map/ppermute | solution.py:453
  35.1 6.3 %collective-permute-start.12 = (bf16[288,256]{1,0:T(8,128)(2,1)S(1)}, bf16[288,256]{1,0:T(8,128)(2,1)S(1)}, u32[]{:S(2)}, u32[]{:S(2)}) collective-permute-start(bf16[288,256]{1,0:T(8,128)(2,1)S(1)} %get-tuple-element.104), channel_id=1, source_target_pairs={{0,4},{1,5},{8,12},{9,13},{4,0},{5,1},{12,8},{13,9},{2,6},{3,7},{1... | collective-permute-start | bytes 442376 | tf_op jit(solution)/shard_map/ppermute | solution.py:453
  36.6 4.9 %collective-permute-start.13 = (bf16[288,256]{1,0:T(8,128)(2,1)S(1)}, bf16[288,256]{1,0:T(8,128)(2,1)S(1)}, u32[]{:S(2)}, u32[]{:S(2)}) collective-permute-start(bf16[288,256]{1,0:T(8,128)(2,1)S(1)} %get-tuple-element.105), channel_id=1, source_target_pairs={{4,8},{5,9},{0,1},{12,13},{8,4},{9,5},{1,0},{13,12},{6,10},{7,11},... | collective-permute-start | bytes 442376 | tf_op jit(solution)/shard_map/ppermute | solution.py:453
  37.0 7.5 %collective-permute-start.18 = (bf16[288,256]{1,0:T(8,128)(2,1)S(1)}, bf16[288,256]{1,0:T(8,128)(2,1)S(1)}, u32[]{:S(2)}, u32[]{:S(2)}) collective-permute-start(bf16[288,256]{1,0:T(8,128)(2,1)S(1)} %get-tuple-element.114), channel_id=1, source_target_pairs={{0,4},{1,5},{8,12},{9,13},{4,0},{5,1},{12,8},{13,9},{2,6},{3,7},{1... | collective-permute-start | bytes 442376 | tf_op jit(solution)/shard_map/ppermute | solution.py:453
  39.7 4.9 %collective-permute-start.19 = (bf16[288,256]{1,0:T(8,128)(2,1)S(1)}, bf16[288,256]{1,0:T(8,128)(2,1)S(1)}, u32[]{:S(2)}, u32[]{:S(2)}) collective-permute-start(bf16[288,256]{1,0:T(8,128)(2,1)S(1)} %get-tuple-element.115), channel_id=1, source_target_pairs={{4,8},{5,9},{0,1},{12,13},{8,4},{9,5},{1,0},{13,12},{6,10},{7,11},... | collective-permute-start | bytes 442376 | tf_op jit(solution)/shard_map/ppermute | solution.py:453
  41.4 6.4 %collective-permute-start.16 = (bf16[288,256]{1,0:T(8,128)(2,1)S(1)}, bf16[288,256]{1,0:T(8,128)(2,1)S(1)}, u32[]{:S(2)}, u32[]{:S(2)}) collective-permute-start(bf16[288,256]{1,0:T(8,128)(2,1)S(1)} %get-tuple-element.112), channel_id=1, source_target_pairs={{0,4},{1,5},{8,12},{9,13},{4,0},{5,1},{12,8},{13,9},{2,6},{3,7},{1... | collective-permute-start | bytes 442376 | tf_op jit(solution)/shard_map/ppermute | solution.py:453
  44.6 6.6 %collective-permute-start.22 = (bf16[288,256]{1,0:T(8,128)(2,1)S(1)}, bf16[288,256]{1,0:T(8,128)(2,1)S(1)}, u32[]{:S(2)}, u32[]{:S(2)}) collective-permute-start(bf16[288,256]{1,0:T(8,128)(2,1)S(1)} %get-tuple-element.122), channel_id=1, source_target_pairs={{0,4},{1,5},{8,12},{9,13},{4,0},{5,1},{12,8},{13,9},{2,6},{3,7},{1... | collective-permute-start | bytes 442376 | tf_op jit(solution)/shard_map/ppermute | solution.py:453
  47.8 6.6 %collective-permute-start.20 = (bf16[288,256]{1,0:T(8,128)(2,1)S(1)}, bf16[288,256]{1,0:T(8,128)(2,1)S(1)}, u32[]{:S(2)}, u32[]{:S(2)}) collective-permute-start(bf16[288,256]{1,0:T(8,128)(2,1)S(1)} %get-tuple-element.120), channel_id=1, source_target_pairs={{0,4},{1,5},{8,12},{9,13},{4,0},{5,1},{12,8},{13,9},{2,6},{3,7},{1... | collective-permute-start | bytes 442376 | tf_op jit(solution)/shard_map/ppermute | solution.py:453
  52.5 6.3 %collective-permute-start.26 = (bf16[288,256]{1,0:T(8,128)(2,1)S(1)}, bf16[288,256]{1,0:T(8,128)(2,1)S(1)}, u32[]{:S(2)}, u32[]{:S(2)}) collective-permute-start(bf16[288,256]{1,0:T(8,128)(2,1)S(1)} %get-tuple-element.131), channel_id=1, source_target_pairs={{0,4},{1,5},{8,12},{9,13},{4,0},{5,1},{12,8},{13,9},{2,6},{3,7},{1... | collective-permute-start | bytes 442376 | tf_op jit(solution)/shard_map/ppermute | solution.py:453
  55.7 6.3 %collective-permute-start.24 = (bf16[288,256]{1,0:T(8,128)(2,1)S(1)}, bf16[288,256]{1,0:T(8,128)(2,1)S(1)}, u32[]{:S(2)}, u32[]{:S(2)}) collective-permute-start(bf16[288,256]{1,0:T(8,128)(2,1)S(1)} %get-tuple-element.128), channel_id=1, source_target_pairs={{0,4},{1,5},{8,12},{9,13},{4,0},{5,1},{12,8},{13,9},{2,6},{3,7},{1... | collective-permute-start | bytes 442376 | tf_op jit(solution)/shard_map/ppermute | solution.py:453
  60.2 5.5 %collective-permute-start.30 = (bf16[288,256]{1,0:T(8,128)(2,1)S(1)}, bf16[288,256]{1,0:T(8,128)(2,1)S(1)}, u32[]{:S(2)}, u32[]{:S(2)}) collective-permute-start(bf16[288,256]{1,0:T(8,128)(2,1)S(1)} %get-tuple-element.137), channel_id=1, source_target_pairs={{0,4},{1,5},{8,12},{9,13},{4,0},{5,1},{12,8},{13,9},{2,6},{3,7},{1... | collective-permute-start | bytes 442376 | tf_op jit(solution)/shard_map/ppermute | solution.py:453
  63.3 6.0 %collective-permute-start.28 = (bf16[288,256]{1,0:T(8,128)(2,1)S(1)}, bf16[288,256]{1,0:T(8,128)(2,1)S(1)}, u32[]{:S(2)}, u32[]{:S(2)}) collective-permute-start(bf16[288,256]{1,0:T(8,128)(2,1)S(1)} %get-tuple-element.135), channel_id=1, source_target_pairs={{0,4},{1,5},{8,12},{9,13},{4,0},{5,1},{12,8},{13,9},{2,6},{3,7},{1... | collective-permute-start | bytes 442376 | tf_op jit(solution)/shard_map/ppermute | solution.py:453
  67.0 5.4 %collective-permute-start.33 = (bf16[288,256]{1,0:T(8,128)(2,1)S(1)}, bf16[288,256]{1,0:T(8,128)(2,1)S(1)}, u32[]{:S(2)}, u32[]{:S(2)}) collective-permute-start(bf16[288,256]{1,0:T(8,128)(2,1)S(1)} %get-tuple-element.142), channel_id=1, source_target_pairs={{0,4},{1,5},{8,12},{9,13},{4,0},{5,1},{12,8},{13,9},{2,6},{3,7},{1... | collective-permute-start | bytes 442376 | tf_op jit(solution)/shard_map/ppermute | solution.py:453
  70.5 5.2 %collective-permute-start.32 = (bf16[288,256]{1,0:T(8,128)(2,1)S(1)}, bf16[288,256]{1,0:T(8,128)(2,1)S(1)}, u32[]{:S(2)}, u32[]{:S(2)}) collective-permute-start(bf16[288,256]{1,0:T(8,128)(2,1)S(1)} %get-tuple-element.141), channel_id=1, source_target_pairs={{0,4},{1,5},{8,12},{9,13},{4,0},{5,1},{12,8},{13,9},{2,6},{3,7},{1... | collective-permute-start | bytes 442376 | tf_op jit(solution)/shard_map/ppermute | solution.py:453
  (10 other events, 40.7 us)

commit v7 on v6

--- a/solution.py
+++ b/solution.py
@@ -151,6 +151,9 @@
 LANES = 128
 
 
+PIECES = 4
+
+
 def offer_kernel(source, near, facts, head, payload, sc, near_out, lines, sems):
     for i in range(sc.shape[0]):
         sc[i] = facts[i, 0]
@@ -181,9 +184,13 @@
 
 def enter_kernel(source, pool, near, sc, src, mask, w, natural, wide, sems):
     own = pl.multiple_of(sc[2], 16)
-    bring = pltpu.make_async_copy(pool, w, sems.at[0])
-    load = pltpu.make_async_copy(source, natural, sems.at[1])
-    load.start()
+    each = source.shape[2] // PIECES
+    loads = []
+    for piece in range(PIECES):
+        lanes = pl.ds(piece * each, each)
+        loads.append(pltpu.make_async_copy(source.at[:, :, lanes], natural.at[:, :, lanes], sems.at[piece]))
+        loads[-1].start()
+    bring = pltpu.make_async_copy(pool, w, sems.at[PIECES])
     bring.start()
     sources = src.shape[0]
     window = mask.shape[2]
@@ -191,8 +198,10 @@
     for slot in range(mask.shape[0]):
         for side in range(2):
             mask[slot, side, pl.ds(own, tile), :] = column(near[slot, 2 * side : 2 * side + 1, :].astype(jnp.float32))
-    load.wait()
-    spread(natural, wide, own, tile, sources, window)
+    for piece in range(PIECES):
+        loads[piece].wait()
+        count = tile // PIECES
+        spread(natural, wide, own, piece * count, count, sources, window)
     for part in range(2):
         for s in range(sources):
             for h in range(2):
@@ -211,7 +220,7 @@
     lax.fori_loop(0, w.shape[0] * 3, turn, 0)
 
 
-def spread(natural, wide, first, count, sources, window):
+def spread(natural, wide, first, begin, count, sources, window):
     def block(n, _):
         for part in range(2):
             for h in range(2):
@@ -221,7 +230,7 @@
                 )
         return 0
 
-    lax.fori_loop(0, count, block, 0, unroll=8)
+    lax.fori_loop(begin, begin + count, block, 0, unroll=8)
 
 
 def join_head_kernel(head, sc, src_in, mask_in, src, mask):
@@ -245,16 +254,13 @@
     sources, window = src.shape[0], src.shape[1] // 2
     halo = arrived.shape[2] // (2 * LANES)
     at = pl.multiple_of(jnp.where(own == 0, window - halo, 0), 16)
-    spread(arrived, wide, at, halo, sources, window)
+    spread(arrived, wide, at, 0, halo, sources, window)
     for part in range(2):
         for s in range(1, sources):
             for h in range(2):
                 src[s, pl.ds(part * window + at, halo), h * LANES : (h + 1) * LANES] = wide[
                     part, h, pl.ds(s * (window + 1) + at, halo), :
                 ].astype(src.dtype)
-
-
-PIECES = 4
 
 
 def leave_kernel(result, sc, out, wide, natural, sems):
@@ -360,7 +366,7 @@
             ),
             in_specs=[IN_HBM, IN_HBM, IN_VMEM, IN_SMEM],
             out_specs=(IN_VMEM,) * 3,
-            scratch_shapes=[pltpu.VMEM(source.shape[1:], bf16), wide, pltpu.SemaphoreType.DMA((2,))],
+            scratch_shapes=[pltpu.VMEM(source.shape[1:], bf16), wide, pltpu.SemaphoreType.DMA((PIECES + 1,))],
             compiler_params=params,
             cost_estimate=cost(1 << 23),
         )(cells, weights, held(near), in_smem(sc))

time: 79.9 us -> 81.5 us (1.020)
  starting transfers between devices: 33.3 us -> 34.7 us
    ppermute x32, starting transfers between devices: 30.2 us -> 31.6 us  [per_device(): lax.ppermute(out.pop(name), ('depth', 'batch'), pairs)]
  transfers between devices with their start and end apart: 34 -> 34, of which waited for: 16 -> 15; matrix products, arithmetic and copies ran while one was open for 0% -> 0% of each run, Pallas kernels for 30% -> 30%
where the time goes in v7:
time: 81.5 us; the launch traced here: 80.1 us
  starting transfers between devices  34.7 us (43%)
  Pallas kernels  27.3 us (33%)
  waiting for transfers between devices  16.3 us (20%)
  between operations  1.69 us (2%)
    ppermute x32, starting transfers between devices, per_device(): lax.ppermute(out.pop(name), ('depth', 'batch'), pairs)  31.6 us
    pallas_call x20, Pallas kernels, section(): pl.pallas_call(functools.partial(section_kernel, depth_n, chunks, step, d...  20.3 us
    ppermute x32, waiting for transfers between devices, per_device(): lax.ppermute(out.pop(name), ('depth', 'batch'), pairs)  15.8 us
    ppermute x1, starting transfers between devices, per_device(): head = lax.ppermute(head, 'plane', [(0, 1), (1, 0)])  3 us
    pallas_call x2, Pallas kernels, leave(): pl.pallas_call(leave_kernel, out_shape=jax.ShapeDtypeStruct(source.shape[...  2.53 us
    pallas_call x1, Pallas kernels, per_device(): pl.pallas_call(enter_kernel, out_shape=(pltpu.VMEM((chunks, rows, block),...  2.05 us
  transfers between devices with their start and end apart: 34, of which 15 were waited for; matrix products, arithmetic and copies ran while one was open for 0% of the time, Pallas kernels for 30%

profile of v7, /device:TPU:0, one launch (start us, length us, event | category | flops | bytes accessed | tf_op | source)
XLA Modules:
  0.0 80.1 jit_solution(15729444065119439963)
XLA Ops:
  2.5 3.0 %collective-permute-start.1 = (bf16[48,256]{1,0:T(8,128)(2,1)S(1)}, bf16[48,256]{1,0:T(8,128)(2,1)S(1)}, u32[]{:S(2)}, u32[]{:S(2)}) collective-permute-start(bf16[48,256]{1,0:T(8,128)(2,1)S(1)} %get-tuple-element.77), channel_id=1, source_target_pairs={{0,2},{2,0},{1,3},{3,1},{4,6},{6,4},{5,7},{7,5},{8,10},{10,8},{9,1... | collective-permute-start | bytes 73736 | tf_op jit(solution)/shard_map/ppermute | solution.py:358
  5.5 2.0 %shard_map.60 = (bf16[8,288,256]{2,1,0:T(8,128)(2,1)S(1)}, f32[3,2,144,128]{3,2,1,0:T(8,128)S(1)}, bf16[3,3,512,256]{3,2,1,0:T(8,128)(2,1)S(1)}) custom-call(bf16[2,8,32768]{2,1,0:T(8,128)(2,1)} %bitcast.8, bf16[3,3,512,256]{3,2,1,0:T(8,128)(2,1)} %bitcast.9, s32[3,3,128]{2,1,0:T(4,128)S(1)} %get-tuple-element.78.near, s32[3]{0:T(128)S(4)} %get-tuple-element.75.sc.refs_0_), custom_call_target="tpu_custom_call" | custom-call | bytes 8388608 | tf_op jit(solution)/shard_map/pallas_call | solution.py:360
  7.8 1.3 %shard_map.63 = (bf16[8,4,288,256]{3,2,1,0:T(8,128)(2,1)S(1)}, bf16[288,256]{1,0:T(8,128)(2,1)S(1)}) custom-call(s32[3]{0:T(128)S(4)} %get-tuple-element.75.sc.refs_0_, bf16[8,288,256]{2,1,0:T(8,128)(2,1)S(1)} %get-tuple-element.81.src_in.refs_1_, bf16[3,3,512,256]{3,2,1,0:T(8,128)(2,1)S(1)} %get-tuple-element.86.refs_2_.w, ...), custom_call_target="tpu_custom_call" | custom-call | flops 1358954496 | bytes 589824 | tf_op jit(solution)/shard_map/pallas_call | solution.py:136
  10.5 1.3 %shard_map.64 = (bf16[8,4,288,256]{3,2,1,0:T(8,128)(2,1)S(1)}, bf16[288,256]{1,0:T(8,128)(2,1)S(1)}) custom-call(s32[3]{0:T(128)S(4)} %get-tuple-element.75.sc.refs_0_, bf16[8,288,256]{2,1,0:T(8,128)(2,1)S(1)} %shard_map.62.refs_1_, bf16[3,3,512,256]{3,2,1,0:T(8,128)(2,1)S(1)} %get-tuple-element.86.refs_2_.w, ...), custom_call_target="tpu_custom_call", output_to_operand_aliasing={{0}: (4, {})} | custom-call | flops 1358954496 | bytes 589824 | tf_op jit(solution)/shard_map/pallas_call | solution.py:136
  13.5 2.5 %collective-permute-done.3.refs_4_ = bf16[288,256]{1,0:T(8,128)(2,1)S(1)} collective-permute-done((bf16[288,256]{1,0:T(8,128)(2,1)S(1)}, bf16[288,256]{1,0:T(8,128)(2,1)S(1)}, u32[]{:S(2)}, u32[]{:S(2)}) %collective-permute-start.3) | collective-permute-done | bytes 147488 | tf_op jit(solution)/shard_map/ppermute | solution.py:459
  20.0 3.1 %collective-permute-done.6.refs_4_ = bf16[288,256]{1,0:T(8,128)(2,1)S(1)} collective-permute-done((bf16[288,256]{1,0:T(8,128)(2,1)S(1)}, bf16[288,256]{1,0:T(8,128)(2,1)S(1)}, u32[]{:S(2)}, u32[]{:S(2)}) %collective-permute-start.6) | collective-permute-done | bytes 147488 | tf_op jit(solution)/shard_map/ppermute | solution.py:459
  24.3 1.6 %collective-permute-start.10 = (bf16[288,256]{1,0:T(8,128)(2,1)S(1)}, bf16[288,256]{1,0:T(8,128)(2,1)S(1)}, u32[]{:S(2)}, u32[]{:S(2)}) collective-permute-start(bf16[288,256]{1,0:T(8,128)(2,1)S(1)} %get-tuple-element.99), channel_id=1, source_target_pairs={{0,4},{1,5},{8,12},{9,13},{4,0},{5,1},{12,8},{13,9},{2,6},{3,7},{1... | collective-permute-start | bytes 442376 | tf_op jit(solution)/shard_map/ppermute | solution.py:459
  27.5 1.6 %collective-permute-start.8 = (bf16[288,256]{1,0:T(8,128)(2,1)S(1)}, bf16[288,256]{1,0:T(8,128)(2,1)S(1)}, u32[]{:S(2)}, u32[]{:S(2)}) collective-permute-start(bf16[288,256]{1,0:T(8,128)(2,1)S(1)} %get-tuple-element.97), channel_id=1, source_target_pairs={{0,4},{1,5},{8,12},{9,13},{4,0},{5,1},{12,8},{13,9},{2,6},{3,7},{1... | collective-permute-start | bytes 442376 | tf_op jit(solution)/shard_map/ppermute | solution.py:459
  30.8 1.3 %collective-permute-start.14 = (bf16[288,256]{1,0:T(8,128)(2,1)S(1)}, bf16[288,256]{1,0:T(8,128)(2,1)S(1)}, u32[]{:S(2)}, u32[]{:S(2)}) collective-permute-start(bf16[288,256]{1,0:T(8,128)(2,1)S(1)} %get-tuple-element.106), channel_id=1, source_target_pairs={{0,4},{1,5},{8,12},{9,13},{4,0},{5,1},{12,8},{13,9},{2,6},{3,7},{1... | collective-permute-start | bytes 442376 | tf_op jit(solution)/shard_map/ppermute | solution.py:459
  32.1 1.4 %collective-permute-done.8.refs_4_ = bf16[288,256]{1,0:T(8,128)(2,1)S(1)} collective-permute-done((bf16[288,256]{1,0:T(8,128)(2,1)S(1)}, bf16[288,256]{1,0:T(8,128)(2,1)S(1)}, u32[]{:S(2)}, u32[]{:S(2)}) %collective-permute-start.8) | collective-permute-done | bytes 147488 | tf_op jit(solution)/shard_map/ppermute | solution.py:459
  36.7 2.3 %collective-permute-start.18 = (bf16[288,256]{1,0:T(8,128)(2,1)S(1)}, bf16[288,256]{1,0:T(8,128)(2,1)S(1)}, u32[]{:S(2)}, u32[]{:S(2)}) collective-permute-start(bf16[288,256]{1,0:T(8,128)(2,1)S(1)} %get-tuple-element.114), channel_id=1, source_target_pairs={{0,4},{1,5},{8,12},{9,13},{4,0},{5,1},{12,8},{13,9},{2,6},{3,7},{1... | collective-permute-start | bytes 442376 | tf_op jit(solution)/shard_map/ppermute | solution.py:459
  39.0 2.0 %collective-permute-done.12.refs_4_ = bf16[288,256]{1,0:T(8,128)(2,1)S(1)} collective-permute-done((bf16[288,256]{1,0:T(8,128)(2,1)S(1)}, bf16[288,256]{1,0:T(8,128)(2,1)S(1)}, u32[]{:S(2)}, u32[]{:S(2)}) %collective-permute-start.12) | collective-permute-done | bytes 147488 | tf_op jit(solution)/shard_map/ppermute | solution.py:459
  40.9 2.9 %collective-permute-start.16 = (bf16[288,256]{1,0:T(8,128)(2,1)S(1)}, bf16[288,256]{1,0:T(8,128)(2,1)S(1)}, u32[]{:S(2)}, u32[]{:S(2)}) collective-permute-start(bf16[288,256]{1,0:T(8,128)(2,1)S(1)} %get-tuple-element.112), channel_id=1, source_target_pairs={{0,4},{1,5},{8,12},{9,13},{4,0},{5,1},{12,8},{13,9},{2,6},{3,7},{1... | collective-permute-start | bytes 442376 | tf_op jit(solution)/shard_map/ppermute | solution.py:459
  44.1 3.2 %collective-permute-start.22 = (bf16[288,256]{1,0:T(8,128)(2,1)S(1)}, bf16[288,256]{1,0:T(8,128)(2,1)S(1)}, u32[]{:S(2)}, u32[]{:S(2)}) collective-permute-start(bf16[288,256]{1,0:T(8,128)(2,1)S(1)} %get-tuple-element.122), channel_id=1, source_target_pairs={{0,4},{1,5},{8,12},{9,13},{4,0},{5,1},{12,8},{13,9},{2,6},{3,7},{1... | collective-permute-start | bytes 442376 | tf_op jit(solution)/shard_map/ppermute | solution.py:459
  47.3 4.3 %collective-permute-start.20 = (bf16[288,256]{1,0:T(8,128)(2,1)S(1)}, bf16[288,256]{1,0:T(8,128)(2,1)S(1)}, u32[]{:S(2)}, u32[]{:S(2)}) collective-permute-start(bf16[288,256]{1,0:T(8,128)(2,1)S(1)} %get-tuple-element.120), channel_id=1, source_target_pairs={{0,4},{1,5},{8,12},{9,13},{4,0},{5,1},{12,8},{13,9},{2,6},{3,7},{1... | collective-permute-start | bytes 442376 | tf_op jit(solution)/shard_map/ppermute | solution.py:459
  51.7 1.3 %shard_map.76 = (bf16[8,4,288,256]{3,2,1,0:T(8,128)(2,1)S(1)}, bf16[8,288,256]{2,1,0:T(8,128)(2,1)S(1)}, bf16[288,256]{1,0:T(8,128)(2,1)S(1)}, bf16[288,256]{1,0:T(8,128)(2,1)S(1)}) custom-call(s32[3]{0:T(128)S(4)} %get-tuple-element.75.sc.refs_0_, bf16[8,288,256]{2,1,0:T(8,128)(2,1)S(1)} %shard_map.62.refs_1_, ...), custom_call_target="tpu_custom_call", output_to_operand_aliasing={{0}: (6, {}), {1}: (7, {})} | custom-call | flops 1358954496 | bytes 589824 | tf_op jit(solution)/shard_map/pallas_call | solution.py:136
  53.0 2.5 %collective-permute-start.26 = (bf16[288,256]{1,0:T(8,128)(2,1)S(1)}, bf16[288,256]{1,0:T(8,128)(2,1)S(1)}, u32[]{:S(2)}, u32[]{:S(2)}) collective-permute-start(bf16[288,256]{1,0:T(8,128)(2,1)S(1)} %get-tuple-element.131), channel_id=1, source_target_pairs={{0,4},{1,5},{8,12},{9,13},{4,0},{5,1},{12,8},{13,9},{2,6},{3,7},{1... | collective-permute-start | bytes 442376 | tf_op jit(solution)/shard_map/ppermute | solution.py:459
  55.4 1.3 %shard_map.77 = (bf16[8,4,288,256]{3,2,1,0:T(8,128)(2,1)S(1)}, bf16[8,288,256]{2,1,0:T(8,128)(2,1)S(1)}, bf16[288,256]{1,0:T(8,128)(2,1)S(1)}, bf16[288,256]{1,0:T(8,128)(2,1)S(1)}) custom-call(s32[3]{0:T(128)S(4)} %get-tuple-element.75.sc.refs_0_, bf16[8,288,256]{2,1,0:T(8,128)(2,1)S(1)} %shard_map.62.refs_1_, ...), custom_call_target="tpu_custom_call", output_to_operand_aliasing={{0}: (6, {}), {1}: (7, {})} | custom-call | flops 1358954496 | bytes 589824 | tf_op jit(solution)/shard_map/pallas_call | solution.py:136
  56.7 2.1 %collective-permute-start.24 = (bf16[288,256]{1,0:T(8,128)(2,1)S(1)}, bf16[288,256]{1,0:T(8,128)(2,1)S(1)}, u32[]{:S(2)}, u32[]{:S(2)}) collective-permute-start(bf16[288,256]{1,0:T(8,128)(2,1)S(1)} %get-tuple-element.128), channel_id=1, source_target_pairs={{0,4},{1,5},{8,12},{9,13},{4,0},{5,1},{12,8},{13,9},{2,6},{3,7},{1... | collective-permute-start | bytes 442376 | tf_op jit(solution)/shard_map/ppermute | solution.py:459
  59.3 1.4 %shard_map.78 = (bf16[8,288,256]{2,1,0:T(8,128)(2,1)S(1)}, bf16[288,256]{1,0:T(8,128)(2,1)S(1)}, bf16[288,256]{1,0:T(8,128)(2,1)S(1)}) custom-call(s32[3]{0:T(128)S(4)} %get-tuple-element.75.sc.refs_0_, bf16[8,288,256]{2,1,0:T(8,128)(2,1)S(1)} %shard_map.62.refs_1_, bf16[3,3,256,512]{3,2,1,0:T(8,128)(2,1)S(1)} %shard_map.65.refs_2_, ...), custom_call_target="tpu_custom_call", output_to_operand_aliasing={{0}: (7, {})} | custom-call | flops 1358954496 | bytes 589824 | tf_op jit(solution)/shard_map/pallas_call | solution.py:136
  60.7 2.4 %collective-permute-start.30 = (bf16[288,256]{1,0:T(8,128)(2,1)S(1)}, bf16[288,256]{1,0:T(8,128)(2,1)S(1)}, u32[]{:S(2)}, u32[]{:S(2)}) collective-permute-start(bf16[288,256]{1,0:T(8,128)(2,1)S(1)} %get-tuple-element.137), channel_id=1, source_target_pairs={{0,4},{1,5},{8,12},{9,13},{4,0},{5,1},{12,8},{13,9},{2,6},{3,7},{1... | collective-permute-start | bytes 442376 | tf_op jit(solution)/shard_map/ppermute | solution.py:459
  64.4 1.9 %collective-permute-start.28 = (bf16[288,256]{1,0:T(8,128)(2,1)S(1)}, bf16[288,256]{1,0:T(8,128)(2,1)S(1)}, u32[]{:S(2)}, u32[]{:S(2)}) collective-permute-start(bf16[288,256]{1,0:T(8,128)(2,1)S(1)} %get-tuple-element.135), channel_id=1, source_target_pairs={{0,4},{1,5},{8,12},{9,13},{4,0},{5,1},{12,8},{13,9},{2,6},{3,7},{1... | collective-permute-start | bytes 442376 | tf_op jit(solution)/shard_map/ppermute | solution.py:459
  67.9 1.5 %collective-permute-start.33 = (bf16[288,256]{1,0:T(8,128)(2,1)S(1)}, bf16[288,256]{1,0:T(8,128)(2,1)S(1)}, u32[]{:S(2)}, u32[]{:S(2)}) collective-permute-start(bf16[288,256]{1,0:T(8,128)(2,1)S(1)} %get-tuple-element.142), channel_id=1, source_target_pairs={{0,4},{1,5},{8,12},{9,13},{4,0},{5,1},{12,8},{13,9},{2,6},{3,7},{1... | collective-permute-start | bytes 442376 | tf_op jit(solution)/shard_map/ppermute | solution.py:459
  69.4 1.3 %collective-permute-done.28.refs_4_ = bf16[288,256]{1,0:T(8,128)(2,1)S(1)} collective-permute-done((bf16[288,256]{1,0:T(8,128)(2,1)S(1)}, bf16[288,256]{1,0:T(8,128)(2,1)S(1)}, u32[]{:S(2)}, u32[]{:S(2)}) %collective-permute-start.28) | collective-permute-done | bytes 147488 | tf_op jit(solution)/shard_map/ppermute | solution.py:459
  (74 shorter events, 28.9 us)
Async XLA Ops:
  2.5 5.1 %collective-permute-start.1 = (bf16[48,256]{1,0:T(8,128)(2,1)S(1)}, bf16[48,256]{1,0:T(8,128)(2,1)S(1)}, u32[]{:S(2)}, u32[]{:S(2)}) collective-permute-start(bf16[48,256]{1,0:T(8,128)(2,1)S(1)} %get-tuple-element.77), channel_id=1, source_target_pairs={{0,2},{2,0},{1,3},{3,1},{4,6},{6,4},{5,7},{7,5},{8,10},{10,8},{9,1... | collective-permute-start | bytes 73736 | tf_op jit(solution)/shard_map/ppermute | solution.py:358
  5.5 5.0 %collective-permute-start = (bf16[2,8,4096]{2,1,0:T(8,128)(2,1)S(1)}, bf16[2,8,4096]{2,1,0:T(8,128)(2,1)S(1)}, u32[]{:S(2)}, u32[]{:S(2)}) collective-permute-start(bf16[2,8,4096]{2,1,0:T(8,128)(2,1)S(1)} %get-tuple-element.76), channel_id=1, source_target_pairs={{0,2},{2,0},{1,3},{3,1},{4,6},{6,4},{5,7},{7,5},{8,10},{10,8},{9,1... | collective-permute-start | bytes 393224 | tf_op jit(solution)/shard_map/ppermute | solution.py:359
  9.1 6.8 %collective-permute-start.3 = (bf16[288,256]{1,0:T(8,128)(2,1)S(1)}, bf16[288,256]{1,0:T(8,128)(2,1)S(1)}, u32[]{:S(2)}, u32[]{:S(2)}) collective-permute-start(bf16[288,256]{1,0:T(8,128)(2,1)S(1)} %get-tuple-element.88), channel_id=1, source_target_pairs={{0,4},{1,5},{8,12},{9,13},{4,0},{5,1},{12,8},{13,9},{2,6},{3,7},{1... | collective-permute-start | bytes 442376 | tf_op jit(solution)/shard_map/ppermute | solution.py:459
  11.8 6.4 %collective-permute-start.2 = (bf16[288,256]{1,0:T(8,128)(2,1)S(1)}, bf16[288,256]{1,0:T(8,128)(2,1)S(1)}, u32[]{:S(2)}, u32[]{:S(2)}) collective-permute-start(bf16[288,256]{1,0:T(8,128)(2,1)S(1)} %get-tuple-element.87), channel_id=1, source_target_pairs={{0,4},{1,5},{8,12},{9,13},{4,0},{5,1},{12,8},{13,9},{2,6},{3,7},{1... | collective-permute-start | bytes 442376 | tf_op jit(solution)/shard_map/ppermute | solution.py:459
  17.2 5.9 %collective-permute-start.6 = (bf16[288,256]{1,0:T(8,128)(2,1)S(1)}, bf16[288,256]{1,0:T(8,128)(2,1)S(1)}, u32[]{:S(2)}, u32[]{:S(2)}) collective-permute-start(bf16[288,256]{1,0:T(8,128)(2,1)S(1)} %get-tuple-element.93), channel_id=1, source_target_pairs={{0,4},{1,5},{8,12},{9,13},{4,0},{5,1},{12,8},{13,9},{2,6},{3,7},{1... | collective-permute-start | bytes 442376 | tf_op jit(solution)/shard_map/ppermute | solution.py:459
  17.3 5.8 %collective-permute-start.7 = (bf16[288,256]{1,0:T(8,128)(2,1)S(1)}, bf16[288,256]{1,0:T(8,128)(2,1)S(1)}, u32[]{:S(2)}, u32[]{:S(2)}) collective-permute-start(bf16[288,256]{1,0:T(8,128)(2,1)S(1)} %get-tuple-element.94), channel_id=1, source_target_pairs={{4,8},{5,9},{0,1},{12,13},{8,4},{9,5},{1,0},{13,12},{6,10},{7,11},... | collective-permute-start | bytes 442376 | tf_op jit(solution)/shard_map/ppermute | solution.py:459
  19.4 6.8 %collective-permute-start.4 = (bf16[288,256]{1,0:T(8,128)(2,1)S(1)}, bf16[288,256]{1,0:T(8,128)(2,1)S(1)}, u32[]{:S(2)}, u32[]{:S(2)}) collective-permute-start(bf16[288,256]{1,0:T(8,128)(2,1)S(1)} %get-tuple-element.91), channel_id=1, source_target_pairs={{0,4},{1,5},{8,12},{9,13},{4,0},{5,1},{12,8},{13,9},{2,6},{3,7},{1... | collective-permute-start | bytes 442376 | tf_op jit(solution)/shard_map/ppermute | solution.py:459
  20.0 6.3 %collective-permute-start.5 = (bf16[288,256]{1,0:T(8,128)(2,1)S(1)}, bf16[288,256]{1,0:T(8,128)(2,1)S(1)}, u32[]{:S(2)}, u32[]{:S(2)}) collective-permute-start(bf16[288,256]{1,0:T(8,128)(2,1)S(1)} %get-tuple-element.92), channel_id=1, source_target_pairs={{4,8},{5,9},{0,1},{12,13},{8,4},{9,5},{1,0},{13,12},{6,10},{7,11},... | collective-permute-start | bytes 442376 | tf_op jit(solution)/shard_map/ppermute | solution.py:459
  24.3 5.2 %collective-permute-start.10 = (bf16[288,256]{1,0:T(8,128)(2,1)S(1)}, bf16[288,256]{1,0:T(8,128)(2,1)S(1)}, u32[]{:S(2)}, u32[]{:S(2)}) collective-permute-start(bf16[288,256]{1,0:T(8,128)(2,1)S(1)} %get-tuple-element.99), channel_id=1, source_target_pairs={{0,4},{1,5},{8,12},{9,13},{4,0},{5,1},{12,8},{13,9},{2,6},{3,7},{1... | collective-permute-start | bytes 442376 | tf_op jit(solution)/shard_map/ppermute | solution.py:459
  27.5 6.0 %collective-permute-start.8 = (bf16[288,256]{1,0:T(8,128)(2,1)S(1)}, bf16[288,256]{1,0:T(8,128)(2,1)S(1)}, u32[]{:S(2)}, u32[]{:S(2)}) collective-permute-start(bf16[288,256]{1,0:T(8,128)(2,1)S(1)} %get-tuple-element.97), channel_id=1, source_target_pairs={{0,4},{1,5},{8,12},{9,13},{4,0},{5,1},{12,8},{13,9},{2,6},{3,7},{1... | collective-permute-start | bytes 442376 | tf_op jit(solution)/shard_map/ppermute | solution.py:459
  30.8 5.9 %collective-permute-start.14 = (bf16[288,256]{1,0:T(8,128)(2,1)S(1)}, bf16[288,256]{1,0:T(8,128)(2,1)S(1)}, u32[]{:S(2)}, u32[]{:S(2)}) collective-permute-start(bf16[288,256]{1,0:T(8,128)(2,1)S(1)} %get-tuple-element.106), channel_id=1, source_target_pairs={{0,4},{1,5},{8,12},{9,13},{4,0},{5,1},{12,8},{13,9},{2,6},{3,7},{1... | collective-permute-start | bytes 442376 | tf_op jit(solution)/shard_map/ppermute | solution.py:459
  34.8 6.2 %collective-permute-start.12 = (bf16[288,256]{1,0:T(8,128)(2,1)S(1)}, bf16[288,256]{1,0:T(8,128)(2,1)S(1)}, u32[]{:S(2)}, u32[]{:S(2)}) collective-permute-start(bf16[288,256]{1,0:T(8,128)(2,1)S(1)} %get-tuple-element.104), channel_id=1, source_target_pairs={{0,4},{1,5},{8,12},{9,13},{4,0},{5,1},{12,8},{13,9},{2,6},{3,7},{1... | collective-permute-start | bytes 442376 | tf_op jit(solution)/shard_map/ppermute | solution.py:459
  35.8 5.1 %collective-permute-start.13 = (bf16[288,256]{1,0:T(8,128)(2,1)S(1)}, bf16[288,256]{1,0:T(8,128)(2,1)S(1)}, u32[]{:S(2)}, u32[]{:S(2)}) collective-permute-start(bf16[288,256]{1,0:T(8,128)(2,1)S(1)} %get-tuple-element.105), channel_id=1, source_target_pairs={{4,8},{5,9},{0,1},{12,13},{8,4},{9,5},{1,0},{13,12},{6,10},{7,11},... | collective-permute-start | bytes 442376 | tf_op jit(solution)/shard_map/ppermute | solution.py:459
  36.7 7.4 %collective-permute-start.18 = (bf16[288,256]{1,0:T(8,128)(2,1)S(1)}, bf16[288,256]{1,0:T(8,128)(2,1)S(1)}, u32[]{:S(2)}, u32[]{:S(2)}) collective-permute-start(bf16[288,256]{1,0:T(8,128)(2,1)S(1)} %get-tuple-element.114), channel_id=1, source_target_pairs={{0,4},{1,5},{8,12},{9,13},{4,0},{5,1},{12,8},{13,9},{2,6},{3,7},{1... | collective-permute-start | bytes 442376 | tf_op jit(solution)/shard_map/ppermute | solution.py:459
  39.0 5.1 %collective-permute-start.19 = (bf16[288,256]{1,0:T(8,128)(2,1)S(1)}, bf16[288,256]{1,0:T(8,128)(2,1)S(1)}, u32[]{:S(2)}, u32[]{:S(2)}) collective-permute-start(bf16[288,256]{1,0:T(8,128)(2,1)S(1)} %get-tuple-element.115), channel_id=1, source_target_pairs={{4,8},{5,9},{0,1},{12,13},{8,4},{9,5},{1,0},{13,12},{6,10},{7,11},... | collective-permute-start | bytes 442376 | tf_op jit(solution)/shard_map/ppermute | solution.py:459
  40.9 6.4 %collective-permute-start.16 = (bf16[288,256]{1,0:T(8,128)(2,1)S(1)}, bf16[288,256]{1,0:T(8,128)(2,1)S(1)}, u32[]{:S(2)}, u32[]{:S(2)}) collective-permute-start(bf16[288,256]{1,0:T(8,128)(2,1)S(1)} %get-tuple-element.112), channel_id=1, source_target_pairs={{0,4},{1,5},{8,12},{9,13},{4,0},{5,1},{12,8},{13,9},{2,6},{3,7},{1... | collective-permute-start | bytes 442376 | tf_op jit(solution)/shard_map/ppermute | solution.py:459
  44.1 7.6 %collective-permute-start.22 = (bf16[288,256]{1,0:T(8,128)(2,1)S(1)}, bf16[288,256]{1,0:T(8,128)(2,1)S(1)}, u32[]{:S(2)}, u32[]{:S(2)}) collective-permute-start(bf16[288,256]{1,0:T(8,128)(2,1)S(1)} %get-tuple-element.122), channel_id=1, source_target_pairs={{0,4},{1,5},{8,12},{9,13},{4,0},{5,1},{12,8},{13,9},{2,6},{3,7},{1... | collective-permute-start | bytes 442376 | tf_op jit(solution)/shard_map/ppermute | solution.py:459
  47.3 8.1 %collective-permute-start.20 = (bf16[288,256]{1,0:T(8,128)(2,1)S(1)}, bf16[288,256]{1,0:T(8,128)(2,1)S(1)}, u32[]{:S(2)}, u32[]{:S(2)}) collective-permute-start(bf16[288,256]{1,0:T(8,128)(2,1)S(1)} %get-tuple-element.120), channel_id=1, source_target_pairs={{0,4},{1,5},{8,12},{9,13},{4,0},{5,1},{12,8},{13,9},{2,6},{3,7},{1... | collective-permute-start | bytes 442376 | tf_op jit(solution)/shard_map/ppermute | solution.py:459
  53.0 6.3 %collective-permute-start.26 = (bf16[288,256]{1,0:T(8,128)(2,1)S(1)}, bf16[288,256]{1,0:T(8,128)(2,1)S(1)}, u32[]{:S(2)}, u32[]{:S(2)}) collective-permute-start(bf16[288,256]{1,0:T(8,128)(2,1)S(1)} %get-tuple-element.131), channel_id=1, source_target_pairs={{0,4},{1,5},{8,12},{9,13},{4,0},{5,1},{12,8},{13,9},{2,6},{3,7},{1... | collective-permute-start | bytes 442376 | tf_op jit(solution)/shard_map/ppermute | solution.py:459
  56.7 6.4 %collective-permute-start.24 = (bf16[288,256]{1,0:T(8,128)(2,1)S(1)}, bf16[288,256]{1,0:T(8,128)(2,1)S(1)}, u32[]{:S(2)}, u32[]{:S(2)}) collective-permute-start(bf16[288,256]{1,0:T(8,128)(2,1)S(1)} %get-tuple-element.128), channel_id=1, source_target_pairs={{0,4},{1,5},{8,12},{9,13},{4,0},{5,1},{12,8},{13,9},{2,6},{3,7},{1... | collective-permute-start | bytes 442376 | tf_op jit(solution)/shard_map/ppermute | solution.py:459
  60.7 5.9 %collective-permute-start.30 = (bf16[288,256]{1,0:T(8,128)(2,1)S(1)}, bf16[288,256]{1,0:T(8,128)(2,1)S(1)}, u32[]{:S(2)}, u32[]{:S(2)}) collective-permute-start(bf16[288,256]{1,0:T(8,128)(2,1)S(1)} %get-tuple-element.137), channel_id=1, source_target_pairs={{0,4},{1,5},{8,12},{9,13},{4,0},{5,1},{12,8},{13,9},{2,6},{3,7},{1... | collective-permute-start | bytes 442376 | tf_op jit(solution)/shard_map/ppermute | solution.py:459
  64.4 6.3 %collective-permute-start.28 = (bf16[288,256]{1,0:T(8,128)(2,1)S(1)}, bf16[288,256]{1,0:T(8,128)(2,1)S(1)}, u32[]{:S(2)}, u32[]{:S(2)}) collective-permute-start(bf16[288,256]{1,0:T(8,128)(2,1)S(1)} %get-tuple-element.135), channel_id=1, source_target_pairs={{0,4},{1,5},{8,12},{9,13},{4,0},{5,1},{12,8},{13,9},{2,6},{3,7},{1... | collective-permute-start | bytes 442376 | tf_op jit(solution)/shard_map/ppermute | solution.py:459
  67.9 6.0 %collective-permute-start.33 = (bf16[288,256]{1,0:T(8,128)(2,1)S(1)}, bf16[288,256]{1,0:T(8,128)(2,1)S(1)}, u32[]{:S(2)}, u32[]{:S(2)}) collective-permute-start(bf16[288,256]{1,0:T(8,128)(2,1)S(1)} %get-tuple-element.142), channel_id=1, source_target_pairs={{0,4},{1,5},{8,12},{9,13},{4,0},{5,1},{12,8},{13,9},{2,6},{3,7},{1... | collective-permute-start | bytes 442376 | tf_op jit(solution)/shard_map/ppermute | solution.py:459
  71.9 5.5 %collective-permute-start.32 = (bf16[288,256]{1,0:T(8,128)(2,1)S(1)}, bf16[288,256]{1,0:T(8,128)(2,1)S(1)}, u32[]{:S(2)}, u32[]{:S(2)}) collective-permute-start(bf16[288,256]{1,0:T(8,128)(2,1)S(1)} %get-tuple-element.141), channel_id=1, source_target_pairs={{0,4},{1,5},{8,12},{9,13},{4,0},{5,1},{12,8},{13,9},{2,6},{3,7},{1... | collective-permute-start | bytes 442376 | tf_op jit(solution)/shard_map/ppermute | solution.py:459
  (10 other events, 40.3 us)
